TPU v7x, 32 devices: a whole 2x2x4 slice. The times are simulated.
32 devices in a mesh: region: 4 (over y, core), local: 8 (over z, x).
Axes of the slice: x: 2, y: 2, z: 4, core: 2. Of those that a mesh axis runs over, the one named last changes fastest.
Arguments:
- block_flags: int32 [32, 192], P(None, ('region', 'local')), may hold values 0 or 1
- trace: bfloat16 [32, 24576], P(None, ('region', 'local')), may hold values from 0.099609375 to 1
- w_region: bfloat16 [4, 6144, 6144], P('region', None, 'local'), may hold values from -0.078125 to 0.078125
- lr_weight: bfloat16 [4, 8, 4, 8, 128, 128], P('region', 'local'), may hold values from -0.1875 to 0.1875
- lr_source: int32 [4, 8, 4, 8], P('region', 'local'), may hold values from 0 to 5
- lr_target: int32 [4, 8, 4, 8], P('region', 'local'), may hold values from 0 to 47
- lr_count: int32 [4, 8, 4], P('region', 'local'), may hold values from 0 to 8, as said below
- g_decay: float32 [24576], P(('region', 'local')), may hold values from 0.5 to 0.97
- v_decay: float32 [24576], P(('region', 'local')), may hold values from 0.4 to 0.95
- g_start: float32 [24576], P(('region', 'local')), may hold values from -6 to 6
- v_start: float32 [24576], P(('region', 'local')), may hold values from -6 to 6
Outputs:
- membrane: float32 [32, 24576], P(None, ('region', 'local'))
- g_final: float32 [24576], P(('region', 'local'))
Inputs may be any that keep to these rules, and one draw needn't show every extreme that they name: lr_count is 0 for a region's own devices, exactly 8 from every device to the next region (d = (r + 1) % 4), and 1 to 8 otherwise.
All inputs are finite; a program needn't handle non-finite values. No bound on the sum of `block_flags` on one device may be relied on, other than what follows from the above.
Results may differ from a plain program's by a relative error of at most 0.0003.
Values may be sent and summed in bfloat16 or wider, within the bound.
No kernel may reach another device: no remote copies, remote signals or barrier semaphores. Data moves between devices by JAX's collectives and lax.ppermute only.
A program may use at most 128 MiB of HBM per device.

v0:
```python
import jax
import jax.numpy as jnp
from jax import lax
from jax.sharding import PartitionSpec as P


def local(
    block_flags,
    trace,
    w_region,
    lr_weight,
    lr_source,
    lr_target,
    lr_count,
    g_decay,
    v_decay,
    g_start,
    v_start,
):
    steps = trace.shape[0]
    own_blocks = block_flags.shape[1]
    width = trace.shape[1] // own_blocks
    drive = (
        trace.reshape(steps, own_blocks, width) * block_flags[:, :, None].astype(jnp.bfloat16)
    ).reshape(steps, own_blocks * width)
    weights = w_region[0]
    rows = weights
    inner = jnp.dot(
        lax.all_gather(drive, "local", axis=1, tiled=True), rows, preferred_element_type=jnp.float32
    )
    counts = lr_count[0, 0]
    targets = lr_target[0, 0]
    sources = lr_source[0, 0]
    tiles = lr_weight[0, 0]
    regions = targets.shape[0]
    slots = targets.shape[1]
    blocks = drive.reshape(steps, own_blocks, width)
    chosen = jnp.take(blocks, sources, axis=1)
    partial_value = jnp.einsum("sdci,dcio->dcso", chosen, tiles, preferred_element_type=jnp.float32)
    live = (jnp.arange(slots, dtype=jnp.int32)[None, :] < counts[:, None]).astype(jnp.float32)
    partial_value = partial_value * live[:, :, None, None]
    arrived, arrived_ids = (
        lax.all_to_all(partial_value, "region", split_axis=0, concat_axis=0, tiled=True),
        lax.all_to_all(targets, "region", split_axis=0, concat_axis=0, tiled=True),
    )
    flat = arrived.reshape(regions * slots, steps * width)
    id_flat = arrived_ids.reshape(regions * slots)
    rows = jnp.arange(lax.axis_size("local") * own_blocks, dtype=jnp.int32)
    onehot = (id_flat[None, :] == rows[:, None]).astype(jnp.float32)
    outer = lax.psum_scatter(
        jnp.dot(onehot, flat, precision=lax.Precision.HIGHEST, preferred_element_type=jnp.float32),
        "local",
        scatter_dimension=0,
        tiled=True,
    )
    outer = (
        outer.reshape(own_blocks, steps, width)
        .transpose(1, 0, 2)
        .reshape(steps, own_blocks * width)
    )
    current = inner + outer

    def advance(carry, now):
        g_state, v_state = carry
        g_state = g_decay * g_state + (1.0 - g_decay) * now
        v_state = v_decay * v_state + (1.0 - v_decay) * g_state
        return ((g_state, v_state), v_state)

    (g_last, v_last), membrane = lax.scan(advance, (g_start, v_start), current)
    return (membrane, g_last)


def solution(mesh):
    return jax.shard_map(
        local,
        mesh=mesh,
        in_specs=(
            P(None, ("region", "local")),
            P(None, ("region", "local")),
            P("region", None, "local"),
            P("region", "local", None, None, None, None),
            P("region", "local", None, None),
            P("region", "local", None, None),
            P("region", "local", None),
            P(("region", "local")),
            P(("region", "local")),
            P(("region", "local")),
            P(("region", "local")),
        ),
        out_specs=(P(None, ("region", "local")), P(("region", "local"))),
        check_vma=False,
    )
```

profile of v0, /device:TPU:0, one launch (start us, length us, event | category | flops | bytes accessed | tf_op | source)
XLA Modules:
  0.0 140.8 jit_solution(12021378501771979889)
XLA Ops:
  0.6 0.0 copy-start
  0.6 4.4 %all-to-all-start = ((s32[4,1,8]{2,1,0:T(1,128)}), s32[4,1,8]{2,1,0:T(1,128)S(1)}, u32[]{:S(2)}, u32[]{:S(2)}) async-start(s32[4,1,8]{2,1,0:T(1,128)} %bitcast.50), calls=%async_computation | async-start | bytes 4096 | tf_op jit(solution)/shard_map/all_to_all | solution.py:44
  5.0 0.7 convert_element_type.12
  5.7 0.7 compare_select_fusion
  6.4 0.1 reshape.90
  6.5 0.8 fusion.12
  7.3 0.9 bitcast_multiply_fusion.1
  8.2 0.6 gather_fusion
  8.8 1.2 convolution_multiply_fusion
  10.0 3.5 %all-to-all-start.1 = ((f32[4,8,32,128]{3,2,1,0:T(8,128)}), f32[4,8,32,128]{3,2,1,0:T(8,128)S(1)}, u32[]{:S(2)}, u32[]{:S(2)}) async-start(f32[4,8,32,128]{3,2,1,0:T(8,128)} %convolution_multiply_fusion), calls=%async_computation.1 | async-start | bytes 1048576 | tf_op jit(solution)/shard_map/all_to_all | solution.py:43
  13.5 0.1 copy.23
  13.6 1.2 dynamic-slice.4
  15.4 0.1 mul.33.clone
  15.5 0.8 bitcast_multiply_fusion
  16.3 0.5 broadcast.63
  16.8 0.6 reduce.5
  17.4 0.1 eq.15
  17.5 4.8 %all-to-all-done.1 = f32[4,8,32,128]{3,2,1,0:T(8,128)S(1)} async-done(((f32[4,8,32,128]{3,2,1,0:T(8,128)}), f32[4,8,32,128]{3,2,1,0:T(8,128)S(1)}, u32[]{:S(2)}, u32[]{:S(2)}) %all-to-all-start.1) | async-done | bytes 524320 | tf_op jit(solution)/shard_map/all_to_all | solution.py:43
  22.3 0.8 fusion.4
  23.1 30.3 %fusion = f32[8,4096]{1,0:T(8,128)S(1)} fusion(f32[48,4096]{1,0:T(8,128)S(1)} %fusion.4), kind=kCustom, calls=%all-reduce-scatter | all-reduce-scatter fusion | flops 262145 | bytes 918016
  53.5 0.0 copy-start.1
  53.5 0.0 copy-start.3
  53.5 0.0 copy-start.4
  53.5 0.0 copy-start.5
  53.5 2.5 %collective-permute-start = (f32[8,4096]{1,0:T(8,128)S(1)}, f32[8,4096]{1,0:T(8,128)S(1)}, u32[]{:S(2)}, u32[]{:S(2)}) collective-permute-start(f32[8,4096]{1,0:T(8,128)S(1)} %fusion), channel_id=1, source_target_pairs={{0,1},{1,2},{2,3},{3,4},{4,5},{5,6},{6,7},{8,9},{9,10},{10,11},{11... | collective-permute-start | bytes 393224
  56.0 1.9 %collective-permute-start.1 = (f32[6,4096]{1,0:T(8,128)S(1)}, f32[6,4096]{1,0:T(8,128)S(1)}, u32[]{:S(2)}, u32[]{:S(2)}) collective-permute-start(f32[6,4096]{1,0:T(8,128)S(1)} %slice.2), channel_id=1, source_target_pairs={{0,2},{1,3},{2,4},{3,5},{4,6},{5,7},{8,10},{9,11},{10,12},{11,13},... | collective-permute-start | bytes 294920
  57.9 31.0 %all_gather.3 = bf16[32,6144]{1,0:T(8,128)(2,1)S(1)} all-gather(bf16[32,768]{1,0:T(8,128)(2,1)S(1)} %bitcast_multiply_fusion), channel_id=1, replica_groups=mesh['region'=4,'local'=8] {'local'}, dimensions={1}, use_global_device_ids=true | all-gather | bytes 442368 | tf_op jit(solution)/shard_map/all_gather | solution.py:29
  88.8 0.4 concatenate
  89.3 5.3 %bitcast_add_fusion = f32[32,768]{1,0:T(8,128)S(1)} fusion(f32[4,8,6,128]{3,2,1,0:T(8,128)S(1)} %bitcast.48, bf16[32,6144]{1,0:T(8,128)(2,1)S(1)} %all_gather.3, bf16[1,6144,768]{2,1,0:T(8,128)(2,1)} %param.15), kind=kOutput, calls=%fused_computation.15 | convolution fusion | flops 302014464 | bytes 10027008 | tf_op jit(solution)/shard_map/dot_general | solution.py:28
  94.6 0.0 copy-done.1
  94.7 45.5 %while.14 = (s32[]{:T(128)}, f32[768]{0:T(1024)S(1)}, f32[768]{0:T(1024)S(1)}, f32[32,768]{1,0:T(8,128)}, f32[768]{0:T(1024)S(1)}, /*index=5*/f32[32,768]{1,0:T(8,128)S(1)}, f32[768]{0:T(1024)S(1)}, s32[]{:T(128)}, s32[]{:T(128)}) while((s32[]{:T(128)}, f32[768]{0:T(1024)S(1)}, f32[768]{0:T(1024)S(1)}, f32[32,768]{1,0:T(8,128)}, ...), condition=%wide.region_2.3_spmd, body=%wide.region_1.2_spmd.sunk | while | flops 6146 | bytes 40037 | solution.py:69
  94.7 1.4 dynamic_update_slice.5
  96.2 1.4 dynamic_update_slice.5
  97.6 1.4 dynamic_update_slice.5
  99.0 1.4 dynamic_update_slice.5
  100.4 1.4 dynamic_update_slice.5
  101.9 1.4 dynamic_update_slice.5
  103.3 1.4 dynamic_update_slice.5
  104.7 1.4 dynamic_update_slice.5
  106.1 1.4 dynamic_update_slice.5
  107.5 1.4 dynamic_update_slice.5
  109.0 1.4 dynamic_update_slice.5
  110.4 1.4 dynamic_update_slice.5
  111.8 1.4 dynamic_update_slice.5
  113.2 1.4 dynamic_update_slice.5
  114.7 1.4 dynamic_update_slice.5
  116.1 1.4 dynamic_update_slice.5
  117.5 1.4 dynamic_update_slice.5
  118.9 1.4 dynamic_update_slice.5
  120.3 1.4 dynamic_update_slice.5
  121.8 1.4 dynamic_update_slice.5
  123.2 1.4 dynamic_update_slice.5
  124.6 1.4 dynamic_update_slice.5
  126.0 1.4 dynamic_update_slice.5
  127.5 1.4 dynamic_update_slice.5
  128.9 1.4 dynamic_update_slice.5
  130.3 1.4 dynamic_update_slice.5
  131.7 1.4 dynamic_update_slice.5
  133.1 1.4 dynamic_update_slice.5
  134.6 1.4 dynamic_update_slice.5
  136.0 1.4 dynamic_update_slice.5
  137.4 1.4 dynamic_update_slice.5
  138.8 1.4 dynamic_update_slice.5
  140.2 0.6 copy-done.2
  (108 shorter events, 1.2 us)
Async XLA Ops:
  0.6 8.1 %copy-start = (bf16[1,1,4,8,128,128]{5,4,3,2,1,0:T(8,128)(2,1)S(1)}, bf16[1,1,4,8,128,128]{5,4,3,2,1,0:T(8,128)(2,1)}, u32[]{:S(2)}) copy-start(bf16[1,1,4,8,128,128]{5,4,3,2,1,0:T(8,128)(2,1)} %param.16) | copy-start | bytes 3145732
  0.6 9.4 %all-to-all-start = ((s32[4,1,8]{2,1,0:T(1,128)}), s32[4,1,8]{2,1,0:T(1,128)S(1)}, u32[]{:S(2)}, u32[]{:S(2)}) async-start(s32[4,1,8]{2,1,0:T(1,128)} %bitcast.50), calls=%async_computation | async-start | bytes 4096 | tf_op jit(solution)/shard_map/all_to_all | solution.py:44
  10.0 12.3 %all-to-all-start.1 = ((f32[4,8,32,128]{3,2,1,0:T(8,128)}), f32[4,8,32,128]{3,2,1,0:T(8,128)S(1)}, u32[]{:S(2)}, u32[]{:S(2)}) async-start(f32[4,8,32,128]{3,2,1,0:T(8,128)} %convolution_multiply_fusion), calls=%async_computation.1 | async-start | bytes 1048576 | tf_op jit(solution)/shard_map/all_to_all | solution.py:43
  53.5 41.2 %copy-start.1 = (f32[768]{0:T(1024)S(1)}, f32[768]{0:T(1024)}, u32[]{:S(2)}) copy-start(f32[768]{0:T(1024)} %param.23) | copy-start | bytes 9220
  53.5 41.2 %copy-start.3 = (f32[768]{0:T(1024)S(1)}, f32[768]{0:T(1024)}, u32[]{:S(2)}) copy-start(f32[768]{0:T(1024)} %param.22) | copy-start | bytes 9220
  53.5 41.2 %copy-start.4 = (f32[768]{0:T(1024)S(1)}, f32[768]{0:T(1024)}, u32[]{:S(2)}) copy-start(f32[768]{0:T(1024)} %param.20) | copy-start | bytes 9220
  53.5 41.2 %copy-start.5 = (f32[768]{0:T(1024)S(1)}, f32[768]{0:T(1024)}, u32[]{:S(2)}) copy-start(f32[768]{0:T(1024)} %param.21) | copy-start | bytes 9220
  53.5 35.3 %collective-permute-start = (f32[8,4096]{1,0:T(8,128)S(1)}, f32[8,4096]{1,0:T(8,128)S(1)}, u32[]{:S(2)}, u32[]{:S(2)}) collective-permute-start(f32[8,4096]{1,0:T(8,128)S(1)} %fusion), channel_id=1, source_target_pairs={{0,1},{1,2},{2,3},{3,4},{4,5},{5,6},{6,7},{8,9},{9,10},{10,11},{11... | collective-permute-start | bytes 393224
  56.0 32.9 %collective-permute-start.1 = (f32[6,4096]{1,0:T(8,128)S(1)}, f32[6,4096]{1,0:T(8,128)S(1)}, u32[]{:S(2)}, u32[]{:S(2)}) collective-permute-start(f32[6,4096]{1,0:T(8,128)S(1)} %slice.2), channel_id=1, source_target_pairs={{0,2},{1,3},{2,4},{3,5},{4,6},{5,7},{8,10},{9,11},{10,12},{11,13},... | collective-permute-start | bytes 294920
  140.2 0.6 copy-start.2
where the time goes:
time: 143 us; the launch traced here: 141 us
  blocking collectives  61.3 us (43%)
  local copies, waits for them, and re-layouts  48.4 us (34%)
  starting transfers between devices  12.2 us (9%)
  matrix products  7.39 us (5%)
  waiting for transfers between devices  4.82 us (3%)
  other arithmetic  4.75 us (3%)
    dynamic_update_slice x32, local copies, waits for them, and re-layouts, local(): (g_last, v_last), membrane = lax.scan(advance, (g_start, v_start), current)  43.8 us
    all_gather x1, blocking collectives, local(): lax.all_gather(drive, 'local', axis=1, tiled=True)  31 us
    unnamed x1, blocking collectives  30.3 us
    dot_general x1, matrix products, local(): jnp.dot(lax.all_gather(drive, 'local', axis=1, tiled=True), rows, preferr...  5.34 us
    all_to_all x1, waiting for transfers between devices, local(): lax.all_to_all(partial_value, 'region', split_axis=0, concat_axis=0, tile...  4.81 us
    all_to_all x1, starting transfers between devices, local(): lax.all_to_all(targets, 'region', split_axis=0, concat_axis=0, tiled=True)  4.38 us
    unnamed x2, starting transfers between devices  4.32 us
    all_to_all x1, starting transfers between devices, local(): lax.all_to_all(partial_value, 'region', split_axis=0, concat_axis=0, tile...  3.47 us
  transfers between devices with their start and end apart: 4, of which 1 were waited for; matrix products, arithmetic and copies ran while one was open for 6% of the time, Pallas kernels for 0%

commit v1 on v0

v1 whole, which is shorter than its diff:
```python
import functools

import jax
import jax.numpy as jnp
from jax import lax
from jax.experimental import pallas as pl
from jax.experimental.pallas import tpu as pltpu
from jax.sharding import PartitionSpec as P

TOP = 32766.0
VMEM = pl.BlockSpec(memory_space=pltpu.VMEM)
SMEM = pl.BlockSpec(memory_space=pltpu.SMEM)
ANY = pl.BlockSpec(memory_space=pl.ANY)


def code(value):
    most = jnp.max(jnp.abs(value), axis=-1, keepdims=True)
    power = jnp.ceil(jnp.log2(jnp.maximum(most, 1e-30)) + 1e-5)
    whole = jnp.round(value * (jnp.exp2(-power) * TOP))
    whole = jnp.clip(whole, -32767.0, 32767.0)
    return whole.astype(jnp.int32).astype(jnp.int16), power


def partial_kernel(
    regions, halves, per_half, flags, trace, source, target, count, weight, drive, *rest
):
    outs = rest[: regions - 1]
    tiles, blocks, sem = rest[regions - 1 :]
    steps = trace.shape[0]
    own_blocks, _, width = blocks.shape
    slots = source.shape[1]
    region = lax.axis_index("region")
    copies = []
    for k in range(1, regions):
        copy = pltpu.make_async_copy(weight.at[region ^ k], tiles.at[k - 1], sem.at[k - 1])
        copy.start()
        copies.append(copy)
    for b in range(own_blocks):
        cols = slice(b * width, (b + 1) * width)
        block = (trace[:, cols].astype(jnp.float32) * flags[:, b : b + 1].astype(jnp.float32)).astype(
            jnp.bfloat16
        )
        blocks[b] = block
        for l in range(drive.shape[0]):
            drive[l, :, cols] = block
    lane = lax.broadcasted_iota(jnp.int32, (steps, width), 1)
    for k in range(1, regions):
        copies[k - 1].wait()
        dest = region ^ k
        live = count[0, dest]
        meta = jnp.zeros((steps, width), jnp.int32)
        for j in range(slots):
            part = jnp.dot(
                blocks[source[dest, j]], tiles[k - 1, j], preferred_element_type=jnp.float32
            )
            whole, power = code(part)
            outs[k - 1][j] = whole
            block = target[dest, j]
            owner = block // own_blocks
            place = (
                (owner % halves) * per_half
                + (owner // halves) * own_blocks
                + block
                - owner * own_blocks
            )
            place = jnp.where(j < live, place, -1)
            meta = jnp.where(lane == j, power.astype(jnp.int32), meta)
            meta = jnp.where(lane == slots + j, place, meta)
        outs[k - 1][slots] = meta.astype(jnp.int16)


def gather_kernel(n_in, n_far, halves, own_blocks, *refs):
    ins = refs[:n_in]
    outs = refs[n_in : n_in + n_far - 1]
    own, total, ids, ids_s, sem = refs[n_in + n_far - 1 :]
    slots = ins[0].shape[0] - 1
    steps, width = ins[0].shape[1:]
    per_half = n_far * own_blocks
    local = lax.axis_index("local")
    half = local % halves
    far = local // halves
    for p in range(n_in):
        ids[p] = ins[p][slots, 0:16].astype(jnp.int32)[0:8]
    copy = pltpu.make_async_copy(ids, ids_s, sem)
    copy.start()
    total[...] = jnp.zeros_like(total)
    copy.wait()
    for p in range(n_in):
        scale = jnp.exp2(ins[p][slots].astype(jnp.float32)) * (1.0 / TOP)
        for j in range(slots):
            place = ids_s[p, 0, slots + j] - half * per_half
            place = jnp.where((place >= 0) & (place < per_half), place, per_half)
            total[place] += ins[p][j].astype(jnp.float32) * scale[:, j : j + 1]
    lane = lax.broadcasted_iota(jnp.int32, (steps, width), 1)
    for i in range(own_blocks):
        own[i] = total[far * own_blocks + i]
    for k in range(1, n_far):
        meta = jnp.zeros((steps, width), jnp.int32)
        for i in range(own_blocks):
            whole, power = code(total[(far ^ k) * own_blocks + i])
            outs[k - 1][i] = whole
            meta = jnp.where(lane == i, power.astype(jnp.int32), meta)
        outs[k - 1][own_blocks] = meta.astype(jnp.int16)


def inner_kernel(drive, weight, out):
    @pl.when(pl.program_id(0) == 0)
    def _():
        out[...] = jnp.zeros_like(out)

    out[...] += jnp.dot(drive[0], weight[...], preferred_element_type=jnp.float32)


def advance_kernel(n_in, inner, own, *refs):
    ins = refs[:n_in]
    g_decay, v_decay, g_start, v_start, membrane, g_last, current = refs[n_in:]
    own_blocks, steps, width = own.shape
    scales = [jnp.exp2(r[own_blocks].astype(jnp.float32)) * (1.0 / TOP) for r in ins]
    for i in range(own_blocks):
        cols = slice(i * width, (i + 1) * width)
        value = inner[:, cols] + own[i]
        for r, scale in zip(ins, scales):
            value += r[i].astype(jnp.float32) * scale[:, i : i + 1]
        current[:, cols] = value
    a, b = g_decay[...], v_decay[...]
    g, v = g_start[...], v_start[...]
    for t in range(steps):
        g = a * g + (1.0 - a) * current[t : t + 1, :]
        v = b * v + (1.0 - b) * g
        membrane[t : t + 1, :] = v
    g_last[...] = g


def local(
    regions,
    locals_,
    block_flags,
    trace,
    w_region,
    lr_weight,
    lr_source,
    lr_target,
    lr_count,
    g_decay,
    v_decay,
    g_start,
    v_start,
):
    steps = trace.shape[0]
    own_blocks = block_flags.shape[1]
    neurons = trace.shape[1]
    width = neurons // own_blocks
    slots = lr_target.shape[3]
    halves = 2
    n_far = locals_ // halves
    per_half = n_far * own_blocks
    f32, i16 = jnp.float32, jnp.int16
    sent = jax.ShapeDtypeStruct((slots + 1, steps, width), i16)
    drive, *parts = pl.pallas_call(
        functools.partial(partial_kernel, regions, halves, per_half),
        out_shape=[jax.ShapeDtypeStruct((locals_, steps, neurons), jnp.bfloat16)]
        + [sent] * (regions - 1),
        in_specs=[VMEM, VMEM, SMEM, SMEM, SMEM, ANY],
        out_specs=[VMEM] * regions,
        scratch_shapes=[
            pltpu.VMEM((regions - 1, slots, width, width), jnp.bfloat16),
            pltpu.VMEM((own_blocks, steps, width), jnp.bfloat16),
            pltpu.SemaphoreType.DMA((regions - 1,)),
        ],
        compiler_params=pltpu.CompilerParams(vmem_limit_bytes=16 << 20),
        name="partials",
    )(block_flags, trace, lr_source[0, 0], lr_target[0, 0], lr_count[0], lr_weight[0, 0])

    arrived = []
    for k in range(regions - 1, 0, -1):
        for h in range(halves - 1, -1, -1):
            pairs = [
                (r * locals_ + l, (r ^ k) * locals_ + (l ^ h))
                for r in range(regions)
                for l in range(locals_)
            ]
            arrived.append(lax.ppermute(parts[k - 1], ("region", "local"), pairs))
    drives = lax.all_to_all(drive, "local", split_axis=0, concat_axis=0, tiled=True)

    n_in = len(arrived)
    far_sent = jax.ShapeDtypeStruct((own_blocks + 1, steps, width), i16)
    *sums, own = pl.pallas_call(
        functools.partial(gather_kernel, n_in, n_far, halves, own_blocks),
        out_shape=[far_sent] * (n_far - 1)
        + [jax.ShapeDtypeStruct((own_blocks, steps, width), f32)],
        in_specs=[VMEM] * n_in,
        out_specs=[VMEM] * n_far,
        scratch_shapes=[
            pltpu.VMEM((per_half + 1, steps, width), f32),
            pltpu.VMEM((n_in, 8, width), jnp.int32),
            pltpu.SMEM((n_in, 8, width), jnp.int32),
            pltpu.SemaphoreType.DMA,
        ],
        compiler_params=pltpu.CompilerParams(vmem_limit_bytes=16 << 20),
        name="add_arrived",
    )(*arrived)

    far = [
        lax.ppermute(sums[k - 1], "local", [(l, l ^ (k * halves)) for l in range(locals_)])
        for k in range(1, n_far)
    ]

    inner = pl.pallas_call(
        inner_kernel,
        grid=(locals_,),
        out_shape=jax.ShapeDtypeStruct((steps, neurons), f32),
        in_specs=[
            pl.BlockSpec((1, steps, neurons), lambda l: (l, 0, 0)),
            pl.BlockSpec((neurons, neurons), lambda l: (l, 0)),
        ],
        out_specs=pl.BlockSpec((steps, neurons), lambda l: (0, 0)),
        compiler_params=pltpu.CompilerParams(vmem_limit_bytes=16 << 20),
        cost_estimate=pl.CostEstimate(
            flops=2 * steps * neurons * neurons * locals_,
            bytes_accessed=2 * neurons * neurons * locals_,
            transcendentals=0,
        ),
        name="inner",
    )(drives, w_region[0])

    row = lambda x: x.reshape(1, neurons)
    membrane, g_last = pl.pallas_call(
        functools.partial(advance_kernel, n_far - 1),
        out_shape=[
            jax.ShapeDtypeStruct((steps, neurons), f32),
            jax.ShapeDtypeStruct((1, neurons), f32),
        ],
        in_specs=[VMEM] * (n_far + 5),
        out_specs=[VMEM] * 2,
        scratch_shapes=[pltpu.VMEM((steps, neurons), f32)],
        compiler_params=pltpu.CompilerParams(vmem_limit_bytes=16 << 20),
        name="advance",
    )(inner, own, *far, row(g_decay), row(v_decay), row(g_start), row(v_start))
    return membrane, g_last.reshape(neurons)


def solution(mesh):
    return jax.shard_map(
        functools.partial(local, mesh.shape["region"], mesh.shape["local"]),
        mesh=mesh,
        in_specs=(
            P(None, ("region", "local")),
            P(None, ("region", "local")),
            P("region", None, "local"),
            P("region", "local", None, None, None, None),
            P("region", "local", None, None),
            P("region", "local", None, None),
            P("region", "local", None),
            P(("region", "local")),
            P(("region", "local")),
            P(("region", "local")),
            P(("region", "local")),
        ),
        out_specs=(P(None, ("region", "local")), P(("region", "local"))),
        check_vma=False,
    )
```

time: 143 us -> 44.1 us (0.31); the launches traced: 141 us -> 43.5 us
  blocking collectives: 61.3 us -> 0 us
  local copies, waits for them, and re-layouts: 48.4 us -> 11.2 us
  starting transfers between devices: 12.2 us -> 19.9 us
  Pallas kernels: 0 us -> 7.49 us
  matrix products: 7.39 us -> 0 us
  other arithmetic: 4.75 us -> 0.6 us
    dynamic_update_slice x32 -> x0, local copies, waits for them, and re-layouts: 43.8 us -> none  [local(): (g_last, v_last), membrane = lax.scan(advance, (g_start, v_start), current)]
    all_gather x1 -> x0, blocking collectives: 31 us -> none  [local(): lax.all_gather(drive, 'local', axis=1, tiled=True)]
    unnamed x1 -> x0, blocking collectives: 30.3 us -> none
    ppermute x0 -> x9, starting transfers between devices: none -> 12.7 us  [the longest x6 8.22 us: local(): arrived.append(lax.ppermute(parts[k - 1], ('region', 'local'), pairs))]
    pallas_call x0 -> x4, Pallas kernels: none -> 7.49 us  [the longest x1 2.64 us: local(): pl.pallas_call(inner_kernel, grid=(locals_,), out_shape=jax.ShapeDtypeStr...]
    dot_general x3 -> x0, matrix products: 7.39 us -> none  [the longest x1 5.34 us: local(): jnp.dot(lax.all_gather(drive, 'local', axis=1, tiled=True), rows, preferr...]
    unnamed x17 -> x13, local copies, waits for them, and re-layouts: 2.4 us -> 8.49 us
    all_to_all x2 -> x1, waiting for transfers between devices: 4.81 us -> 0.01 us  [local(): lax.all_to_all(drive, 'local', split_axis=0, concat_axis=0, tiled=True)]
  transfers between devices with their start and end apart: 4 -> 10, of which waited for: 1 -> 3; matrix products, arithmetic and copies ran while one was open for 6% -> 6% of each run, Pallas kernels for 0% -> 10%
where the time goes in v1:
time: 44.1 us; the launch traced here: 43.5 us
  starting transfers between devices  19.9 us (45%)
  local copies, waits for them, and re-layouts  11.2 us (25%)
  Pallas kernels  7.49 us (17%)
  waiting for transfers between devices  3.57 us (8%)
  between operations  0.68 us (2%)
  other arithmetic  0.6 us (1%)
    unnamed x13, local copies, waits for them, and re-layouts  8.49 us
    ppermute x6, starting transfers between devices, local(): arrived.append(lax.ppermute(parts[k - 1], ('region', 'local'), pairs))  8.22 us
    all_to_all x1, starting transfers between devices, local(): lax.all_to_all(drive, 'local', split_axis=0, concat_axis=0, tiled=True)  7.27 us
    ppermute x3, starting transfers between devices, local(): lax.ppermute(sums[k - 1], 'local', [(l, l ^ k * halves) for l in range(lo...  4.45 us
    ppermute x6, waiting for transfers between devices, local(): arrived.append(lax.ppermute(parts[k - 1], ('region', 'local'), pairs))  3.55 us
    reshape x4, local copies, waits for them, and re-layouts, local(): row = lambda x: x.reshape(1, neurons)  2.76 us
    pallas_call x1, Pallas kernels, local(): pl.pallas_call(inner_kernel, grid=(locals_,), out_shape=jax.ShapeDtypeStr...  2.64 us
    pallas_call x1, Pallas kernels, local(): pl.pallas_call(functools.partial(partial_kernel, regions, halves, per_hal...  2.4 us
  transfers between devices with their start and end apart: 10, of which 3 were waited for; matrix products, arithmetic and copies ran while one was open for 6% of the time, Pallas kernels for 10%

profile of v1, /device:TPU:0, one launch (start us, length us, event | category | flops | bytes accessed | tf_op | source)
XLA Modules:
  0.0 43.5 jit_solution(17652945332790103873)
XLA Ops:
  0.6 0.8 %copy.13.flags = s32[32,6]{1,0:T(8,128)S(1)} copy(s32[32,6]{0,1:T(8,128)} %param.11) | data formatting | bytes 1536 | tf_op args[0]
  1.4 0.0 copy-start.1
  1.4 1.2 %copy-done.1 = bf16[1,1,4,8,128,128]{5,4,3,2,1,0:T(8,128)(2,1)S(1)} copy-done((bf16[1,1,4,8,128,128]{5,4,3,2,1,0:T(8,128)(2,1)S(1)}, bf16[1,1,4,8,128,128]{5,4,3,2,1,0:T(8,128)(2,1)}, u32[]{:S(2)}) %copy-start.1) | copy-done | bytes 1048600
  2.6 0.0 copy-start.2
  2.6 0.8 %copy-done.2 = bf16[32,768]{1,0:T(8,128)(2,1)S(1)} copy-done((bf16[32,768]{1,0:T(8,128)(2,1)S(1)}, bf16[32,768]{1,0:T(8,128)(2,1)}, u32[]{:S(2)}) %copy-start.2) | copy-done | bytes 49176
  3.4 0.0 copy-start.3
  3.4 0.7 %copy-done.3 = s32[1,1,4,8]{3,2,1,0:T(4,128)S(1)} copy-done((s32[1,1,4,8]{3,2,1,0:T(4,128)S(1)}, s32[1,1,4,8]{3,2,1,0:T(4,128)}, u32[]{:S(2)}) %copy-start.3) | copy-done | bytes 152
  4.1 0.0 copy-start.4
  4.1 0.7 %copy-done.4 = s32[1,1,4,8]{3,2,1,0:T(4,128)S(1)} copy-done((s32[1,1,4,8]{3,2,1,0:T(4,128)S(1)}, s32[1,1,4,8]{3,2,1,0:T(4,128)}, u32[]{:S(2)}) %copy-start.4) | copy-done | bytes 152
  4.8 0.0 copy-start.5
  4.8 0.7 %copy-done.5 = s32[1,1,4]{2,1,0:T(1,128)S(1)} copy-done((s32[1,1,4]{2,1,0:T(1,128)S(1)}, s32[1,1,4]{2,1,0:T(1,128)}, u32[]{:S(2)}) %copy-start.5) | copy-done | bytes 40
  5.4 2.4 %partials.1 = (bf16[8,32,768]{2,1,0:T(8,128)(2,1)}, s16[9,32,128]{2,1,0:T(8,128)(2,1)S(1)}, s16[9,32,128]{2,1,0:T(8,128)(2,1)S(1)}, s16[9,32,128]{2,1,0:T(8,128)(2,1)S(1)}) custom-call(s32[32,6]{1,0:T(8,128)S(1)} %copy.13.flags, bf16[32,768]{1,0:T(8,128)(2,1)S(1)} %copy-done.2, s32[4,8]{1,0:T(4,128)S(1)} %bitcast.7, s32[4,8]{1,0:T(4,128)S(1)} %bitcast.8, ...), custom_call_target="tpu_custom_call" | custom-call | tf_op jit(solution)/shard_map/partials/pallas_call | solution.py:159
  7.8 7.3 %all-to-all-start = ((bf16[8,32,768]{2,1,0:T(8,128)(2,1)}), bf16[8,32,768]{2,1,0:T(8,128)(2,1)S(1)}, u32[]{:S(2)}, u32[]{:S(2)}) async-start(bf16[8,32,768]{2,1,0:T(8,128)(2,1)} %get-tuple-element.12), calls=%async_computation | async-start | bytes 786432 | tf_op jit(solution)/shard_map/all_to_all | solution.py:183
  15.1 1.9 %collective-permute-start = (s16[9,32,128]{2,1,0:T(8,128)(2,1)S(1)}, s16[9,32,128]{2,1,0:T(8,128)(2,1)S(1)}, u32[]{:S(2)}, u32[]{:S(2)}) collective-permute-start(s16[9,32,128]{2,1,0:T(8,128)(2,1)S(1)} %get-tuple-element.13), channel_id=1, source_target_pairs={{0,25},{1,24},{2,27},{3,26},{4,29},{5,28},{6,31},{7,30},{8,17},{9,... | collective-permute-start | bytes 221192 | tf_op jit(solution)/shard_map/ppermute | solution.py:182
  17.0 1.3 %collective-permute-start.1 = (s16[9,32,128]{2,1,0:T(8,128)(2,1)S(1)}, s16[9,32,128]{2,1,0:T(8,128)(2,1)S(1)}, u32[]{:S(2)}, u32[]{:S(2)}) collective-permute-start(s16[9,32,128]{2,1,0:T(8,128)(2,1)S(1)} %get-tuple-element.13), channel_id=1, source_target_pairs={{0,24},{1,25},{2,26},{3,27},{4,28},{5,29},{6,30},{7,31},{8,16},{9,... | collective-permute-start | bytes 221192 | tf_op jit(solution)/shard_map/ppermute | solution.py:182
  18.3 1.0 %collective-permute-start.2 = (s16[9,32,128]{2,1,0:T(8,128)(2,1)S(1)}, s16[9,32,128]{2,1,0:T(8,128)(2,1)S(1)}, u32[]{:S(2)}, u32[]{:S(2)}) collective-permute-start(s16[9,32,128]{2,1,0:T(8,128)(2,1)S(1)} %get-tuple-element.14), channel_id=1, source_target_pairs={{0,17},{1,16},{2,19},{3,18},{4,21},{5,20},{6,23},{7,22},{8,25},{9,... | collective-permute-start | bytes 221192 | tf_op jit(solution)/shard_map/ppermute | solution.py:182
  19.3 0.6 %collective-permute-start.3 = (s16[9,32,128]{2,1,0:T(8,128)(2,1)S(1)}, s16[9,32,128]{2,1,0:T(8,128)(2,1)S(1)}, u32[]{:S(2)}, u32[]{:S(2)}) collective-permute-start(s16[9,32,128]{2,1,0:T(8,128)(2,1)S(1)} %get-tuple-element.14), channel_id=1, source_target_pairs={{0,16},{1,17},{2,18},{3,19},{4,20},{5,21},{6,22},{7,23},{8,24},{9,... | collective-permute-start | bytes 221192 | tf_op jit(solution)/shard_map/ppermute | solution.py:182
  19.8 0.9 %collective-permute-start.4 = (s16[9,32,128]{2,1,0:T(8,128)(2,1)S(1)}, s16[9,32,128]{2,1,0:T(8,128)(2,1)S(1)}, u32[]{:S(2)}, u32[]{:S(2)}) collective-permute-start(s16[9,32,128]{2,1,0:T(8,128)(2,1)S(1)} %get-tuple-element.15), channel_id=1, source_target_pairs={{0,9},{1,8},{2,11},{3,10},{4,13},{5,12},{6,15},{7,14},{8,1},{9,0},... | collective-permute-start | bytes 221192 | tf_op jit(solution)/shard_map/ppermute | solution.py:182
  20.7 0.2 collective-permute-done.refs_0_
  21.0 2.6 %collective-permute-start.5 = (s16[9,32,128]{2,1,0:T(8,128)(2,1)S(1)}, s16[9,32,128]{2,1,0:T(8,128)(2,1)S(1)}, u32[]{:S(2)}, u32[]{:S(2)}) collective-permute-start(s16[9,32,128]{2,1,0:T(8,128)(2,1)S(1)} %get-tuple-element.15), channel_id=1, source_target_pairs={{0,8},{1,9},{2,10},{3,11},{4,12},{5,13},{6,14},{7,15},{8,0},{9,1},... | collective-permute-start | bytes 221192 | tf_op jit(solution)/shard_map/ppermute | solution.py:182
  23.6 0.0 collective-permute-done.1.refs_1_
  23.6 2.4 %collective-permute-done.2.refs_2_ = s16[9,32,128]{2,1,0:T(8,128)(2,1)S(1)} collective-permute-done((s16[9,32,128]{2,1,0:T(8,128)(2,1)S(1)}, s16[9,32,128]{2,1,0:T(8,128)(2,1)S(1)}, u32[]{:S(2)}, u32[]{:S(2)}) %collective-permute-start.2) | collective-permute-done | bytes 73760 | tf_op jit(solution)/shard_map/ppermute | solution.py:182
  25.9 0.0 collective-permute-done.3.refs_3_
  25.9 0.9 %collective-permute-done.4.refs_4_ = s16[9,32,128]{2,1,0:T(8,128)(2,1)S(1)} collective-permute-done((s16[9,32,128]{2,1,0:T(8,128)(2,1)S(1)}, s16[9,32,128]{2,1,0:T(8,128)(2,1)S(1)}, u32[]{:S(2)}, u32[]{:S(2)}) %collective-permute-start.4) | collective-permute-done | bytes 73760 | tf_op jit(solution)/shard_map/ppermute | solution.py:182
  26.9 0.0 collective-permute-done.5.refs_5_
  26.9 1.6 %add_arrived.1 = (s16[7,32,128]{2,1,0:T(8,128)(2,1)S(1)}, s16[7,32,128]{2,1,0:T(8,128)(2,1)S(1)}, s16[7,32,128]{2,1,0:T(8,128)(2,1)S(1)}, f32[6,32,128]{2,1,0:T(8,128)S(1)}) custom-call(s16[9,32,128]{2,1,0:T(8,128)(2,1)S(1)} %collective-permute-done.refs_0_, s16[9,32,128]{2,1,0:T(8,128)(2,1)S(1)} %collective-permute-done.1.refs_1_, ...), custom_call_target="tpu_custom_call" | custom-call | tf_op jit(solution)/shard_map/add_arrived/pallas_call | solution.py:187
  28.5 1.9 %collective-permute-start.6 = (s16[7,32,128]{2,1,0:T(8,128)(2,1)S(1)}, s16[7,32,128]{2,1,0:T(8,128)(2,1)S(1)}, u32[]{:S(2)}, u32[]{:S(2)}) collective-permute-start(s16[7,32,128]{2,1,0:T(8,128)(2,1)S(1)} %get-tuple-element.17), channel_id=1, source_target_pairs={{0,2},{1,3},{2,0},{3,1},{4,6},{5,7},{6,4},{7,5},{8,10},{9,11},{10,... | collective-permute-start | bytes 172040 | tf_op jit(solution)/shard_map/ppermute | solution.py:204
  30.4 2.1 %collective-permute-start.7 = (s16[7,32,128]{2,1,0:T(8,128)(2,1)S(1)}, s16[7,32,128]{2,1,0:T(8,128)(2,1)S(1)}, u32[]{:S(2)}, u32[]{:S(2)}) collective-permute-start(s16[7,32,128]{2,1,0:T(8,128)(2,1)S(1)} %get-tuple-element.18), channel_id=1, source_target_pairs={{0,4},{1,5},{2,6},{3,7},{4,0},{5,1},{6,2},{7,3},{8,12},{9,13},{10,... | collective-permute-start | bytes 172040 | tf_op jit(solution)/shard_map/ppermute | solution.py:204
  32.5 0.4 %collective-permute-start.8 = (s16[7,32,128]{2,1,0:T(8,128)(2,1)S(1)}, s16[7,32,128]{2,1,0:T(8,128)(2,1)S(1)}, u32[]{:S(2)}, u32[]{:S(2)}) collective-permute-start(s16[7,32,128]{2,1,0:T(8,128)(2,1)S(1)} %get-tuple-element.19), channel_id=1, source_target_pairs={{0,6},{1,7},{2,4},{3,5},{4,2},{5,3},{6,0},{7,1},{8,14},{9,15},{10,... | collective-permute-start | bytes 172040 | tf_op jit(solution)/shard_map/ppermute | solution.py:204
  32.9 0.7 %reshape.19.refs_3_ = f32[1,768]{1,0:T(1,128)S(1)} reshape(f32[768]{0:T(1024)} %param.18) | data formatting | bytes 6144 | tf_op jit(solution)/shard_map/reshape | solution.py:226
  33.6 0.7 %reshape.20.refs_4_ = f32[1,768]{1,0:T(1,128)S(1)} reshape(f32[768]{0:T(1024)} %param.19) | data formatting | bytes 6144 | tf_op jit(solution)/shard_map/reshape | solution.py:226
  34.3 0.7 %reshape.21.refs_5_ = f32[1,768]{1,0:T(1,128)S(1)} reshape(f32[768]{0:T(1024)} %param.20) | data formatting | bytes 6144 | tf_op jit(solution)/shard_map/reshape | solution.py:226
  35.0 0.7 %reshape.22.refs_6_ = f32[1,768]{1,0:T(1,128)S(1)} reshape(f32[768]{0:T(1024)} %param.21) | data formatting | bytes 6144 | tf_op jit(solution)/shard_map/reshape | solution.py:226
  35.7 0.0 all-to-all-done.drive
  35.7 0.0 copy-start
  35.7 3.7 %copy-done = bf16[1,6144,768]{2,1,0:T(8,128)(2,1)S(1)} copy-done((bf16[1,6144,768]{2,1,0:T(8,128)(2,1)S(1)}, bf16[1,6144,768]{2,1,0:T(8,128)(2,1)}, u32[]{:S(2)}) %copy-start) | copy-done | bytes 9437208
  39.4 2.6 %inner.1 = f32[32,768]{1,0:T(8,128)S(1)} custom-call(bf16[8,32,768]{2,1,0:T(8,128)(2,1)S(1)} %all-to-all-done.drive, bf16[6144,768]{1,0:T(8,128)(2,1)S(1)} %bitcast.5), custom_call_target="tpu_custom_call" | custom-call | flops 301989888 | bytes 9437184 | tf_op jit(solution)/shard_map/inner/pallas_call | solution.py:208
  42.0 0.0 collective-permute-done.6.refs_0_
  42.0 0.0 collective-permute-done.7.refs_1_
  42.0 0.0 collective-permute-done.8.refs_2_
  42.0 0.9 %advance.1 = (f32[32,768]{1,0:T(8,128)}, f32[1,768]{1,0:T(1,128)S(1)}) custom-call(f32[32,768]{1,0:T(8,128)S(1)} %inner.1, f32[6,32,128]{2,1,0:T(8,128)S(1)} %get-tuple-element.16.own, s16[7,32,128]{2,1,0:T(8,128)(2,1)S(1)} %collective-permute-done.6.refs_0_, s16[7,32,128]{2,1,0:T(8,128)(2,1)S(1)} %collective-permute-done.7.refs_1_, ...), custom_call_target="tpu_custom_call" | custom-call | tf_op jit(solution)/shard_map/advance/pallas_call | solution.py:227
  42.9 0.6 %reduce = f32[768]{0:T(1024)} reduce(f32[1,768]{1,0:T(1,128)S(1)} %get-tuple-element.21, f32[]{:T(128)} %constant.6), dimensions={0}, to_apply=%get-tuple-element.21.reduce_sub_computation | reduce | bytes 6148 | tf_op jit(solution)/shard_map/advance/pallas_call | solution.py:227
Async XLA Ops:
  1.4 1.2 %copy-start.1 = (bf16[1,1,4,8,128,128]{5,4,3,2,1,0:T(8,128)(2,1)S(1)}, bf16[1,1,4,8,128,128]{5,4,3,2,1,0:T(8,128)(2,1)}, u32[]{:S(2)}) copy-start(bf16[1,1,4,8,128,128]{5,4,3,2,1,0:T(8,128)(2,1)} %param.14) | copy-start | bytes 3145732
  2.6 0.8 %copy-start.2 = (bf16[32,768]{1,0:T(8,128)(2,1)S(1)}, bf16[32,768]{1,0:T(8,128)(2,1)}, u32[]{:S(2)}) copy-start(bf16[32,768]{1,0:T(8,128)(2,1)} %trace.1) | copy-start | bytes 147460
  3.4 0.7 %copy-start.3 = (s32[1,1,4,8]{3,2,1,0:T(4,128)S(1)}, s32[1,1,4,8]{3,2,1,0:T(4,128)}, u32[]{:S(2)}) copy-start(s32[1,1,4,8]{3,2,1,0:T(4,128)} %param.15) | copy-start | bytes 388
  4.1 0.7 %copy-start.4 = (s32[1,1,4,8]{3,2,1,0:T(4,128)S(1)}, s32[1,1,4,8]{3,2,1,0:T(4,128)}, u32[]{:S(2)}) copy-start(s32[1,1,4,8]{3,2,1,0:T(4,128)} %param.16) | copy-start | bytes 388
  4.8 0.7 %copy-start.5 = (s32[1,1,4]{2,1,0:T(1,128)S(1)}, s32[1,1,4]{2,1,0:T(1,128)}, u32[]{:S(2)}) copy-start(s32[1,1,4]{2,1,0:T(1,128)} %param.17) | copy-start | bytes 52
  7.8 27.8 %all-to-all-start = ((bf16[8,32,768]{2,1,0:T(8,128)(2,1)}), bf16[8,32,768]{2,1,0:T(8,128)(2,1)S(1)}, u32[]{:S(2)}, u32[]{:S(2)}) async-start(bf16[8,32,768]{2,1,0:T(8,128)(2,1)} %get-tuple-element.12), calls=%async_computation | async-start | bytes 786432 | tf_op jit(solution)/shard_map/all_to_all | solution.py:183
  15.1 5.9 %collective-permute-start = (s16[9,32,128]{2,1,0:T(8,128)(2,1)S(1)}, s16[9,32,128]{2,1,0:T(8,128)(2,1)S(1)}, u32[]{:S(2)}, u32[]{:S(2)}) collective-permute-start(s16[9,32,128]{2,1,0:T(8,128)(2,1)S(1)} %get-tuple-element.13), channel_id=1, source_target_pairs={{0,25},{1,24},{2,27},{3,26},{4,29},{5,28},{6,31},{7,30},{8,17},{9,... | collective-permute-start | bytes 221192 | tf_op jit(solution)/shard_map/ppermute | solution.py:182
  17.0 6.6 %collective-permute-start.1 = (s16[9,32,128]{2,1,0:T(8,128)(2,1)S(1)}, s16[9,32,128]{2,1,0:T(8,128)(2,1)S(1)}, u32[]{:S(2)}, u32[]{:S(2)}) collective-permute-start(s16[9,32,128]{2,1,0:T(8,128)(2,1)S(1)} %get-tuple-element.13), channel_id=1, source_target_pairs={{0,24},{1,25},{2,26},{3,27},{4,28},{5,29},{6,30},{7,31},{8,16},{9,... | collective-permute-start | bytes 221192 | tf_op jit(solution)/shard_map/ppermute | solution.py:182
  18.3 7.6 %collective-permute-start.2 = (s16[9,32,128]{2,1,0:T(8,128)(2,1)S(1)}, s16[9,32,128]{2,1,0:T(8,128)(2,1)S(1)}, u32[]{:S(2)}, u32[]{:S(2)}) collective-permute-start(s16[9,32,128]{2,1,0:T(8,128)(2,1)S(1)} %get-tuple-element.14), channel_id=1, source_target_pairs={{0,17},{1,16},{2,19},{3,18},{4,21},{5,20},{6,23},{7,22},{8,25},{9,... | collective-permute-start | bytes 221192 | tf_op jit(solution)/shard_map/ppermute | solution.py:182
  19.3 6.7 %collective-permute-start.3 = (s16[9,32,128]{2,1,0:T(8,128)(2,1)S(1)}, s16[9,32,128]{2,1,0:T(8,128)(2,1)S(1)}, u32[]{:S(2)}, u32[]{:S(2)}) collective-permute-start(s16[9,32,128]{2,1,0:T(8,128)(2,1)S(1)} %get-tuple-element.14), channel_id=1, source_target_pairs={{0,16},{1,17},{2,18},{3,19},{4,20},{5,21},{6,22},{7,23},{8,24},{9,... | collective-permute-start | bytes 221192 | tf_op jit(solution)/shard_map/ppermute | solution.py:182
  19.8 7.0 %collective-permute-start.4 = (s16[9,32,128]{2,1,0:T(8,128)(2,1)S(1)}, s16[9,32,128]{2,1,0:T(8,128)(2,1)S(1)}, u32[]{:S(2)}, u32[]{:S(2)}) collective-permute-start(s16[9,32,128]{2,1,0:T(8,128)(2,1)S(1)} %get-tuple-element.15), channel_id=1, source_target_pairs={{0,9},{1,8},{2,11},{3,10},{4,13},{5,12},{6,15},{7,14},{8,1},{9,0},... | collective-permute-start | bytes 221192 | tf_op jit(solution)/shard_map/ppermute | solution.py:182
  21.0 5.9 %collective-permute-start.5 = (s16[9,32,128]{2,1,0:T(8,128)(2,1)S(1)}, s16[9,32,128]{2,1,0:T(8,128)(2,1)S(1)}, u32[]{:S(2)}, u32[]{:S(2)}) collective-permute-start(s16[9,32,128]{2,1,0:T(8,128)(2,1)S(1)} %get-tuple-element.15), channel_id=1, source_target_pairs={{0,8},{1,9},{2,10},{3,11},{4,12},{5,13},{6,14},{7,15},{8,0},{9,1},... | collective-permute-start | bytes 221192 | tf_op jit(solution)/shard_map/ppermute | solution.py:182
  28.5 13.5 %collective-permute-start.6 = (s16[7,32,128]{2,1,0:T(8,128)(2,1)S(1)}, s16[7,32,128]{2,1,0:T(8,128)(2,1)S(1)}, u32[]{:S(2)}, u32[]{:S(2)}) collective-permute-start(s16[7,32,128]{2,1,0:T(8,128)(2,1)S(1)} %get-tuple-element.17), channel_id=1, source_target_pairs={{0,2},{1,3},{2,0},{3,1},{4,6},{5,7},{6,4},{7,5},{8,10},{9,11},{10,... | collective-permute-start | bytes 172040 | tf_op jit(solution)/shard_map/ppermute | solution.py:204
  30.4 11.6 %collective-permute-start.7 = (s16[7,32,128]{2,1,0:T(8,128)(2,1)S(1)}, s16[7,32,128]{2,1,0:T(8,128)(2,1)S(1)}, u32[]{:S(2)}, u32[]{:S(2)}) collective-permute-start(s16[7,32,128]{2,1,0:T(8,128)(2,1)S(1)} %get-tuple-element.18), channel_id=1, source_target_pairs={{0,4},{1,5},{2,6},{3,7},{4,0},{5,1},{6,2},{7,3},{8,12},{9,13},{10,... | collective-permute-start | bytes 172040 | tf_op jit(solution)/shard_map/ppermute | solution.py:204
  32.5 9.5 %collective-permute-start.8 = (s16[7,32,128]{2,1,0:T(8,128)(2,1)S(1)}, s16[7,32,128]{2,1,0:T(8,128)(2,1)S(1)}, u32[]{:S(2)}, u32[]{:S(2)}) collective-permute-start(s16[7,32,128]{2,1,0:T(8,128)(2,1)S(1)} %get-tuple-element.19), channel_id=1, source_target_pairs={{0,6},{1,7},{2,4},{3,5},{4,2},{5,3},{6,0},{7,1},{8,14},{9,15},{10,... | collective-permute-start | bytes 172040 | tf_op jit(solution)/shard_map/ppermute | solution.py:204
  35.7 3.7 %copy-start = (bf16[1,6144,768]{2,1,0:T(8,128)(2,1)S(1)}, bf16[1,6144,768]{2,1,0:T(8,128)(2,1)}, u32[]{:S(2)}) copy-start(bf16[1,6144,768]{2,1,0:T(8,128)(2,1)} %param.13) | copy-start | bytes 28311556

commit v2 on v0

v2 whole, which is shorter than its diff:
```python
import functools

import jax
import jax.numpy as jnp
from jax import lax
from jax.experimental import pallas as pl
from jax.experimental.pallas import tpu as pltpu
from jax.sharding import PartitionSpec as P

TOP = 32766.0
VMEM = pl.BlockSpec(memory_space=pltpu.VMEM)
HBM = pl.BlockSpec(memory_space=pltpu.HBM)
PARAMS = pltpu.CompilerParams(vmem_limit_bytes=24 << 20)
CORES = 2
HALVES = 2


def code(value):
    most = jnp.max(jnp.abs(value), axis=-1, keepdims=True)
    power = jnp.ceil(jnp.log2(jnp.maximum(most, 1e-30)) + 1e-5)
    whole = jnp.round(value * (jnp.exp2(-power) * TOP))
    whole = jnp.clip(whole, -32767.0, 32767.0)
    return whole.astype(jnp.int32).astype(jnp.int16), power


def scales_of(meta):
    return jnp.exp2(meta.astype(jnp.float32)) * (1.0 / TOP)


def load_all(pairs, sems):
    copies = [pltpu.make_async_copy(a, b, sems.at[i]) for i, (a, b) in enumerate(pairs)]
    for copy in copies:
        copy.start()
    return copies


def send_slots(dest, blocks, tiles, source, target, count, per_half, out):
    own_blocks, steps, width = blocks.shape
    slots = source.shape[1]
    lane = lax.broadcasted_iota(jnp.int32, (steps, width), 1)
    live = count[0, dest]
    meta = jnp.zeros((steps, width), jnp.int32)
    for j in range(slots):
        part = jnp.dot(blocks[source[dest, j]], tiles[j], preferred_element_type=jnp.float32)
        whole, power = code(part)
        out[j] = whole
        block = target[dest, j]
        owner = block // own_blocks
        place = (
            (owner % HALVES) * per_half
            + (owner // HALVES) * own_blocks
            + block
            - owner * own_blocks
        )
        place = jnp.where(j < live, place, -1)
        meta = jnp.where(lane == j, power.astype(jnp.int32), meta)
        meta = jnp.where(lane == slots + j, place, meta)
    out[slots] = meta.astype(jnp.int16)


def first_kernel(
    per_half,
    flags_h,
    trace_h,
    source_h,
    target_h,
    count_h,
    weight,
    drive,
    out,
    flags,
    trace,
    source,
    target,
    count,
    tiles,
    sems,
):
    n = out.shape[0]
    own_blocks, steps, width = drive.shape
    region = lax.axis_index("region")
    copies = load_all(
        [(flags_h, flags), (trace_h, trace), (source_h, source), (target_h, target), (count_h, count)]
        + [(weight.at[region ^ 1 ^ (CORES * k)], tiles.at[k]) for k in range(n)],
        sems,
    )
    for copy in copies[:5]:
        copy.wait()
    row = lax.broadcasted_iota(jnp.int32, (steps, steps), 0)
    col = lax.broadcasted_iota(jnp.int32, (steps, steps), 1)
    for b in range(own_blocks):
        across = jnp.where(row == col, flags[b : b + 1, :], 0).astype(jnp.float32)
        on = jnp.sum(across, axis=1, keepdims=True)
        part = trace[:, b * width : (b + 1) * width].astype(jnp.float32)
        drive[b] = (part * on).astype(jnp.bfloat16)
    for k in range(n):
        copies[5 + k].wait()
        dest = region ^ 1 ^ (CORES * k)
        send_slots(dest, drive, tiles.at[k], source, target, count, per_half, out.at[k])


def second_kernel(
    per_half, drive, source_h, target_h, count_h, weight, out, source, target, count, tiles, sems
):
    n = out.shape[0]
    region = lax.axis_index("region")
    copies = load_all(
        [(source_h, source), (target_h, target), (count_h, count)]
        + [(weight.at[region ^ (CORES * (k + 1))], tiles.at[k]) for k in range(n)],
        sems,
    )
    for copy in copies[:3]:
        copy.wait()
    for k in range(n):
        copies[3 + k].wait()
        dest = region ^ (CORES * (k + 1))
        send_slots(dest, drive, tiles.at[k], source, target, count, per_half, out.at[k])


def merge_kernel(n, sibling, mine, drive, drive_x, *outs):
    for k in range(n):
        outs[k][0] = mine[k]
        outs[k][1] = sibling[k + 1]
    outs[n][...] = sibling[0]
    half = lax.axis_index("local") % HALVES
    outs[n + 1][half] = drive[...]
    outs[n + 1][1 - half] = drive_x[...]


def gather_kernel(n_in, n_far, own_blocks, *refs):
    ins = refs[:n_in]
    outs = refs[n_in : n_in + n_far - 1]
    own, total, ids, ids_s, sem = refs[n_in + n_far - 1 :]
    packs = []
    for r in ins:
        packs += [r] if len(r.shape) == 3 else [r.at[i] for i in range(r.shape[0])]
    slots = packs[0].shape[0] - 1
    steps, width = packs[0].shape[1:]
    per_half = n_far * own_blocks
    local = lax.axis_index("local")
    half = local % HALVES
    far = local // HALVES
    for p, pack in enumerate(packs):
        ids[p] = pack[slots, 0:16].astype(jnp.int32)[0:8]
    copy = pltpu.make_async_copy(ids, ids_s, sem)
    copy.start()
    total[...] = jnp.zeros_like(total)
    copy.wait()
    for p, pack in enumerate(packs):
        scale = scales_of(pack[slots])
        for j in range(slots):
            place = ids_s[p, 0, slots + j] - half * per_half
            place = jnp.where((place >= 0) & (place < per_half), place, per_half)
            total[place] += pack[j].astype(jnp.float32) * scale[:, j : j + 1]
    lane = lax.broadcasted_iota(jnp.int32, (steps, width), 1)
    for i in range(own_blocks):
        own[i] = total[far * own_blocks + i]
    for k in range(1, n_far):
        meta = jnp.zeros((steps, width), jnp.int32)
        for i in range(own_blocks):
            whole, power = code(total[(far ^ k) * own_blocks + i])
            outs[k - 1][i] = whole
            meta = jnp.where(lane == i, power.astype(jnp.int32), meta)
        outs[k - 1][own_blocks] = meta.astype(jnp.int16)


def inner_kernel(n_far, *refs):
    pairs = refs[:n_far]
    weight, out, held, sems = refs[n_far:]
    halves, own_blocks, steps, width = pairs[0].shape
    depth = own_blocks * width
    far = lax.axis_index("local") // HALVES
    copies = load_all(
        [
            (
                weight.at[pl.ds(pl.multiple_of(((far ^ k) * halves + h) * depth, depth), depth)],
                held.at[k * halves + h],
            )
            for k in range(n_far)
            for h in range(halves)
        ],
        sems,
    )
    total = jnp.zeros(out.shape, jnp.float32)
    for k in range(n_far):
        for h in range(halves):
            left = jnp.concatenate([pairs[k][h, b] for b in range(own_blocks)], axis=1)
            copies[k * halves + h].wait()
            total += jnp.dot(left, held[k * halves + h], preferred_element_type=jnp.float32)
    out[...] = total


def advance_kernel(n_in, inner, own, *refs):
    ins = refs[:n_in]
    g_decay, v_decay, g_start, v_start, membrane, g_last, current = refs[n_in:]
    own_blocks, steps, width = own.shape
    scales = [scales_of(r[own_blocks]) for r in ins]
    for i in range(own_blocks):
        cols = slice(i * width, (i + 1) * width)
        value = inner[:, cols] + own[i]
        for r, scale in zip(ins, scales):
            value += r[i].astype(jnp.float32) * scale[:, i : i + 1]
        current[:, cols] = value
    neurons = own_blocks * width
    a, b = g_decay[...].reshape(1, neurons), v_decay[...].reshape(1, neurons)
    g, v = g_start[...].reshape(1, neurons), v_start[...].reshape(1, neurons)
    for t in range(steps):
        g = a * g + (1.0 - a) * current[t : t + 1, :]
        v = b * v + (1.0 - b) * g
        membrane[t : t + 1, :] = v
    g_last[...] = g.reshape(neurons)


def local(
    regions,
    locals_,
    block_flags,
    trace,
    w_region,
    lr_weight,
    lr_source,
    lr_target,
    lr_count,
    g_decay,
    v_decay,
    g_start,
    v_start,
):
    steps = trace.shape[0]
    own_blocks = block_flags.shape[1]
    neurons = trace.shape[1]
    width = neurons // own_blocks
    slots = lr_target.shape[3]
    n_far = locals_ // HALVES
    n_hi = regions // CORES
    per_half = n_far * own_blocks
    f32, i16, bf16, i32 = jnp.float32, jnp.int16, jnp.bfloat16, jnp.int32
    shape = jax.ShapeDtypeStruct

    def to(value, k, j):
        pairs = [
            (r * locals_ + l, (r ^ k) * locals_ + (l ^ j))
            for r in range(regions)
            for l in range(locals_)
        ]
        return lax.ppermute(value, ("region", "local"), pairs)

    ids = (lr_source[0, 0], lr_target[0, 0], lr_count[0])
    id_scratch = [
        pltpu.SMEM((regions, slots), i32),
        pltpu.SMEM((regions, slots), i32),
        pltpu.SMEM((1, regions), i32),
    ]
    drive, theirs = pl.pallas_call(
        functools.partial(first_kernel, per_half),
        out_shape=[
            shape((own_blocks, steps, width), bf16),
            shape((n_hi, slots + 1, steps, width), i16),
        ],
        in_specs=[HBM] * 6,
        out_specs=[VMEM] * 2,
        scratch_shapes=[pltpu.VMEM((own_blocks, steps), i32), pltpu.VMEM((steps, neurons), bf16)]
        + id_scratch
        + [pltpu.VMEM((n_hi, slots, width, width), bf16), pltpu.SemaphoreType.DMA((5 + n_hi,))],
        compiler_params=PARAMS,
        name="first_partials",
    )(block_flags.T, trace, *ids, lr_weight[0, 0])
    sibling = to(theirs, 1, 0)
    drive_x = to(drive, 0, 1)
    mine = pl.pallas_call(
        functools.partial(second_kernel, per_half),
        out_shape=shape((n_hi - 1, slots + 1, steps, width), i16),
        in_specs=[VMEM] + [HBM] * 4,
        out_specs=VMEM,
        scratch_shapes=id_scratch
        + [pltpu.VMEM((n_hi - 1, slots, width, width), bf16), pltpu.SemaphoreType.DMA((2 + n_hi,))],
        compiler_params=PARAMS,
        name="second_partials",
    )(drive, *ids, lr_weight[0, 0])
    *merged, beside, pair = pl.pallas_call(
        functools.partial(merge_kernel, n_hi - 1),
        out_shape=[shape((2, slots + 1, steps, width), i16)] * (n_hi - 1)
        + [
            shape((slots + 1, steps, width), i16),
            shape((HALVES, own_blocks, steps, width), bf16),
        ],
        in_specs=[VMEM] * 4,
        out_specs=[VMEM] * (n_hi + 1),
        compiler_params=PARAMS,
        name="merge",
    )(sibling, mine, drive, drive_x)
    arrived = [beside]
    for k in range(1, n_hi):
        for h in range(HALVES):
            arrived.append(to(merged[k - 1], CORES * k, h))
    arrived.append(to(beside, 0, 1))
    far_first = sorted(range(1, n_far), key=lambda k: (k == 1, k))
    pairs = {k: to(pair, 0, k * HALVES) for k in far_first}

    n_packs = 2 + (n_hi - 1) * HALVES * 2
    far_sent = shape((own_blocks + 1, steps, width), i16)
    *sums, own = pl.pallas_call(
        functools.partial(gather_kernel, len(arrived), n_far, own_blocks),
        out_shape=[far_sent] * (n_far - 1) + [shape((own_blocks, steps, width), f32)],
        in_specs=[VMEM] * len(arrived),
        out_specs=[VMEM] * n_far,
        scratch_shapes=[
            pltpu.VMEM((per_half + 1, steps, width), f32),
            pltpu.VMEM((n_packs, 8, width), i32),
            pltpu.SMEM((n_packs, 8, width), i32),
            pltpu.SemaphoreType.DMA,
        ],
        compiler_params=PARAMS,
        name="add_arrived",
    )(*arrived)
    far = [to(sums[k - 1], 0, k * HALVES) for k in far_first]

    inner = pl.pallas_call(
        functools.partial(inner_kernel, n_far),
        out_shape=shape((steps, neurons), f32),
        in_specs=[VMEM] * n_far + [HBM],
        out_specs=VMEM,
        scratch_shapes=[
            pltpu.VMEM((locals_, neurons, neurons), bf16),
            pltpu.SemaphoreType.DMA((locals_,)),
        ],
        compiler_params=PARAMS,
        cost_estimate=pl.CostEstimate(
            flops=2 * steps * neurons * neurons * locals_,
            bytes_accessed=2 * neurons * neurons * locals_,
            transcendentals=0,
        ),
        name="inner",
    )(pair, *[pairs[k] for k in range(1, n_far)], w_region[0])

    return pl.pallas_call(
        functools.partial(advance_kernel, n_far - 1),
        out_shape=[shape((steps, neurons), f32), shape((neurons,), f32)],
        in_specs=[VMEM] * (n_far + 5),
        out_specs=[VMEM] * 2,
        scratch_shapes=[pltpu.VMEM((steps, neurons), f32)],
        compiler_params=PARAMS,
        name="advance",
    )(inner, own, *far, g_decay, v_decay, g_start, v_start)


def solution(mesh):
    return jax.shard_map(
        functools.partial(local, mesh.shape["region"], mesh.shape["local"]),
        mesh=mesh,
        in_specs=(
            P(None, ("region", "local")),
            P(None, ("region", "local")),
            P("region", None, "local"),
            P("region", "local", None, None, None, None),
            P("region", "local", None, None),
            P("region", "local", None, None),
            P("region", "local", None),
            P(("region", "local")),
            P(("region", "local")),
            P(("region", "local")),
            P(("region", "local")),
        ),
        out_specs=(P(None, ("region", "local")), P(("region", "local"))),
        check_vma=False,
    )
```

time: 143 us -> 39.3 us (0.27); the launches traced: 141 us -> 38.9 us
  blocking collectives: 61.3 us -> 0 us
  local copies, waits for them, and re-layouts: 48.4 us -> 11.7 us
  Pallas kernels: 0 us -> 9.07 us
  matrix products: 7.39 us -> 0 us
  other arithmetic: 4.75 us -> 0 us
  starting transfers between devices: 12.2 us -> 16 us
  waiting for transfers between devices: 4.82 us -> 1.43 us
    dynamic_update_slice x32 -> x0, local copies, waits for them, and re-layouts: 43.8 us -> none  [local(): (g_last, v_last), membrane = lax.scan(advance, (g_start, v_start), current)]
    all_gather x1 -> x0, blocking collectives: 31 us -> none  [local(): lax.all_gather(drive, 'local', axis=1, tiled=True)]
    unnamed x1 -> x0, blocking collectives: 30.3 us -> none
    ppermute x0 -> x11, starting transfers between devices: none -> 16 us  [to(): return lax.ppermute(value, ('region', 'local'), pairs)]
    unnamed x17 -> x30, local copies, waits for them, and re-layouts: 2.4 us -> 11.7 us
    pallas_call x0 -> x6, Pallas kernels: none -> 9.07 us  [the longest x1 4.26 us: local(): pl.pallas_call(functools.partial(inner_kernel, n_far), out_shape=shape((s...]
    all_to_all x2 -> x0, starting transfers between devices: 7.85 us -> none  [the longest x1 4.38 us: local(): lax.all_to_all(targets, 'region', split_axis=0, concat_axis=0, tiled=True)]
    dot_general x3 -> x0, matrix products: 7.39 us -> none  [the longest x1 5.34 us: local(): jnp.dot(lax.all_gather(drive, 'local', axis=1, tiled=True), rows, preferr...]
  transfers between devices with their start and end apart: 4 -> 11, of which waited for: 1 -> 1; matrix products, arithmetic and copies ran while one was open for 6% -> 0% of each run, Pallas kernels for 0% -> 17%
where the time goes in v2:
time: 39.3 us; the launch traced here: 38.9 us
  starting transfers between devices  16 us (41%)
  local copies, waits for them, and re-layouts  11.7 us (30%)
  Pallas kernels  9.07 us (23%)
  waiting for transfers between devices  1.43 us (4%)
  between operations  0.79 us (2%)
    ppermute x11, starting transfers between devices, to(): return lax.ppermute(value, ('region', 'local'), pairs)  16 us
    unnamed x30, local copies, waits for them, and re-layouts  11.7 us
    pallas_call x1, Pallas kernels, local(): pl.pallas_call(functools.partial(inner_kernel, n_far), out_shape=shape((s...  4.26 us
    pallas_call x1, Pallas kernels, local(): pl.pallas_call(functools.partial(gather_kernel, len(arrived), n_far, own_...  1.58 us
    ppermute x11, waiting for transfers between devices, to(): return lax.ppermute(value, ('region', 'local'), pairs)  1.43 us
    pallas_call x1, Pallas kernels, local(): pl.pallas_call(functools.partial(first_kernel, per_half), out_shape=[shap...  1.4 us
    pallas_call x1, Pallas kernels, local(): pl.pallas_call(functools.partial(second_kernel, per_half), out_shape=shap...  0.92 us
    pallas_call x1, Pallas kernels, local(): pl.pallas_call(functools.partial(advance_kernel, n_far - 1), out_shape=[s...  0.87 us
  transfers between devices with their start and end apart: 11, of which 1 were waited for; matrix products, arithmetic and copies ran while one was open for 0% of the time, Pallas kernels for 17%

profile of v2, /device:TPU:0, one launch (start us, length us, event | category | flops | bytes accessed | tf_op | source)
XLA Modules:
  0.0 38.9 jit_solution(3152808709462742061)
XLA Ops:
  0.6 0.0 copy-start.10
  0.6 0.0 copy-start.9
  0.7 0.0 copy-start.1
  0.7 1.2 %copy-done.1 = bf16[1,1,4,8,128,128]{5,4,3,2,1,0:T(8,128)(2,1)S(1)} copy-done((bf16[1,1,4,8,128,128]{5,4,3,2,1,0:T(8,128)(2,1)S(1)}, bf16[1,1,4,8,128,128]{5,4,3,2,1,0:T(8,128)(2,1)}, u32[]{:S(2)}) %copy-start.1) | copy-done | bytes 1048600
  1.9 0.0 copy-start.3
  1.9 0.8 %copy-done.3 = bf16[32,768]{1,0:T(8,128)(2,1)S(1)} copy-done((bf16[32,768]{1,0:T(8,128)(2,1)S(1)}, bf16[32,768]{1,0:T(8,128)(2,1)}, u32[]{:S(2)}) %copy-start.3) | copy-done | bytes 49176
  2.7 0.0 copy-start.4
  2.7 0.7 %copy-done.4 = s32[1,1,4,8]{3,2,1,0:T(4,128)S(1)} copy-done((s32[1,1,4,8]{3,2,1,0:T(4,128)S(1)}, s32[1,1,4,8]{3,2,1,0:T(4,128)}, u32[]{:S(2)}) %copy-start.4) | copy-done | bytes 152
  3.4 0.0 copy-start.6
  3.4 0.7 %copy-done.6 = s32[1,1,4,8]{3,2,1,0:T(4,128)S(1)} copy-done((s32[1,1,4,8]{3,2,1,0:T(4,128)S(1)}, s32[1,1,4,8]{3,2,1,0:T(4,128)}, u32[]{:S(2)}) %copy-start.6) | copy-done | bytes 152
  4.1 0.0 copy-start.8
  4.1 0.7 %copy-done.8 = s32[32,6]{0,1:T(8,128)S(1)} copy-done((s32[32,6]{0,1:T(8,128)S(1)}, s32[32,6]{0,1:T(8,128)}, u32[]{:S(2)}) %copy-start.8) | copy-done | bytes 792
  4.7 0.0 copy-start.13
  4.7 0.7 %copy-done.13 = s32[1,1,4]{2,1,0:T(1,128)S(1)} copy-done((s32[1,1,4]{2,1,0:T(1,128)S(1)}, s32[1,1,4]{2,1,0:T(1,128)}, u32[]{:S(2)}) %copy-start.13) | copy-done | bytes 40
  5.4 0.0 copy-start.11
  5.4 0.0 copy-start.12
  5.4 1.4 %first_partials.1 = (bf16[6,32,128]{2,1,0:T(8,128)(2,1)S(1)}, s16[2,9,32,128]{3,2,1,0:T(8,128)(2,1)S(1)}) custom-call(s32[6,32]{1,0:T(8,128)S(1)} %bitcast.13, bf16[32,768]{1,0:T(8,128)(2,1)S(1)} %copy-done.3, s32[4,8]{1,0:T(4,128)S(1)} %bitcast.9, s32[4,8]{1,0:T(4,128)S(1)} %bitcast.11, s32[1,4]{1,0:T(1,128)S(1)} %bitcast.14, ...), custom_call_target="tpu_custom_call" | custom-call | tf_op jit(solution)/shard_map/first_partials/pallas_call | solution.py:254
  6.8 0.5 %collective-permute-start = (s16[2,9,32,128]{3,2,1,0:T(8,128)(2,1)S(1)}, s16[2,9,32,128]{3,2,1,0:T(8,128)(2,1)S(1)}, u32[]{:S(2)}, u32[]{:S(2)}) collective-permute-start(s16[2,9,32,128]{3,2,1,0:T(8,128)(2,1)S(1)} %get-tuple-element.11), channel_id=1, source_target_pairs={{0,8},{1,9},{2,10},{3,11},{4,12},{5,13},{6,14},{7,15},{8,0},{9,1},... | collective-permute-start | bytes 442376 | tf_op jit(solution)/shard_map/ppermute | solution.py:246
  7.3 2.6 %collective-permute-start.1 = (bf16[6,32,128]{2,1,0:T(8,128)(2,1)S(1)}, bf16[6,32,128]{2,1,0:T(8,128)(2,1)S(1)}, u32[]{:S(2)}, u32[]{:S(2)}) collective-permute-start(bf16[6,32,128]{2,1,0:T(8,128)(2,1)S(1)} %get-tuple-element.12.drive), channel_id=1, source_target_pairs={{0,1},{1,0},{2,3},{3,2},{4,5},{5,4},{6,7},{7,6},{8,9},{9,8},{10,11... | collective-permute-start | bytes 147464 | tf_op jit(solution)/shard_map/ppermute | solution.py:246
  9.9 0.0 copy-start.2
  9.9 1.2 %copy-done.2 = bf16[1,1,4,8,128,128]{5,4,3,2,1,0:T(8,128)(2,1)S(1)} copy-done((bf16[1,1,4,8,128,128]{5,4,3,2,1,0:T(8,128)(2,1)S(1)}, bf16[1,1,4,8,128,128]{5,4,3,2,1,0:T(8,128)(2,1)}, u32[]{:S(2)}) %copy-start.2) | copy-done | bytes 1048600
  11.1 0.0 copy-start.5
  11.1 0.7 %copy-done.5 = s32[1,1,4,8]{3,2,1,0:T(4,128)S(1)} copy-done((s32[1,1,4,8]{3,2,1,0:T(4,128)S(1)}, s32[1,1,4,8]{3,2,1,0:T(4,128)}, u32[]{:S(2)}) %copy-start.5) | copy-done | bytes 152
  11.8 0.0 copy-start.7
  11.8 0.7 %copy-done.7 = s32[1,1,4,8]{3,2,1,0:T(4,128)S(1)} copy-done((s32[1,1,4,8]{3,2,1,0:T(4,128)S(1)}, s32[1,1,4,8]{3,2,1,0:T(4,128)}, u32[]{:S(2)}) %copy-start.7) | copy-done | bytes 152
  12.5 0.0 copy-start.14
  12.5 0.7 %copy-done.14 = s32[1,1,4]{2,1,0:T(1,128)S(1)} copy-done((s32[1,1,4]{2,1,0:T(1,128)S(1)}, s32[1,1,4]{2,1,0:T(1,128)}, u32[]{:S(2)}) %copy-start.14) | copy-done | bytes 40
  13.1 0.9 %second_partials.1.mine = s16[1,9,32,128]{3,2,1,0:T(8,128)(2,1)S(1)} custom-call(bf16[6,32,128]{2,1,0:T(8,128)(2,1)S(1)} %get-tuple-element.12.drive, s32[4,8]{1,0:T(4,128)S(1)} %bitcast.10, s32[4,8]{1,0:T(4,128)S(1)} %bitcast.12, s32[1,4]{1,0:T(1,128)S(1)} %bitcast.15, bf16[4,8,128,128]{3,2,1,0:T(8,128)(2,1)S(1)} %bitcast.8), custom_call_target="tpu_custom_call" | custom-call | tf_op jit(solution)/shard_map/second_partials/pallas_call | solution.py:270
  14.1 0.0 collective-permute-done.1.drive_x
  14.1 0.0 collective-permute-done.sibling
  14.1 1.6 %collective-permute-start.6 = (s16[2,9,32,128]{3,2,1,0:T(8,128)(2,1)S(1)}, s16[2,9,32,128]{3,2,1,0:T(8,128)(2,1)S(1)}, u32[]{:S(2)}, u32[]{:S(2)}) collective-permute-start(s16[2,9,32,128]{3,2,1,0:T(8,128)(2,1)S(1)} %get-tuple-element.15), channel_id=1, source_target_pairs={{0,17},{1,16},{2,19},{3,18},{4,21},{5,20},{6,23},{7,22},{8,25},{9,... | collective-permute-start | bytes 442376 | tf_op jit(solution)/shard_map/ppermute | solution.py:246
  15.7 0.1 collective-permute-start.5
  15.8 1.9 %collective-permute-start.7 = (s16[9,32,128]{2,1,0:T(8,128)(2,1)S(1)}, s16[9,32,128]{2,1,0:T(8,128)(2,1)S(1)}, u32[]{:S(2)}, u32[]{:S(2)}) collective-permute-start(s16[9,32,128]{2,1,0:T(8,128)(2,1)S(1)} %get-tuple-element.14.refs_0_), channel_id=1, source_target_pairs={{0,1},{1,0},{2,3},{3,2},{4,5},{5,4},{6,7},{7,6},{8,9},{9,8},{10,11... | collective-permute-start | bytes 221192 | tf_op jit(solution)/shard_map/ppermute | solution.py:246
  17.7 3.6 %collective-permute-start.4 = (bf16[2,6,32,128]{3,2,1,0:T(8,128)(2,1)S(1)}, bf16[2,6,32,128]{3,2,1,0:T(8,128)(2,1)S(1)}, u32[]{:S(2)}, u32[]{:S(2)}) collective-permute-start(bf16[2,6,32,128]{3,2,1,0:T(8,128)(2,1)S(1)} %get-tuple-element.13.refs_0_), channel_id=1, source_target_pairs={{0,6},{1,7},{2,4},{3,5},{4,2},{5,3},{6,0},{7,1},{8,14},{9,15},{10,... | collective-permute-start | bytes 294920 | tf_op jit(solution)/shard_map/ppermute | solution.py:246
  21.3 0.0 collective-permute-start.3
  21.3 1.4 %collective-permute-done.7.refs_3_ = s16[9,32,128]{2,1,0:T(8,128)(2,1)S(1)} collective-permute-done((s16[9,32,128]{2,1,0:T(8,128)(2,1)S(1)}, s16[9,32,128]{2,1,0:T(8,128)(2,1)S(1)}, u32[]{:S(2)}, u32[]{:S(2)}) %collective-permute-start.7) | collective-permute-done | bytes 73760 | tf_op jit(solution)/shard_map/ppermute | solution.py:246
  22.7 1.6 %collective-permute-start.2 = (bf16[2,6,32,128]{3,2,1,0:T(8,128)(2,1)S(1)}, bf16[2,6,32,128]{3,2,1,0:T(8,128)(2,1)S(1)}, u32[]{:S(2)}, u32[]{:S(2)}) collective-permute-start(bf16[2,6,32,128]{3,2,1,0:T(8,128)(2,1)S(1)} %get-tuple-element.13.refs_0_), channel_id=1, source_target_pairs={{0,2},{1,3},{2,0},{3,1},{4,6},{5,7},{6,4},{7,5},{8,10},{9,11},{10,... | collective-permute-start | bytes 294920 | tf_op jit(solution)/shard_map/ppermute | solution.py:246
  24.3 0.0 collective-permute-done.6.refs_2_
  24.3 0.0 collective-permute-done.5.refs_1_
  24.3 1.6 %add_arrived.1 = (s16[7,32,128]{2,1,0:T(8,128)(2,1)S(1)}, s16[7,32,128]{2,1,0:T(8,128)(2,1)S(1)}, s16[7,32,128]{2,1,0:T(8,128)(2,1)S(1)}, f32[6,32,128]{2,1,0:T(8,128)S(1)}) custom-call(s16[9,32,128]{2,1,0:T(8,128)(2,1)S(1)} %get-tuple-element.14.refs_0_, s16[2,9,32,128]{3,2,1,0:T(8,128)(2,1)S(1)} %collective-permute-done.5.refs_1_, ...), custom_call_target="tpu_custom_call" | custom-call | tf_op jit(solution)/shard_map/add_arrived/pallas_call | solution.py:302
  25.9 2.7 %collective-permute-start.8 = (s16[7,32,128]{2,1,0:T(8,128)(2,1)S(1)}, s16[7,32,128]{2,1,0:T(8,128)(2,1)S(1)}, u32[]{:S(2)}, u32[]{:S(2)}) collective-permute-start(s16[7,32,128]{2,1,0:T(8,128)(2,1)S(1)} %get-tuple-element.17), channel_id=1, source_target_pairs={{0,4},{1,5},{2,6},{3,7},{4,0},{5,1},{6,2},{7,3},{8,12},{9,13},{10,... | collective-permute-start | bytes 172040 | tf_op jit(solution)/shard_map/ppermute | solution.py:246
  28.5 1.2 %collective-permute-start.9 = (s16[7,32,128]{2,1,0:T(8,128)(2,1)S(1)}, s16[7,32,128]{2,1,0:T(8,128)(2,1)S(1)}, u32[]{:S(2)}, u32[]{:S(2)}) collective-permute-start(s16[7,32,128]{2,1,0:T(8,128)(2,1)S(1)} %get-tuple-element.18), channel_id=1, source_target_pairs={{0,6},{1,7},{2,4},{3,5},{4,2},{5,3},{6,0},{7,1},{8,14},{9,15},{10,... | collective-permute-start | bytes 172040 | tf_op jit(solution)/shard_map/ppermute | solution.py:246
  29.8 0.0 collective-permute-done.4.refs_3_
  29.8 0.2 collective-permute-start.10
  30.0 0.0 collective-permute-done.3.refs_2_
  30.0 0.0 collective-permute-done.2.refs_1_
  30.0 0.0 copy-start
  30.0 3.7 %copy-done = bf16[1,6144,768]{2,1,0:T(8,128)(2,1)S(1)} copy-done((bf16[1,6144,768]{2,1,0:T(8,128)(2,1)S(1)}, bf16[1,6144,768]{2,1,0:T(8,128)(2,1)}, u32[]{:S(2)}) %copy-start) | copy-done | bytes 9437208
  33.7 4.3 %inner.1 = f32[32,768]{1,0:T(8,128)S(1)} custom-call(bf16[2,6,32,128]{3,2,1,0:T(8,128)(2,1)S(1)} %get-tuple-element.13.refs_0_, bf16[2,6,32,128]{3,2,1,0:T(8,128)(2,1)S(1)} %collective-permute-done.2.refs_1_, bf16[2,6,32,128]{3,2,1,0:T(8,128)(2,1)S(1)} %collective-permute-done.3.refs_2_, bf16[2,6,32,128]{3,2,1,0:T(8,128)(2,1)S(1)} %collective-permute-done.4.refs_3_, ...), custom_call_target="tpu_custom_call" | custom-call | flops 301989888 | bytes 9437184 | tf_op jit(solution)/shard_map/inner/pallas_call | solution.py:318
  38.0 0.0 collective-permute-done.8.refs_0_
  38.0 0.0 collective-permute-done.9.refs_1_
  38.0 0.0 collective-permute-done.10.refs_2_
  38.0 0.0 copy-done.10
  38.0 0.0 copy-done.9
  38.0 0.0 copy-done.11
  38.0 0.0 copy-done.12
  38.0 0.9 %advance.1 = (f32[32,768]{1,0:T(8,128)}, f32[768]{0:T(1024)}) custom-call(f32[32,768]{1,0:T(8,128)S(1)} %inner.1, f32[6,32,128]{2,1,0:T(8,128)S(1)} %get-tuple-element.16.own, s16[7,32,128]{2,1,0:T(8,128)(2,1)S(1)} %collective-permute-done.8.refs_0_, s16[7,32,128]{2,1,0:T(8,128)(2,1)S(1)} %collective-permute-done.9.refs_1_, ...), custom_call_target="tpu_custom_call" | custom-call | tf_op jit(solution)/shard_map/advance/pallas_call | solution.py:336
  (1 shorter events, 0.0 us)
Async XLA Ops:
  0.6 37.4 %copy-start.10 = (f32[768]{0:T(1024)S(1)}, f32[768]{0:T(1024)}, u32[]{:S(2)}) copy-start(f32[768]{0:T(1024)} %refs_4_.1) | copy-start | bytes 9220
  0.6 37.4 %copy-start.9 = (f32[768]{0:T(1024)S(1)}, f32[768]{0:T(1024)}, u32[]{:S(2)}) copy-start(f32[768]{0:T(1024)} %refs_3_.1) | copy-start | bytes 9220
  0.7 1.2 %copy-start.1 = (bf16[1,1,4,8,128,128]{5,4,3,2,1,0:T(8,128)(2,1)S(1)}, bf16[1,1,4,8,128,128]{5,4,3,2,1,0:T(8,128)(2,1)}, u32[]{:S(2)}) copy-start(bf16[1,1,4,8,128,128]{5,4,3,2,1,0:T(8,128)(2,1)} %param.14) | copy-start | bytes 3145732
  1.9 0.8 %copy-start.3 = (bf16[32,768]{1,0:T(8,128)(2,1)S(1)}, bf16[32,768]{1,0:T(8,128)(2,1)}, u32[]{:S(2)}) copy-start(bf16[32,768]{1,0:T(8,128)(2,1)} %trace_h.1) | copy-start | bytes 147460
  2.7 0.7 %copy-start.4 = (s32[1,1,4,8]{3,2,1,0:T(4,128)S(1)}, s32[1,1,4,8]{3,2,1,0:T(4,128)}, u32[]{:S(2)}) copy-start(s32[1,1,4,8]{3,2,1,0:T(4,128)} %param.15) | copy-start | bytes 388
  3.4 0.7 %copy-start.6 = (s32[1,1,4,8]{3,2,1,0:T(4,128)S(1)}, s32[1,1,4,8]{3,2,1,0:T(4,128)}, u32[]{:S(2)}) copy-start(s32[1,1,4,8]{3,2,1,0:T(4,128)} %param.16) | copy-start | bytes 388
  4.1 0.7 %copy-start.8 = (s32[32,6]{0,1:T(8,128)S(1)}, s32[32,6]{0,1:T(8,128)}, u32[]{:S(2)}) copy-start(s32[32,6]{0,1:T(8,128)} %param.11) | copy-start | bytes 2308
  4.7 0.7 %copy-start.13 = (s32[1,1,4]{2,1,0:T(1,128)S(1)}, s32[1,1,4]{2,1,0:T(1,128)}, u32[]{:S(2)}) copy-start(s32[1,1,4]{2,1,0:T(1,128)} %param.17) | copy-start | bytes 52
  5.4 32.6 %copy-start.11 = (f32[768]{0:T(1024)S(1)}, f32[768]{0:T(1024)}, u32[]{:S(2)}) copy-start(f32[768]{0:T(1024)} %refs_5_.1) | copy-start | bytes 9220
  5.4 32.6 %copy-start.12 = (f32[768]{0:T(1024)S(1)}, f32[768]{0:T(1024)}, u32[]{:S(2)}) copy-start(f32[768]{0:T(1024)} %refs_6_.1) | copy-start | bytes 9220
  6.8 7.3 %collective-permute-start = (s16[2,9,32,128]{3,2,1,0:T(8,128)(2,1)S(1)}, s16[2,9,32,128]{3,2,1,0:T(8,128)(2,1)S(1)}, u32[]{:S(2)}, u32[]{:S(2)}) collective-permute-start(s16[2,9,32,128]{3,2,1,0:T(8,128)(2,1)S(1)} %get-tuple-element.11), channel_id=1, source_target_pairs={{0,8},{1,9},{2,10},{3,11},{4,12},{5,13},{6,14},{7,15},{8,0},{9,1},... | collective-permute-start | bytes 442376 | tf_op jit(solution)/shard_map/ppermute | solution.py:246
  7.3 6.7 %collective-permute-start.1 = (bf16[6,32,128]{2,1,0:T(8,128)(2,1)S(1)}, bf16[6,32,128]{2,1,0:T(8,128)(2,1)S(1)}, u32[]{:S(2)}, u32[]{:S(2)}) collective-permute-start(bf16[6,32,128]{2,1,0:T(8,128)(2,1)S(1)} %get-tuple-element.12.drive), channel_id=1, source_target_pairs={{0,1},{1,0},{2,3},{3,2},{4,5},{5,4},{6,7},{7,6},{8,9},{9,8},{10,11... | collective-permute-start | bytes 147464 | tf_op jit(solution)/shard_map/ppermute | solution.py:246
  9.9 1.2 %copy-start.2 = (bf16[1,1,4,8,128,128]{5,4,3,2,1,0:T(8,128)(2,1)S(1)}, bf16[1,1,4,8,128,128]{5,4,3,2,1,0:T(8,128)(2,1)}, u32[]{:S(2)}) copy-start(bf16[1,1,4,8,128,128]{5,4,3,2,1,0:T(8,128)(2,1)} %param.14) | copy-start | bytes 3145732
  11.1 0.7 %copy-start.5 = (s32[1,1,4,8]{3,2,1,0:T(4,128)S(1)}, s32[1,1,4,8]{3,2,1,0:T(4,128)}, u32[]{:S(2)}) copy-start(s32[1,1,4,8]{3,2,1,0:T(4,128)} %param.15) | copy-start | bytes 388
  11.8 0.7 %copy-start.7 = (s32[1,1,4,8]{3,2,1,0:T(4,128)S(1)}, s32[1,1,4,8]{3,2,1,0:T(4,128)}, u32[]{:S(2)}) copy-start(s32[1,1,4,8]{3,2,1,0:T(4,128)} %param.16) | copy-start | bytes 388
  12.5 0.7 %copy-start.14 = (s32[1,1,4]{2,1,0:T(1,128)S(1)}, s32[1,1,4]{2,1,0:T(1,128)}, u32[]{:S(2)}) copy-start(s32[1,1,4]{2,1,0:T(1,128)} %param.17) | copy-start | bytes 52
  14.1 10.1 %collective-permute-start.6 = (s16[2,9,32,128]{3,2,1,0:T(8,128)(2,1)S(1)}, s16[2,9,32,128]{3,2,1,0:T(8,128)(2,1)S(1)}, u32[]{:S(2)}, u32[]{:S(2)}) collective-permute-start(s16[2,9,32,128]{3,2,1,0:T(8,128)(2,1)S(1)} %get-tuple-element.15), channel_id=1, source_target_pairs={{0,17},{1,16},{2,19},{3,18},{4,21},{5,20},{6,23},{7,22},{8,25},{9,... | collective-permute-start | bytes 442376 | tf_op jit(solution)/shard_map/ppermute | solution.py:246
  15.7 8.6 %collective-permute-start.5 = (s16[2,9,32,128]{3,2,1,0:T(8,128)(2,1)S(1)}, s16[2,9,32,128]{3,2,1,0:T(8,128)(2,1)S(1)}, u32[]{:S(2)}, u32[]{:S(2)}) collective-permute-start(s16[2,9,32,128]{3,2,1,0:T(8,128)(2,1)S(1)} %get-tuple-element.15), channel_id=1, source_target_pairs={{0,16},{1,17},{2,18},{3,19},{4,20},{5,21},{6,22},{7,23},{8,24},{9,... | collective-permute-start | bytes 442376 | tf_op jit(solution)/shard_map/ppermute | solution.py:246
  15.8 6.9 %collective-permute-start.7 = (s16[9,32,128]{2,1,0:T(8,128)(2,1)S(1)}, s16[9,32,128]{2,1,0:T(8,128)(2,1)S(1)}, u32[]{:S(2)}, u32[]{:S(2)}) collective-permute-start(s16[9,32,128]{2,1,0:T(8,128)(2,1)S(1)} %get-tuple-element.14.refs_0_), channel_id=1, source_target_pairs={{0,1},{1,0},{2,3},{3,2},{4,5},{5,4},{6,7},{7,6},{8,9},{9,8},{10,11... | collective-permute-start | bytes 221192 | tf_op jit(solution)/shard_map/ppermute | solution.py:246
  17.7 12.1 %collective-permute-start.4 = (bf16[2,6,32,128]{3,2,1,0:T(8,128)(2,1)S(1)}, bf16[2,6,32,128]{3,2,1,0:T(8,128)(2,1)S(1)}, u32[]{:S(2)}, u32[]{:S(2)}) collective-permute-start(bf16[2,6,32,128]{3,2,1,0:T(8,128)(2,1)S(1)} %get-tuple-element.13.refs_0_), channel_id=1, source_target_pairs={{0,6},{1,7},{2,4},{3,5},{4,2},{5,3},{6,0},{7,1},{8,14},{9,15},{10,... | collective-permute-start | bytes 294920 | tf_op jit(solution)/shard_map/ppermute | solution.py:246
  21.3 8.7 %collective-permute-start.3 = (bf16[2,6,32,128]{3,2,1,0:T(8,128)(2,1)S(1)}, bf16[2,6,32,128]{3,2,1,0:T(8,128)(2,1)S(1)}, u32[]{:S(2)}, u32[]{:S(2)}) collective-permute-start(bf16[2,6,32,128]{3,2,1,0:T(8,128)(2,1)S(1)} %get-tuple-element.13.refs_0_), channel_id=1, source_target_pairs={{0,4},{1,5},{2,6},{3,7},{4,0},{5,1},{6,2},{7,3},{8,12},{9,13},{10,... | collective-permute-start | bytes 294920 | tf_op jit(solution)/shard_map/ppermute | solution.py:246
  22.7 7.3 %collective-permute-start.2 = (bf16[2,6,32,128]{3,2,1,0:T(8,128)(2,1)S(1)}, bf16[2,6,32,128]{3,2,1,0:T(8,128)(2,1)S(1)}, u32[]{:S(2)}, u32[]{:S(2)}) collective-permute-start(bf16[2,6,32,128]{3,2,1,0:T(8,128)(2,1)S(1)} %get-tuple-element.13.refs_0_), channel_id=1, source_target_pairs={{0,2},{1,3},{2,0},{3,1},{4,6},{5,7},{6,4},{7,5},{8,10},{9,11},{10,... | collective-permute-start | bytes 294920 | tf_op jit(solution)/shard_map/ppermute | solution.py:246
  25.9 12.1 %collective-permute-start.8 = (s16[7,32,128]{2,1,0:T(8,128)(2,1)S(1)}, s16[7,32,128]{2,1,0:T(8,128)(2,1)S(1)}, u32[]{:S(2)}, u32[]{:S(2)}) collective-permute-start(s16[7,32,128]{2,1,0:T(8,128)(2,1)S(1)} %get-tuple-element.17), channel_id=1, source_target_pairs={{0,4},{1,5},{2,6},{3,7},{4,0},{5,1},{6,2},{7,3},{8,12},{9,13},{10,... | collective-permute-start | bytes 172040 | tf_op jit(solution)/shard_map/ppermute | solution.py:246
  28.5 9.5 %collective-permute-start.9 = (s16[7,32,128]{2,1,0:T(8,128)(2,1)S(1)}, s16[7,32,128]{2,1,0:T(8,128)(2,1)S(1)}, u32[]{:S(2)}, u32[]{:S(2)}) collective-permute-start(s16[7,32,128]{2,1,0:T(8,128)(2,1)S(1)} %get-tuple-element.18), channel_id=1, source_target_pairs={{0,6},{1,7},{2,4},{3,5},{4,2},{5,3},{6,0},{7,1},{8,14},{9,15},{10,... | collective-permute-start | bytes 172040 | tf_op jit(solution)/shard_map/ppermute | solution.py:246
  29.8 8.2 %collective-permute-start.10 = (s16[7,32,128]{2,1,0:T(8,128)(2,1)S(1)}, s16[7,32,128]{2,1,0:T(8,128)(2,1)S(1)}, u32[]{:S(2)}, u32[]{:S(2)}) collective-permute-start(s16[7,32,128]{2,1,0:T(8,128)(2,1)S(1)} %get-tuple-element.19), channel_id=1, source_target_pairs={{0,2},{1,3},{2,0},{3,1},{4,6},{5,7},{6,4},{7,5},{8,10},{9,11},{10,... | collective-permute-start | bytes 172040 | tf_op jit(solution)/shard_map/ppermute | solution.py:246
  30.0 3.7 %copy-start = (bf16[1,6144,768]{2,1,0:T(8,128)(2,1)S(1)}, bf16[1,6144,768]{2,1,0:T(8,128)(2,1)}, u32[]{:S(2)}) copy-start(bf16[1,6144,768]{2,1,0:T(8,128)(2,1)} %param.13) | copy-start | bytes 28311556

commit v3 on v2

--- a/solution.py
+++ b/solution.py
@@ -10,6 +10,7 @@
 TOP = 32766.0
 VMEM = pl.BlockSpec(memory_space=pltpu.VMEM)
 HBM = pl.BlockSpec(memory_space=pltpu.HBM)
+in_hbm = functools.partial(pltpu.with_memory_space_constraint, memory_space=pltpu.HBM)
 PARAMS = pltpu.CompilerParams(vmem_limit_bytes=24 << 20)
 CORES = 2
 HALVES = 2
@@ -34,16 +35,14 @@
     return copies
 
 
-def send_slots(dest, blocks, tiles, source, target, count, per_half, out):
+def choose(dest, blocks, source, target, count, per_half, chosen):
     own_blocks, steps, width = blocks.shape
     slots = source.shape[1]
     lane = lax.broadcasted_iota(jnp.int32, (steps, width), 1)
     live = count[0, dest]
     meta = jnp.zeros((steps, width), jnp.int32)
     for j in range(slots):
-        part = jnp.dot(blocks[source[dest, j]], tiles[j], preferred_element_type=jnp.float32)
-        whole, power = code(part)
-        out[j] = whole
+        chosen[j] = blocks[source[dest, j]]
         block = target[dest, j]
         owner = block // own_blocks
         place = (
@@ -53,8 +52,18 @@
             - owner * own_blocks
         )
         place = jnp.where(j < live, place, -1)
+        meta = jnp.where(lane == slots + j, place, meta)
+    return meta
+
+
+def send_slots(chosen, tiles, meta, out):
+    slots, steps, width = chosen.shape
+    lane = lax.broadcasted_iota(jnp.int32, (steps, width), 1)
+    for j in range(slots):
+        part = jnp.dot(chosen[j], tiles[j], preferred_element_type=jnp.float32)
+        whole, power = code(part)
+        out[j] = whole
         meta = jnp.where(lane == j, power.astype(jnp.int32), meta)
-        meta = jnp.where(lane == slots + j, place, meta)
     out[slots] = meta.astype(jnp.int16)
 
 
@@ -68,12 +77,16 @@
     weight,
     drive,
     out,
+    next_tiles,
+    next_chosen,
+    next_meta,
     flags,
     trace,
     source,
     target,
     count,
     tiles,
+    chosen,
     sems,
 ):
     n = out.shape[0]
@@ -81,7 +94,8 @@
     region = lax.axis_index("region")
     copies = load_all(
         [(flags_h, flags), (trace_h, trace), (source_h, source), (target_h, target), (count_h, count)]
-        + [(weight.at[region ^ 1 ^ (CORES * k)], tiles.at[k]) for k in range(n)],
+        + [(weight.at[region ^ 1 ^ (CORES * k)], tiles.at[k]) for k in range(n)]
+        + [(weight.at[region ^ (CORES * (k + 1))], next_tiles.at[k]) for k in range(n - 1)],
         sems,
     )
     for copy in copies[:5]:
@@ -93,28 +107,24 @@
         on = jnp.sum(across, axis=1, keepdims=True)
         part = trace[:, b * width : (b + 1) * width].astype(jnp.float32)
         drive[b] = (part * on).astype(jnp.bfloat16)
+    for k in range(n - 1):
+        next_meta[k] = choose(
+            region ^ (CORES * (k + 1)), drive, source, target, count, per_half, next_chosen.at[k]
+        )
+    metas = [
+        choose(region ^ 1 ^ (CORES * k), drive, source, target, count, per_half, chosen.at[k])
+        for k in range(n)
+    ]
     for k in range(n):
         copies[5 + k].wait()
-        dest = region ^ 1 ^ (CORES * k)
-        send_slots(dest, drive, tiles.at[k], source, target, count, per_half, out.at[k])
-
-
-def second_kernel(
-    per_half, drive, source_h, target_h, count_h, weight, out, source, target, count, tiles, sems
-):
-    n = out.shape[0]
-    region = lax.axis_index("region")
-    copies = load_all(
-        [(source_h, source), (target_h, target), (count_h, count)]
-        + [(weight.at[region ^ (CORES * (k + 1))], tiles.at[k]) for k in range(n)],
-        sems,
-    )
-    for copy in copies[:3]:
+        send_slots(chosen.at[k], tiles.at[k], metas[k], out.at[k])
+    for copy in copies[5 + n :]:
         copy.wait()
-    for k in range(n):
-        copies[3 + k].wait()
-        dest = region ^ (CORES * (k + 1))
-        send_slots(dest, drive, tiles.at[k], source, target, count, per_half, out.at[k])
+
+
+def second_kernel(chosen, meta, tiles, out):
+    for k in range(out.shape[0]):
+        send_slots(chosen.at[k], tiles.at[k], meta[k], out.at[k])
 
 
 def merge_kernel(n, sibling, mine, drive, drive_x, *outs):
@@ -245,38 +255,46 @@
         ]
         return lax.ppermute(value, ("region", "local"), pairs)
 
-    ids = (lr_source[0, 0], lr_target[0, 0], lr_count[0])
-    id_scratch = [
-        pltpu.SMEM((regions, slots), i32),
-        pltpu.SMEM((regions, slots), i32),
-        pltpu.SMEM((1, regions), i32),
-    ]
-    drive, theirs = pl.pallas_call(
+    drive, theirs, *rest = pl.pallas_call(
         functools.partial(first_kernel, per_half),
         out_shape=[
             shape((own_blocks, steps, width), bf16),
             shape((n_hi, slots + 1, steps, width), i16),
+            shape((n_hi - 1, slots, width, width), bf16),
+            shape((n_hi - 1, slots, steps, width), bf16),
+            shape((n_hi - 1, steps, width), i32),
         ],
         in_specs=[HBM] * 6,
-        out_specs=[VMEM] * 2,
-        scratch_shapes=[pltpu.VMEM((own_blocks, steps), i32), pltpu.VMEM((steps, neurons), bf16)]
-        + id_scratch
-        + [pltpu.VMEM((n_hi, slots, width, width), bf16), pltpu.SemaphoreType.DMA((5 + n_hi,))],
+        out_specs=[VMEM] * 5,
+        scratch_shapes=[
+            pltpu.VMEM((own_blocks, steps), i32),
+            pltpu.VMEM((steps, neurons), bf16),
+            pltpu.SMEM((regions, slots), i32),
+            pltpu.SMEM((regions, slots), i32),
+            pltpu.SMEM((1, regions), i32),
+            pltpu.VMEM((n_hi, slots, width, width), bf16),
+            pltpu.VMEM((n_hi, slots, steps, width), bf16),
+            pltpu.SemaphoreType.DMA((4 + 2 * n_hi,)),
+        ],
         compiler_params=PARAMS,
         name="first_partials",
-    )(block_flags.T, trace, *ids, lr_weight[0, 0])
+    )(
+        *[
+            in_hbm(x)
+            for x in (block_flags.T, trace, lr_source[0, 0], lr_target[0, 0], lr_count[0], lr_weight[0, 0])
+        ]
+    )
     sibling = to(theirs, 1, 0)
     drive_x = to(drive, 0, 1)
+    tiles, chosen, meta = rest
     mine = pl.pallas_call(
-        functools.partial(second_kernel, per_half),
+        second_kernel,
         out_shape=shape((n_hi - 1, slots + 1, steps, width), i16),
-        in_specs=[VMEM] + [HBM] * 4,
+        in_specs=[VMEM] * 3,
         out_specs=VMEM,
-        scratch_shapes=id_scratch
-        + [pltpu.VMEM((n_hi - 1, slots, width, width), bf16), pltpu.SemaphoreType.DMA((2 + n_hi,))],
         compiler_params=PARAMS,
         name="second_partials",
-    )(drive, *ids, lr_weight[0, 0])
+    )(chosen, meta, tiles)
     *merged, beside, pair = pl.pallas_call(
         functools.partial(merge_kernel, n_hi - 1),
         out_shape=[shape((2, slots + 1, steps, width), i16)] * (n_hi - 1)
@@ -331,7 +349,7 @@
             transcendentals=0,
         ),
         name="inner",
-    )(pair, *[pairs[k] for k in range(1, n_far)], w_region[0])
+    )(pair, *[pairs[k] for k in range(1, n_far)], in_hbm(w_region[0]))
 
     return pl.pallas_call(
         functools.partial(advance_kernel, n_far - 1),

time: 39.3 us -> 28.9 us (0.74)
  local copies, waits for them, and re-layouts: 11.7 us -> 0.02 us
  waiting for transfers between devices: 1.43 us -> 3.2 us
    unnamed x30 -> x8, local copies, waits for them, and re-layouts: 11.7 us -> 0.02 us
    ppermute x11, waiting for transfers between devices: 1.43 us -> 3.2 us  [to(): return lax.ppermute(value, ('region', 'local'), pairs)]
    pallas_call x1, Pallas kernels: 0.92 us -> 0.29 us  [local(): pl.pallas_call(second_kernel, out_shape=shape((n_hi - 1, slots + 1, steps...]
    pallas_call x1, Pallas kernels: 1.4 us -> 1.85 us  [local(): pl.pallas_call(functools.partial(first_kernel, per_half), out_shape=[shap...]
  transfers between devices with their start and end apart: 11 -> 11, of which waited for: 1 -> 4; matrix products, arithmetic and copies ran while one was open for 0% -> 0% of each run, Pallas kernels for 17% -> 21%
where the time goes in v3:
time: 28.9 us; the launch traced here: 28.7 us
  starting transfers between devices  16 us (55%)
  Pallas kernels  8.77 us (30%)
  waiting for transfers between devices  3.2 us (11%)
  between operations  0.73 us (3%)
    ppermute x11, starting transfers between devices, to(): return lax.ppermute(value, ('region', 'local'), pairs)  16 us
    pallas_call x1, Pallas kernels, local(): pl.pallas_call(functools.partial(inner_kernel, n_far), out_shape=shape((s...  4.14 us
    ppermute x11, waiting for transfers between devices, to(): return lax.ppermute(value, ('region', 'local'), pairs)  3.2 us
    pallas_call x1, Pallas kernels, local(): pl.pallas_call(functools.partial(first_kernel, per_half), out_shape=[shap...  1.85 us
    pallas_call x1, Pallas kernels, local(): pl.pallas_call(functools.partial(gather_kernel, len(arrived), n_far, own_...  1.59 us
    pallas_call x1, Pallas kernels, local(): pl.pallas_call(functools.partial(advance_kernel, n_far - 1), out_shape=[s...  0.87 us
  transfers between devices with their start and end apart: 11, of which 4 were waited for; matrix products, arithmetic and copies ran while one was open for 0% of the time, Pallas kernels for 21%

profile of v3, /device:TPU:0, one launch (start us, length us, event | category | flops | bytes accessed | tf_op | source)
XLA Modules:
  0.0 28.7 jit_solution(10647721362261640330)
XLA Ops:
  0.6 0.0 copy-start.3
  0.6 0.0 copy-start.2
  0.7 0.0 copy-start.1
  0.7 0.0 copy-start
  0.7 1.8 %first_partials.1 = (bf16[6,32,128]{2,1,0:T(8,128)(2,1)S(1)}, s16[2,9,32,128]{3,2,1,0:T(8,128)(2,1)S(1)}, bf16[1,8,128,128]{3,2,1,0:T(8,128)(2,1)S(1)}, bf16[1,8...) custom-call(s32[6,32]{1,0:T(8,128)} %bitcast.8, bf16[32,768]{1,0:T(8,128)(2,1)} %trace_h.1, s32[4,8]{1,0:T(4,128)} %bitcast.9, ...), custom_call_target="tpu_custom_call" | custom-call | tf_op jit(solution)/shard_map/first_partials/pallas_call | solution.py:258
  2.5 0.5 %collective-permute-start = (s16[2,9,32,128]{3,2,1,0:T(8,128)(2,1)S(1)}, s16[2,9,32,128]{3,2,1,0:T(8,128)(2,1)S(1)}, u32[]{:S(2)}, u32[]{:S(2)}) collective-permute-start(s16[2,9,32,128]{3,2,1,0:T(8,128)(2,1)S(1)} %get-tuple-element.14), channel_id=1, source_target_pairs={{0,8},{1,9},{2,10},{3,11},{4,12},{5,13},{6,14},{7,15},{8,0},{9,1},... | collective-permute-start | bytes 442376 | tf_op jit(solution)/shard_map/ppermute | solution.py:256
  3.0 2.6 %collective-permute-start.1 = (bf16[6,32,128]{2,1,0:T(8,128)(2,1)S(1)}, bf16[6,32,128]{2,1,0:T(8,128)(2,1)S(1)}, u32[]{:S(2)}, u32[]{:S(2)}) collective-permute-start(bf16[6,32,128]{2,1,0:T(8,128)(2,1)S(1)} %get-tuple-element.18.drive), channel_id=1, source_target_pairs={{0,1},{1,0},{2,3},{3,2},{4,5},{5,4},{6,7},{7,6},{8,9},{9,8},{10,11... | collective-permute-start | bytes 147464 | tf_op jit(solution)/shard_map/ppermute | solution.py:256
  5.6 0.3 second_partials.1.mine
  5.9 2.0 %collective-permute-done.1.drive_x = bf16[6,32,128]{2,1,0:T(8,128)(2,1)S(1)} collective-permute-done((bf16[6,32,128]{2,1,0:T(8,128)(2,1)S(1)}, bf16[6,32,128]{2,1,0:T(8,128)(2,1)S(1)}, u32[]{:S(2)}, u32[]{:S(2)}) %collective-permute-start.1) | collective-permute-done | bytes 49184 | tf_op jit(solution)/shard_map/ppermute | solution.py:256
  7.9 0.0 collective-permute-done.sibling
  8.0 2.8 %collective-permute-start.6 = (s16[2,9,32,128]{3,2,1,0:T(8,128)(2,1)S(1)}, s16[2,9,32,128]{3,2,1,0:T(8,128)(2,1)S(1)}, u32[]{:S(2)}, u32[]{:S(2)}) collective-permute-start(s16[2,9,32,128]{3,2,1,0:T(8,128)(2,1)S(1)} %get-tuple-element.21), channel_id=1, source_target_pairs={{0,17},{1,16},{2,19},{3,18},{4,21},{5,20},{6,23},{7,22},{8,25},{9,... | collective-permute-start | bytes 442376 | tf_op jit(solution)/shard_map/ppermute | solution.py:256
  10.8 0.5 %collective-permute-start.5 = (s16[2,9,32,128]{3,2,1,0:T(8,128)(2,1)S(1)}, s16[2,9,32,128]{3,2,1,0:T(8,128)(2,1)S(1)}, u32[]{:S(2)}, u32[]{:S(2)}) collective-permute-start(s16[2,9,32,128]{3,2,1,0:T(8,128)(2,1)S(1)} %get-tuple-element.21), channel_id=1, source_target_pairs={{0,16},{1,17},{2,18},{3,19},{4,20},{5,21},{6,22},{7,23},{8,24},{9,... | collective-permute-start | bytes 442376 | tf_op jit(solution)/shard_map/ppermute | solution.py:256
  11.3 0.3 collective-permute-start.7
  11.5 3.9 %collective-permute-start.4 = (bf16[2,6,32,128]{3,2,1,0:T(8,128)(2,1)S(1)}, bf16[2,6,32,128]{3,2,1,0:T(8,128)(2,1)S(1)}, u32[]{:S(2)}, u32[]{:S(2)}) collective-permute-start(bf16[2,6,32,128]{3,2,1,0:T(8,128)(2,1)S(1)} %get-tuple-element.19.refs_0_), channel_id=1, source_target_pairs={{0,6},{1,7},{2,4},{3,5},{4,2},{5,3},{6,0},{7,1},{8,14},{9,15},{10,... | collective-permute-start | bytes 294920 | tf_op jit(solution)/shard_map/ppermute | solution.py:256
  15.4 0.0 collective-permute-start.3
  15.4 0.5 %collective-permute-done.7.refs_3_ = s16[9,32,128]{2,1,0:T(8,128)(2,1)S(1)} collective-permute-done((s16[9,32,128]{2,1,0:T(8,128)(2,1)S(1)}, s16[9,32,128]{2,1,0:T(8,128)(2,1)S(1)}, u32[]{:S(2)}, u32[]{:S(2)}) %collective-permute-start.7) | collective-permute-done | bytes 73760 | tf_op jit(solution)/shard_map/ppermute | solution.py:256
  15.9 1.6 %collective-permute-start.2 = (bf16[2,6,32,128]{3,2,1,0:T(8,128)(2,1)S(1)}, bf16[2,6,32,128]{3,2,1,0:T(8,128)(2,1)S(1)}, u32[]{:S(2)}, u32[]{:S(2)}) collective-permute-start(bf16[2,6,32,128]{3,2,1,0:T(8,128)(2,1)S(1)} %get-tuple-element.19.refs_0_), channel_id=1, source_target_pairs={{0,2},{1,3},{2,0},{3,1},{4,6},{5,7},{6,4},{7,5},{8,10},{9,11},{10,... | collective-permute-start | bytes 294920 | tf_op jit(solution)/shard_map/ppermute | solution.py:256
  17.5 0.0 collective-permute-done.6.refs_2_
  17.5 0.2 collective-permute-done.5.refs_1_
  17.7 1.6 %add_arrived.1 = (s16[7,32,128]{2,1,0:T(8,128)(2,1)S(1)}, s16[7,32,128]{2,1,0:T(8,128)(2,1)S(1)}, s16[7,32,128]{2,1,0:T(8,128)(2,1)S(1)}, f32[6,32,128]{2,1,0:T(8,128)S(1)}) custom-call(s16[9,32,128]{2,1,0:T(8,128)(2,1)S(1)} %get-tuple-element.20.refs_0_, s16[2,9,32,128]{3,2,1,0:T(8,128)(2,1)S(1)} %collective-permute-done.5.refs_1_, ...), custom_call_target="tpu_custom_call" | custom-call | tf_op jit(solution)/shard_map/add_arrived/pallas_call | solution.py:320
  19.3 2.4 %collective-permute-start.8 = (s16[7,32,128]{2,1,0:T(8,128)(2,1)S(1)}, s16[7,32,128]{2,1,0:T(8,128)(2,1)S(1)}, u32[]{:S(2)}, u32[]{:S(2)}) collective-permute-start(s16[7,32,128]{2,1,0:T(8,128)(2,1)S(1)} %get-tuple-element.23), channel_id=1, source_target_pairs={{0,4},{1,5},{2,6},{3,7},{4,0},{5,1},{6,2},{7,3},{8,12},{9,13},{10,... | collective-permute-start | bytes 172040 | tf_op jit(solution)/shard_map/ppermute | solution.py:256
  21.7 1.3 %collective-permute-start.9 = (s16[7,32,128]{2,1,0:T(8,128)(2,1)S(1)}, s16[7,32,128]{2,1,0:T(8,128)(2,1)S(1)}, u32[]{:S(2)}, u32[]{:S(2)}) collective-permute-start(s16[7,32,128]{2,1,0:T(8,128)(2,1)S(1)} %get-tuple-element.24), channel_id=1, source_target_pairs={{0,6},{1,7},{2,4},{3,5},{4,2},{5,3},{6,0},{7,1},{8,14},{9,15},{10,... | collective-permute-start | bytes 172040 | tf_op jit(solution)/shard_map/ppermute | solution.py:256
  23.0 0.0 collective-permute-done.4.refs_3_
  23.0 0.2 collective-permute-start.10
  23.2 0.0 collective-permute-done.3.refs_2_
  23.2 0.0 collective-permute-done.2.refs_1_
  23.2 4.1 %inner.1 = f32[32,768]{1,0:T(8,128)S(1)} custom-call(bf16[2,6,32,128]{3,2,1,0:T(8,128)(2,1)S(1)} %get-tuple-element.19.refs_0_, bf16[2,6,32,128]{3,2,1,0:T(8,128)(2,1)S(1)} %collective-permute-done.2.refs_1_, bf16[2,6,32,128]{3,2,1,0:T(8,128)(2,1)S(1)} %collective-permute-done.3.refs_2_, bf16[2,6,32,128]{3,2,1,0:T(8,128)(2,1)S(1)} %collective-permute-done.4.refs_3_, ...), custom_call_target="tpu_custom_call" | custom-call | flops 301989888 | bytes 9437184 | tf_op jit(solution)/shard_map/inner/pallas_call | solution.py:336
  27.4 0.0 collective-permute-done.8.refs_0_
  27.4 0.4 %collective-permute-done.9.refs_1_ = s16[7,32,128]{2,1,0:T(8,128)(2,1)S(1)} collective-permute-done((s16[7,32,128]{2,1,0:T(8,128)(2,1)S(1)}, s16[7,32,128]{2,1,0:T(8,128)(2,1)S(1)}, u32[]{:S(2)}, u32[]{:S(2)}) %collective-permute-start.9) | collective-permute-done | bytes 57376 | tf_op jit(solution)/shard_map/ppermute | solution.py:256
  27.8 0.0 collective-permute-done.10.refs_2_
  27.8 0.0 copy-done.3
  27.8 0.0 copy-done.2
  27.8 0.0 copy-done.1
  27.8 0.0 copy-done
  27.8 0.9 %advance.1 = (f32[32,768]{1,0:T(8,128)}, f32[768]{0:T(1024)}) custom-call(f32[32,768]{1,0:T(8,128)S(1)} %inner.1, f32[6,32,128]{2,1,0:T(8,128)S(1)} %get-tuple-element.22.own, s16[7,32,128]{2,1,0:T(8,128)(2,1)S(1)} %collective-permute-done.8.refs_0_, s16[7,32,128]{2,1,0:T(8,128)(2,1)S(1)} %collective-permute-done.9.refs_1_, ...), custom_call_target="tpu_custom_call" | custom-call | tf_op jit(solution)/shard_map/advance/pallas_call | solution.py:354
  (1 shorter events, 0.0 us)
Async XLA Ops:
  0.6 27.2 %copy-start.3 = (f32[768]{0:T(1024)S(1)}, f32[768]{0:T(1024)}, u32[]{:S(2)}) copy-start(f32[768]{0:T(1024)} %refs_6_.1) | copy-start | bytes 9220
  0.6 27.2 %copy-start.2 = (f32[768]{0:T(1024)S(1)}, f32[768]{0:T(1024)}, u32[]{:S(2)}) copy-start(f32[768]{0:T(1024)} %refs_5_.1) | copy-start | bytes 9220
  0.7 27.2 %copy-start.1 = (f32[768]{0:T(1024)S(1)}, f32[768]{0:T(1024)}, u32[]{:S(2)}) copy-start(f32[768]{0:T(1024)} %refs_4_.1) | copy-start | bytes 9220
  0.7 27.2 %copy-start = (f32[768]{0:T(1024)S(1)}, f32[768]{0:T(1024)}, u32[]{:S(2)}) copy-start(f32[768]{0:T(1024)} %refs_3_.1) | copy-start | bytes 9220
  2.5 5.4 %collective-permute-start = (s16[2,9,32,128]{3,2,1,0:T(8,128)(2,1)S(1)}, s16[2,9,32,128]{3,2,1,0:T(8,128)(2,1)S(1)}, u32[]{:S(2)}, u32[]{:S(2)}) collective-permute-start(s16[2,9,32,128]{3,2,1,0:T(8,128)(2,1)S(1)} %get-tuple-element.14), channel_id=1, source_target_pairs={{0,8},{1,9},{2,10},{3,11},{4,12},{5,13},{6,14},{7,15},{8,0},{9,1},... | collective-permute-start | bytes 442376 | tf_op jit(solution)/shard_map/ppermute | solution.py:256
  3.0 4.9 %collective-permute-start.1 = (bf16[6,32,128]{2,1,0:T(8,128)(2,1)S(1)}, bf16[6,32,128]{2,1,0:T(8,128)(2,1)S(1)}, u32[]{:S(2)}, u32[]{:S(2)}) collective-permute-start(bf16[6,32,128]{2,1,0:T(8,128)(2,1)S(1)} %get-tuple-element.18.drive), channel_id=1, source_target_pairs={{0,1},{1,0},{2,3},{3,2},{4,5},{5,4},{6,7},{7,6},{8,9},{9,8},{10,11... | collective-permute-start | bytes 147464 | tf_op jit(solution)/shard_map/ppermute | solution.py:256
  8.0 9.5 %collective-permute-start.6 = (s16[2,9,32,128]{3,2,1,0:T(8,128)(2,1)S(1)}, s16[2,9,32,128]{3,2,1,0:T(8,128)(2,1)S(1)}, u32[]{:S(2)}, u32[]{:S(2)}) collective-permute-start(s16[2,9,32,128]{3,2,1,0:T(8,128)(2,1)S(1)} %get-tuple-element.21), channel_id=1, source_target_pairs={{0,17},{1,16},{2,19},{3,18},{4,21},{5,20},{6,23},{7,22},{8,25},{9,... | collective-permute-start | bytes 442376 | tf_op jit(solution)/shard_map/ppermute | solution.py:256
  10.8 7.0 %collective-permute-start.5 = (s16[2,9,32,128]{3,2,1,0:T(8,128)(2,1)S(1)}, s16[2,9,32,128]{3,2,1,0:T(8,128)(2,1)S(1)}, u32[]{:S(2)}, u32[]{:S(2)}) collective-permute-start(s16[2,9,32,128]{3,2,1,0:T(8,128)(2,1)S(1)} %get-tuple-element.21), channel_id=1, source_target_pairs={{0,16},{1,17},{2,18},{3,19},{4,20},{5,21},{6,22},{7,23},{8,24},{9,... | collective-permute-start | bytes 442376 | tf_op jit(solution)/shard_map/ppermute | solution.py:256
  11.3 4.6 %collective-permute-start.7 = (s16[9,32,128]{2,1,0:T(8,128)(2,1)S(1)}, s16[9,32,128]{2,1,0:T(8,128)(2,1)S(1)}, u32[]{:S(2)}, u32[]{:S(2)}) collective-permute-start(s16[9,32,128]{2,1,0:T(8,128)(2,1)S(1)} %get-tuple-element.20.refs_0_), channel_id=1, source_target_pairs={{0,1},{1,0},{2,3},{3,2},{4,5},{5,4},{6,7},{7,6},{8,9},{9,8},{10,11... | collective-permute-start | bytes 221192 | tf_op jit(solution)/shard_map/ppermute | solution.py:256
  11.5 11.5 %collective-permute-start.4 = (bf16[2,6,32,128]{3,2,1,0:T(8,128)(2,1)S(1)}, bf16[2,6,32,128]{3,2,1,0:T(8,128)(2,1)S(1)}, u32[]{:S(2)}, u32[]{:S(2)}) collective-permute-start(bf16[2,6,32,128]{3,2,1,0:T(8,128)(2,1)S(1)} %get-tuple-element.19.refs_0_), channel_id=1, source_target_pairs={{0,6},{1,7},{2,4},{3,5},{4,2},{5,3},{6,0},{7,1},{8,14},{9,15},{10,... | collective-permute-start | bytes 294920 | tf_op jit(solution)/shard_map/ppermute | solution.py:256
  15.4 7.8 %collective-permute-start.3 = (bf16[2,6,32,128]{3,2,1,0:T(8,128)(2,1)S(1)}, bf16[2,6,32,128]{3,2,1,0:T(8,128)(2,1)S(1)}, u32[]{:S(2)}, u32[]{:S(2)}) collective-permute-start(bf16[2,6,32,128]{3,2,1,0:T(8,128)(2,1)S(1)} %get-tuple-element.19.refs_0_), channel_id=1, source_target_pairs={{0,4},{1,5},{2,6},{3,7},{4,0},{5,1},{6,2},{7,3},{8,12},{9,13},{10,... | collective-permute-start | bytes 294920 | tf_op jit(solution)/shard_map/ppermute | solution.py:256
  15.9 7.4 %collective-permute-start.2 = (bf16[2,6,32,128]{3,2,1,0:T(8,128)(2,1)S(1)}, bf16[2,6,32,128]{3,2,1,0:T(8,128)(2,1)S(1)}, u32[]{:S(2)}, u32[]{:S(2)}) collective-permute-start(bf16[2,6,32,128]{3,2,1,0:T(8,128)(2,1)S(1)} %get-tuple-element.19.refs_0_), channel_id=1, source_target_pairs={{0,2},{1,3},{2,0},{3,1},{4,6},{5,7},{6,4},{7,5},{8,10},{9,11},{10,... | collective-permute-start | bytes 294920 | tf_op jit(solution)/shard_map/ppermute | solution.py:256
  19.3 8.1 %collective-permute-start.8 = (s16[7,32,128]{2,1,0:T(8,128)(2,1)S(1)}, s16[7,32,128]{2,1,0:T(8,128)(2,1)S(1)}, u32[]{:S(2)}, u32[]{:S(2)}) collective-permute-start(s16[7,32,128]{2,1,0:T(8,128)(2,1)S(1)} %get-tuple-element.23), channel_id=1, source_target_pairs={{0,4},{1,5},{2,6},{3,7},{4,0},{5,1},{6,2},{7,3},{8,12},{9,13},{10,... | collective-permute-start | bytes 172040 | tf_op jit(solution)/shard_map/ppermute | solution.py:256
  21.7 6.1 %collective-permute-start.9 = (s16[7,32,128]{2,1,0:T(8,128)(2,1)S(1)}, s16[7,32,128]{2,1,0:T(8,128)(2,1)S(1)}, u32[]{:S(2)}, u32[]{:S(2)}) collective-permute-start(s16[7,32,128]{2,1,0:T(8,128)(2,1)S(1)} %get-tuple-element.24), channel_id=1, source_target_pairs={{0,6},{1,7},{2,4},{3,5},{4,2},{5,3},{6,0},{7,1},{8,14},{9,15},{10,... | collective-permute-start | bytes 172040 | tf_op jit(solution)/shard_map/ppermute | solution.py:256
  23.0 4.8 %collective-permute-start.10 = (s16[7,32,128]{2,1,0:T(8,128)(2,1)S(1)}, s16[7,32,128]{2,1,0:T(8,128)(2,1)S(1)}, u32[]{:S(2)}, u32[]{:S(2)}) collective-permute-start(s16[7,32,128]{2,1,0:T(8,128)(2,1)S(1)} %get-tuple-element.25), channel_id=1, source_target_pairs={{0,2},{1,3},{2,0},{3,1},{4,6},{5,7},{6,4},{7,5},{8,10},{9,11},{10,... | collective-permute-start | bytes 172040 | tf_op jit(solution)/shard_map/ppermute | solution.py:256

commit v4 on v3

--- a/solution.py
+++ b/solution.py
@@ -77,6 +77,7 @@
     weight,
     drive,
     out,
+    across,
     next_tiles,
     next_chosen,
     next_meta,
@@ -103,8 +104,8 @@
     row = lax.broadcasted_iota(jnp.int32, (steps, steps), 0)
     col = lax.broadcasted_iota(jnp.int32, (steps, steps), 1)
     for b in range(own_blocks):
-        across = jnp.where(row == col, flags[b : b + 1, :], 0).astype(jnp.float32)
-        on = jnp.sum(across, axis=1, keepdims=True)
+        spread = jnp.where(row == col, flags[b : b + 1, :], 0).astype(jnp.float32)
+        on = jnp.sum(spread, axis=1, keepdims=True)
         part = trace[:, b * width : (b + 1) * width].astype(jnp.float32)
         drive[b] = (part * on).astype(jnp.bfloat16)
     for k in range(n - 1):
@@ -118,6 +119,7 @@
     for k in range(n):
         copies[5 + k].wait()
         send_slots(chosen.at[k], tiles.at[k], metas[k], out.at[k])
+    across[...] = out[0]
     for copy in copies[5 + n :]:
         copy.wait()
 
@@ -127,22 +129,24 @@
         send_slots(chosen.at[k], tiles.at[k], meta[k], out.at[k])
 
 
-def merge_kernel(n, sibling, mine, drive, drive_x, *outs):
+def merge_kernel(n, sibling, mine, *outs):
     for k in range(n):
         outs[k][0] = mine[k]
         outs[k][1] = sibling[k + 1]
-    outs[n][...] = sibling[0]
+
+
+def pair_kernel(drive, drive_x, pair):
     half = lax.axis_index("local") % HALVES
-    outs[n + 1][half] = drive[...]
-    outs[n + 1][1 - half] = drive_x[...]
+    pair[half] = drive[...]
+    pair[1 - half] = drive_x[...]
 
 
 def gather_kernel(n_in, n_far, own_blocks, *refs):
     ins = refs[:n_in]
     outs = refs[n_in : n_in + n_far - 1]
     own, total, ids, ids_s, sem = refs[n_in + n_far - 1 :]
-    packs = []
-    for r in ins:
+    packs = [ins[0].at[0]]
+    for r in ins[1:]:
         packs += [r] if len(r.shape) == 3 else [r.at[i] for i in range(r.shape[0])]
     slots = packs[0].shape[0] - 1
     steps, width = packs[0].shape[1:]
@@ -174,29 +178,19 @@
         outs[k - 1][own_blocks] = meta.astype(jnp.int16)
 
 
-def inner_kernel(n_far, *refs):
+def inner_kernel(n_far, order, *refs):
     pairs = refs[:n_far]
-    weight, out, held, sems = refs[n_far:]
+    weight, out = refs[n_far:]
     halves, own_blocks, steps, width = pairs[0].shape
     depth = own_blocks * width
     far = lax.axis_index("local") // HALVES
-    copies = load_all(
-        [
-            (
-                weight.at[pl.ds(pl.multiple_of(((far ^ k) * halves + h) * depth, depth), depth)],
-                held.at[k * halves + h],
-            )
-            for k in range(n_far)
-            for h in range(halves)
-        ],
-        sems,
-    )
     total = jnp.zeros(out.shape, jnp.float32)
     for k in range(n_far):
-        for h in range(halves):
-            left = jnp.concatenate([pairs[k][h, b] for b in range(own_blocks)], axis=1)
-            copies[k * halves + h].wait()
-            total += jnp.dot(left, held[k * halves + h], preferred_element_type=jnp.float32)
+        left = jnp.concatenate(
+            [pairs[k][h, b] for h in range(halves) for b in range(own_blocks)], axis=1
+        )
+        rows = pl.ds(pl.multiple_of((far ^ order[k]) * halves * depth, halves * depth), halves * depth)
+        total += jnp.dot(left, weight[rows, :], preferred_element_type=jnp.float32)
     out[...] = total
 
 
@@ -255,17 +249,18 @@
         ]
         return lax.ppermute(value, ("region", "local"), pairs)
 
-    drive, theirs, *rest = pl.pallas_call(
+    drive, theirs, across, *rest = pl.pallas_call(
         functools.partial(first_kernel, per_half),
         out_shape=[
             shape((own_blocks, steps, width), bf16),
             shape((n_hi, slots + 1, steps, width), i16),
+            shape((slots + 1, steps, width), i16),
             shape((n_hi - 1, slots, width, width), bf16),
             shape((n_hi - 1, slots, steps, width), bf16),
             shape((n_hi - 1, steps, width), i32),
         ],
         in_specs=[HBM] * 6,
-        out_specs=[VMEM] * 5,
+        out_specs=[VMEM] * 6,
         scratch_shapes=[
             pltpu.VMEM((own_blocks, steps), i32),
             pltpu.VMEM((steps, neurons), bf16),
@@ -286,6 +281,7 @@
     )
     sibling = to(theirs, 1, 0)
     drive_x = to(drive, 0, 1)
+    beside = to(across, 1, 1)
     tiles, chosen, meta = rest
     mine = pl.pallas_call(
         second_kernel,
@@ -295,25 +291,32 @@
         compiler_params=PARAMS,
         name="second_partials",
     )(chosen, meta, tiles)
-    *merged, beside, pair = pl.pallas_call(
+    merged = pl.pallas_call(
         functools.partial(merge_kernel, n_hi - 1),
-        out_shape=[shape((2, slots + 1, steps, width), i16)] * (n_hi - 1)
-        + [
-            shape((slots + 1, steps, width), i16),
-            shape((HALVES, own_blocks, steps, width), bf16),
-        ],
-        in_specs=[VMEM] * 4,
-        out_specs=[VMEM] * (n_hi + 1),
+        out_shape=[shape((2, slots + 1, steps, width), i16)] * (n_hi - 1),
+        in_specs=[VMEM] * 2,
+        out_specs=[VMEM] * (n_hi - 1),
         compiler_params=PARAMS,
         name="merge",
-    )(sibling, mine, drive, drive_x)
-    arrived = [beside]
+    )(sibling, mine)
+    pair = pl.pallas_call(
+        pair_kernel,
+        out_shape=shape((HALVES, own_blocks, steps, width), bf16),
+        in_specs=[VMEM] * 2,
+        out_specs=VMEM,
+        compiler_params=PARAMS,
+        cost_estimate=pl.CostEstimate(flops=1 << 36, bytes_accessed=1 << 28, transcendentals=1 << 26),
+        name="pair",
+    )(drive, drive_x)
+    arrived = [sibling, beside]
     for k in range(1, n_hi):
         for h in range(HALVES):
             arrived.append(to(merged[k - 1], CORES * k, h))
-    arrived.append(to(beside, 0, 1))
-    far_first = sorted(range(1, n_far), key=lambda k: (k == 1, k))
-    pairs = {k: to(pair, 0, k * HALVES) for k in far_first}
+    drive_order = [2, 3, 1] if n_far == 4 else list(range(1, n_far))
+    use_order = [2, 3, 1] if n_far == 4 else list(range(1, n_far))
+    sum_order = [2, 3, 1] if n_far == 4 else list(range(1, n_far))
+    add_order = [1, 2, 3] if n_far == 4 else list(range(1, n_far))
+    pairs = {k: to(pair, 0, k * HALVES) for k in drive_order}
 
     n_packs = 2 + (n_hi - 1) * HALVES * 2
     far_sent = shape((own_blocks + 1, steps, width), i16)
@@ -329,19 +332,16 @@
             pltpu.SemaphoreType.DMA,
         ],
         compiler_params=PARAMS,
+        cost_estimate=pl.CostEstimate(flops=1 << 36, bytes_accessed=1 << 28, transcendentals=1 << 26),
         name="add_arrived",
     )(*arrived)
-    far = [to(sums[k - 1], 0, k * HALVES) for k in far_first]
+    far = {k: to(sums[k - 1], 0, k * HALVES) for k in sum_order}
 
     inner = pl.pallas_call(
-        functools.partial(inner_kernel, n_far),
+        functools.partial(inner_kernel, n_far, (0, *use_order)),
         out_shape=shape((steps, neurons), f32),
-        in_specs=[VMEM] * n_far + [HBM],
+        in_specs=[VMEM] * (n_far + 1),
         out_specs=VMEM,
-        scratch_shapes=[
-            pltpu.VMEM((locals_, neurons, neurons), bf16),
-            pltpu.SemaphoreType.DMA((locals_,)),
-        ],
         compiler_params=PARAMS,
         cost_estimate=pl.CostEstimate(
             flops=2 * steps * neurons * neurons * locals_,
@@ -349,7 +349,7 @@
             transcendentals=0,
         ),
         name="inner",
-    )(pair, *[pairs[k] for k in range(1, n_far)], in_hbm(w_region[0]))
+    )(pair, *[pairs[k] for k in use_order], w_region[0])
 
     return pl.pallas_call(
         functools.partial(advance_kernel, n_far - 1),
@@ -359,7 +359,7 @@
         scratch_shapes=[pltpu.VMEM((steps, neurons), f32)],
         compiler_params=PARAMS,
         name="advance",
-    )(inner, own, *far, g_decay, v_decay, g_start, v_start)
+    )(inner, own, *[far[k] for k in add_order], g_decay, v_decay, g_start, v_start)
 
 
 def solution(mesh):

time: 28.9 us -> 27.1 us (0.938)
  Pallas kernels: 8.77 us -> 6.37 us
  waiting for transfers between devices: 3.2 us -> 4.57 us
  starting transfers between devices: 16 us -> 15.2 us
    pallas_call x1 -> x2, Pallas kernels: 4.14 us -> 1.75 us  [the longest x1 1.73 us: local(): pl.pallas_call(functools.partial(inner_kernel, n_far, (0, *use_order)), o...]
    ppermute x11, waiting for transfers between devices: 3.2 us -> 4.57 us  [to(): return lax.ppermute(value, ('region', 'local'), pairs)]
    ppermute x11, starting transfers between devices: 16 us -> 15.2 us  [to(): return lax.ppermute(value, ('region', 'local'), pairs)]
  transfers between devices with their start and end apart: 11 -> 11, of which waited for: 4 -> 3; matrix products, arithmetic and copies ran while one was open for 0% -> 0% of each run, Pallas kernels for 21% -> 14%
where the time goes in v4:
time: 27.1 us; the launch traced here: 26.9 us
  starting transfers between devices  15.2 us (56%)
  Pallas kernels  6.37 us (24%)
  waiting for transfers between devices  4.57 us (17%)
  between operations  0.78 us (3%)
    ppermute x11, starting transfers between devices, to(): return lax.ppermute(value, ('region', 'local'), pairs)  15.2 us
    ppermute x11, waiting for transfers between devices, to(): return lax.ppermute(value, ('region', 'local'), pairs)  4.57 us
    pallas_call x1, Pallas kernels, local(): pl.pallas_call(functools.partial(first_kernel, per_half), out_shape=[shap...  1.85 us
    pallas_call x1, Pallas kernels, local(): pl.pallas_call(functools.partial(inner_kernel, n_far, (0, *use_order)), o...  1.73 us
    pallas_call x1, Pallas kernels, local(): pl.pallas_call(functools.partial(gather_kernel, len(arrived), n_far, own_...  1.59 us
    pallas_call x1, Pallas kernels, local(): pl.pallas_call(functools.partial(advance_kernel, n_far - 1), out_shape=[s...  0.87 us
  transfers between devices with their start and end apart: 11, of which 3 were waited for; matrix products, arithmetic and copies ran while one was open for 0% of the time, Pallas kernels for 14%

profile of v4, /device:TPU:0, one launch (start us, length us, event | category | flops | bytes accessed | tf_op | source)
XLA Modules:
  0.0 26.9 jit_solution(4597890680711805698)
XLA Ops:
  0.6 1.9 %first_partials.1 = (bf16[6,32,128]{2,1,0:T(8,128)(2,1)S(1)}, s16[2,9,32,128]{3,2,1,0:T(8,128)(2,1)S(1)}, s16[9,32,128]{2,1,0:T(8,128)(2,1)S(1)}, bf16[1,8,128,1...) custom-call(s32[6,32]{1,0:T(8,128)} %bitcast.10, bf16[32,768]{1,0:T(8,128)(2,1)} %trace_h.1, ...), custom_call_target="tpu_custom_call" | custom-call | tf_op jit(solution)/shard_map/first_partials/pallas_call | solution.py:252
  2.5 0.5 %collective-permute-start.4 = (s16[2,9,32,128]{3,2,1,0:T(8,128)(2,1)S(1)}, s16[2,9,32,128]{3,2,1,0:T(8,128)(2,1)S(1)}, u32[]{:S(2)}, u32[]{:S(2)}) collective-permute-start(s16[2,9,32,128]{3,2,1,0:T(8,128)(2,1)S(1)} %get-tuple-element.13), channel_id=1, source_target_pairs={{0,8},{1,9},{2,10},{3,11},{4,12},{5,13},{6,14},{7,15},{8,0},{9,1},... | collective-permute-start | bytes 442376 | tf_op jit(solution)/shard_map/ppermute | solution.py:250
  3.0 2.6 %collective-permute-start = (bf16[6,32,128]{2,1,0:T(8,128)(2,1)S(1)}, bf16[6,32,128]{2,1,0:T(8,128)(2,1)S(1)}, u32[]{:S(2)}, u32[]{:S(2)}) collective-permute-start(bf16[6,32,128]{2,1,0:T(8,128)(2,1)S(1)} %get-tuple-element.12.drive), channel_id=1, source_target_pairs={{0,1},{1,0},{2,3},{3,2},{4,5},{5,4},{6,7},{7,6},{8,9},{9,8},{10,11... | collective-permute-start | bytes 147464 | tf_op jit(solution)/shard_map/ppermute | solution.py:250
  5.6 0.1 collective-permute-start.5
  5.6 0.3 %second_partials.1.mine = s16[1,9,32,128]{3,2,1,0:T(8,128)(2,1)S(1)} custom-call(bf16[1,8,32,128]{3,2,1,0:T(8,128)(2,1)S(1)} %get-tuple-element.15.chosen, s32[1,32,128]{2,1,0:T(8,128)S(1)} %get-tuple-element.16.meta, bf16[1,8,128,128]{3,2,1,0:T(8,128)(2,1)S(1)} %get-tuple-element.17.tiles), custom_call_target="tpu_custom_call" | custom-call | tf_op jit(solution)/shard_map/second_partials/pallas_call | solution.py:286
  5.9 0.0 collective-permute-done.4.sibling.refs_0_
  6.0 1.8 %collective-permute-start.6 = (s16[2,9,32,128]{3,2,1,0:T(8,128)(2,1)S(1)}, s16[2,9,32,128]{3,2,1,0:T(8,128)(2,1)S(1)}, u32[]{:S(2)}, u32[]{:S(2)}) collective-permute-start(s16[2,9,32,128]{3,2,1,0:T(8,128)(2,1)S(1)} %merge.1), channel_id=1, source_target_pairs={{0,16},{1,17},{2,18},{3,19},{4,20},{5,21},{6,22},{7,23},{8,24},{9,... | collective-permute-start | bytes 442376 | tf_op jit(solution)/shard_map/ppermute | solution.py:250
  7.8 1.4 %collective-permute-start.7 = (s16[2,9,32,128]{3,2,1,0:T(8,128)(2,1)S(1)}, s16[2,9,32,128]{3,2,1,0:T(8,128)(2,1)S(1)}, u32[]{:S(2)}, u32[]{:S(2)}) collective-permute-start(s16[2,9,32,128]{3,2,1,0:T(8,128)(2,1)S(1)} %merge.1), channel_id=1, source_target_pairs={{0,17},{1,16},{2,19},{3,18},{4,21},{5,20},{6,23},{7,22},{8,25},{9,... | collective-permute-start | bytes 442376 | tf_op jit(solution)/shard_map/ppermute | solution.py:250
  9.2 0.0 collective-permute-done.drive_x
  9.2 0.0 slice-start
  9.2 0.0 slice-start.1
  9.3 0.0 slice-start.2
  9.3 2.7 %collective-permute-start.1 = (bf16[2,6,32,128]{3,2,1,0:T(8,128)(2,1)S(1)}, bf16[2,6,32,128]{3,2,1,0:T(8,128)(2,1)S(1)}, u32[]{:S(2)}, u32[]{:S(2)}) collective-permute-start(bf16[2,6,32,128]{3,2,1,0:T(8,128)(2,1)S(1)} %pair.1.refs_0_), channel_id=1, source_target_pairs={{0,4},{1,5},{2,6},{3,7},{4,0},{5,1},{6,2},{7,3},{8,12},{9,13},{10,... | collective-permute-start | bytes 294920 | tf_op jit(solution)/shard_map/ppermute | solution.py:250
  11.9 1.3 %collective-permute-start.2 = (bf16[2,6,32,128]{3,2,1,0:T(8,128)(2,1)S(1)}, bf16[2,6,32,128]{3,2,1,0:T(8,128)(2,1)S(1)}, u32[]{:S(2)}, u32[]{:S(2)}) collective-permute-start(bf16[2,6,32,128]{3,2,1,0:T(8,128)(2,1)S(1)} %pair.1.refs_0_), channel_id=1, source_target_pairs={{0,6},{1,7},{2,4},{3,5},{4,2},{5,3},{6,0},{7,1},{8,14},{9,15},{10,... | collective-permute-start | bytes 294920 | tf_op jit(solution)/shard_map/ppermute | solution.py:250
  13.3 0.0 collective-permute-done.5.refs_1_
  13.3 0.2 collective-permute-start.3
  13.5 1.8 %collective-permute-done.6.refs_2_ = s16[2,9,32,128]{3,2,1,0:T(8,128)(2,1)S(1)} collective-permute-done((s16[2,9,32,128]{3,2,1,0:T(8,128)(2,1)S(1)}, s16[2,9,32,128]{3,2,1,0:T(8,128)(2,1)S(1)}, u32[]{:S(2)}, u32[]{:S(2)}) %collective-permute-start.6) | collective-permute-done | bytes 147488 | tf_op jit(solution)/shard_map/ppermute | solution.py:250
  15.3 0.0 collective-permute-done.7.refs_3_
  15.3 1.6 %add_arrived.1 = (s16[7,32,128]{2,1,0:T(8,128)(2,1)S(1)}, s16[7,32,128]{2,1,0:T(8,128)(2,1)S(1)}, s16[7,32,128]{2,1,0:T(8,128)(2,1)S(1)}, f32[6,32,128]{2,1,0:T(8,128)S(1)}) custom-call(s16[2,9,32,128]{3,2,1,0:T(8,128)(2,1)S(1)} %collective-permute-done.4.sibling.refs_0_, s16[9,32,128]{2,1,0:T(8,128)(2,1)S(1)} %collective-permute-done.5.refs_1_, ...), custom_call_target="tpu_custom_call" | custom-call | flops 68719476736 | bytes 268435456 | tf_op jit(solution)/shard_map/add_arrived/pallas_call | solution.py:323
  16.9 0.0 copy-start
  16.9 0.0 copy-start.1
  16.9 0.0 copy-start.2
  16.9 0.0 copy-start.3
  17.0 3.9 %collective-permute-start.10 = (s16[7,32,128]{2,1,0:T(8,128)(2,1)S(1)}, s16[7,32,128]{2,1,0:T(8,128)(2,1)S(1)}, u32[]{:S(2)}, u32[]{:S(2)}) collective-permute-start(s16[7,32,128]{2,1,0:T(8,128)(2,1)S(1)} %get-tuple-element.21), channel_id=1, source_target_pairs={{0,6},{1,7},{2,4},{3,5},{4,2},{5,3},{6,0},{7,1},{8,14},{9,15},{10,... | collective-permute-start | bytes 172040 | tf_op jit(solution)/shard_map/ppermute | solution.py:250
  20.8 0.0 collective-permute-start.8
  20.8 0.0 collective-permute-done.1.refs_1_
  20.8 0.6 %collective-permute-start.9 = (s16[7,32,128]{2,1,0:T(8,128)(2,1)S(1)}, s16[7,32,128]{2,1,0:T(8,128)(2,1)S(1)}, u32[]{:S(2)}, u32[]{:S(2)}) collective-permute-start(s16[7,32,128]{2,1,0:T(8,128)(2,1)S(1)} %get-tuple-element.20), channel_id=1, source_target_pairs={{0,4},{1,5},{2,6},{3,7},{4,0},{5,1},{6,2},{7,3},{8,12},{9,13},{10,... | collective-permute-start | bytes 172040 | tf_op jit(solution)/shard_map/ppermute | solution.py:250
  21.5 0.0 collective-permute-done.2.refs_2_
  21.5 0.0 collective-permute-done.3.refs_3_
  21.5 0.0 slice-done
  21.5 0.0 slice-done.1
  21.5 0.0 slice-done.2
  21.5 1.7 %inner.1 = f32[32,768]{1,0:T(8,128)S(1)} custom-call(bf16[2,6,32,128]{3,2,1,0:T(8,128)(2,1)S(1)} %pair.1.refs_0_, bf16[2,6,32,128]{3,2,1,0:T(8,128)(2,1)S(1)} %collective-permute-done.1.refs_1_, bf16[2,6,32,128]{3,2,1,0:T(8,128)(2,1)S(1)} %collective-permute-done.2.refs_2_, bf16[2,6,32,128]{3,2,1,0:T(8,128)(2,1)S(1)} %collective-permute-done.3.refs_3_, ...), custom_call_target="tpu_custom_call" | custom-call | flops 301989888 | bytes 9437184 | tf_op jit(solution)/shard_map/inner/pallas_call | solution.py:340
  23.3 0.0 collective-permute-done.10.refs_2_
  23.3 1.7 %collective-permute-done.8.refs_0_ = s16[7,32,128]{2,1,0:T(8,128)(2,1)S(1)} collective-permute-done((s16[7,32,128]{2,1,0:T(8,128)(2,1)S(1)}, s16[7,32,128]{2,1,0:T(8,128)(2,1)S(1)}, u32[]{:S(2)}, u32[]{:S(2)}) %collective-permute-start.8) | collective-permute-done | bytes 57376 | tf_op jit(solution)/shard_map/ppermute | solution.py:250
  25.0 1.0 %collective-permute-done.9.refs_1_ = s16[7,32,128]{2,1,0:T(8,128)(2,1)S(1)} collective-permute-done((s16[7,32,128]{2,1,0:T(8,128)(2,1)S(1)}, s16[7,32,128]{2,1,0:T(8,128)(2,1)S(1)}, u32[]{:S(2)}, u32[]{:S(2)}) %collective-permute-start.9) | collective-permute-done | bytes 57376 | tf_op jit(solution)/shard_map/ppermute | solution.py:250
  26.0 0.0 copy-done
  26.0 0.0 copy-done.1
  26.0 0.0 copy-done.2
  26.0 0.0 copy-done.3
  26.0 0.9 %advance.1 = (f32[32,768]{1,0:T(8,128)}, f32[768]{0:T(1024)}) custom-call(f32[32,768]{1,0:T(8,128)S(1)} %inner.1, f32[6,32,128]{2,1,0:T(8,128)S(1)} %get-tuple-element.18.own, s16[7,32,128]{2,1,0:T(8,128)(2,1)S(1)} %collective-permute-done.8.refs_0_, s16[7,32,128]{2,1,0:T(8,128)(2,1)S(1)} %collective-permute-done.9.refs_1_, ...), custom_call_target="tpu_custom_call" | custom-call | tf_op jit(solution)/shard_map/advance/pallas_call | solution.py:354
  (3 shorter events, 0.0 us)
Async XLA Ops:
  2.5 3.4 %collective-permute-start.4 = (s16[2,9,32,128]{3,2,1,0:T(8,128)(2,1)S(1)}, s16[2,9,32,128]{3,2,1,0:T(8,128)(2,1)S(1)}, u32[]{:S(2)}, u32[]{:S(2)}) collective-permute-start(s16[2,9,32,128]{3,2,1,0:T(8,128)(2,1)S(1)} %get-tuple-element.13), channel_id=1, source_target_pairs={{0,8},{1,9},{2,10},{3,11},{4,12},{5,13},{6,14},{7,15},{8,0},{9,1},... | collective-permute-start | bytes 442376 | tf_op jit(solution)/shard_map/ppermute | solution.py:250
  3.0 6.2 %collective-permute-start = (bf16[6,32,128]{2,1,0:T(8,128)(2,1)S(1)}, bf16[6,32,128]{2,1,0:T(8,128)(2,1)S(1)}, u32[]{:S(2)}, u32[]{:S(2)}) collective-permute-start(bf16[6,32,128]{2,1,0:T(8,128)(2,1)S(1)} %get-tuple-element.12.drive), channel_id=1, source_target_pairs={{0,1},{1,0},{2,3},{3,2},{4,5},{5,4},{6,7},{7,6},{8,9},{9,8},{10,11... | collective-permute-start | bytes 147464 | tf_op jit(solution)/shard_map/ppermute | solution.py:250
  5.6 7.7 %collective-permute-start.5 = (s16[9,32,128]{2,1,0:T(8,128)(2,1)S(1)}, s16[9,32,128]{2,1,0:T(8,128)(2,1)S(1)}, u32[]{:S(2)}, u32[]{:S(2)}) collective-permute-start(s16[9,32,128]{2,1,0:T(8,128)(2,1)S(1)} %get-tuple-element.14), channel_id=1, source_target_pairs={{0,9},{1,8},{2,11},{3,10},{4,13},{5,12},{6,15},{7,14},{8,1},{9,0},... | collective-permute-start | bytes 221192 | tf_op jit(solution)/shard_map/ppermute | solution.py:250
  6.0 9.3 %collective-permute-start.6 = (s16[2,9,32,128]{3,2,1,0:T(8,128)(2,1)S(1)}, s16[2,9,32,128]{3,2,1,0:T(8,128)(2,1)S(1)}, u32[]{:S(2)}, u32[]{:S(2)}) collective-permute-start(s16[2,9,32,128]{3,2,1,0:T(8,128)(2,1)S(1)} %merge.1), channel_id=1, source_target_pairs={{0,16},{1,17},{2,18},{3,19},{4,20},{5,21},{6,22},{7,23},{8,24},{9,... | collective-permute-start | bytes 442376 | tf_op jit(solution)/shard_map/ppermute | solution.py:250
  7.8 7.5 %collective-permute-start.7 = (s16[2,9,32,128]{3,2,1,0:T(8,128)(2,1)S(1)}, s16[2,9,32,128]{3,2,1,0:T(8,128)(2,1)S(1)}, u32[]{:S(2)}, u32[]{:S(2)}) collective-permute-start(s16[2,9,32,128]{3,2,1,0:T(8,128)(2,1)S(1)} %merge.1), channel_id=1, source_target_pairs={{0,17},{1,16},{2,19},{3,18},{4,21},{5,20},{6,23},{7,22},{8,25},{9,... | collective-permute-start | bytes 442376 | tf_op jit(solution)/shard_map/ppermute | solution.py:250
  9.2 12.3 %slice-start = ((s8[9437184]{0:T(1024)(128)(4,1)}), s8[4194304]{0:T(1024)(128)(4,1)S(1)}, s32[]{:S(2)}) async-start(s8[9437184]{0:T(1024)(128)(4,1)} %bitcast.6), calls=%async_computation | async-start | bytes 8388608
  9.2 12.3 %slice-start.1 = ((s8[9437184]{0:T(1024)(128)(4,1)}), s8[4194304]{0:T(1024)(128)(4,1)S(1)}, s32[]{:S(2)}) async-start(s8[9437184]{0:T(1024)(128)(4,1)} %bitcast.6), calls=%async_computation.1 | async-start | bytes 8388608
  9.3 12.3 %slice-start.2 = ((s8[9437184]{0:T(1024)(128)(4,1)}), s8[1048576]{0:T(1024)(128)(4,1)S(1)}, s32[]{:S(2)}) async-start(s8[9437184]{0:T(1024)(128)(4,1)} %bitcast.6), calls=%async_computation.2 | async-start | bytes 2097152
  9.3 11.6 %collective-permute-start.1 = (bf16[2,6,32,128]{3,2,1,0:T(8,128)(2,1)S(1)}, bf16[2,6,32,128]{3,2,1,0:T(8,128)(2,1)S(1)}, u32[]{:S(2)}, u32[]{:S(2)}) collective-permute-start(bf16[2,6,32,128]{3,2,1,0:T(8,128)(2,1)S(1)} %pair.1.refs_0_), channel_id=1, source_target_pairs={{0,4},{1,5},{2,6},{3,7},{4,0},{5,1},{6,2},{7,3},{8,12},{9,13},{10,... | collective-permute-start | bytes 294920 | tf_op jit(solution)/shard_map/ppermute | solution.py:250
  11.9 9.6 %collective-permute-start.2 = (bf16[2,6,32,128]{3,2,1,0:T(8,128)(2,1)S(1)}, bf16[2,6,32,128]{3,2,1,0:T(8,128)(2,1)S(1)}, u32[]{:S(2)}, u32[]{:S(2)}) collective-permute-start(bf16[2,6,32,128]{3,2,1,0:T(8,128)(2,1)S(1)} %pair.1.refs_0_), channel_id=1, source_target_pairs={{0,6},{1,7},{2,4},{3,5},{4,2},{5,3},{6,0},{7,1},{8,14},{9,15},{10,... | collective-permute-start | bytes 294920 | tf_op jit(solution)/shard_map/ppermute | solution.py:250
  13.3 8.2 %collective-permute-start.3 = (bf16[2,6,32,128]{3,2,1,0:T(8,128)(2,1)S(1)}, bf16[2,6,32,128]{3,2,1,0:T(8,128)(2,1)S(1)}, u32[]{:S(2)}, u32[]{:S(2)}) collective-permute-start(bf16[2,6,32,128]{3,2,1,0:T(8,128)(2,1)S(1)} %pair.1.refs_0_), channel_id=1, source_target_pairs={{0,2},{1,3},{2,0},{3,1},{4,6},{5,7},{6,4},{7,5},{8,10},{9,11},{10,... | collective-permute-start | bytes 294920 | tf_op jit(solution)/shard_map/ppermute | solution.py:250
  16.9 9.1 %copy-start = (f32[768]{0:T(1024)S(1)}, f32[768]{0:T(1024)}, u32[]{:S(2)}) copy-start(f32[768]{0:T(1024)} %refs_3_.1) | copy-start | bytes 9220
  16.9 9.1 %copy-start.1 = (f32[768]{0:T(1024)S(1)}, f32[768]{0:T(1024)}, u32[]{:S(2)}) copy-start(f32[768]{0:T(1024)} %refs_4_.1) | copy-start | bytes 9220
  16.9 9.1 %copy-start.2 = (f32[768]{0:T(1024)S(1)}, f32[768]{0:T(1024)}, u32[]{:S(2)}) copy-start(f32[768]{0:T(1024)} %refs_5_.1) | copy-start | bytes 9220
  16.9 9.1 %copy-start.3 = (f32[768]{0:T(1024)S(1)}, f32[768]{0:T(1024)}, u32[]{:S(2)}) copy-start(f32[768]{0:T(1024)} %refs_6_.1) | copy-start | bytes 9220
  17.0 6.3 %collective-permute-start.10 = (s16[7,32,128]{2,1,0:T(8,128)(2,1)S(1)}, s16[7,32,128]{2,1,0:T(8,128)(2,1)S(1)}, u32[]{:S(2)}, u32[]{:S(2)}) collective-permute-start(s16[7,32,128]{2,1,0:T(8,128)(2,1)S(1)} %get-tuple-element.21), channel_id=1, source_target_pairs={{0,6},{1,7},{2,4},{3,5},{4,2},{5,3},{6,0},{7,1},{8,14},{9,15},{10,... | collective-permute-start | bytes 172040 | tf_op jit(solution)/shard_map/ppermute | solution.py:250
  20.8 4.2 %collective-permute-start.8 = (s16[7,32,128]{2,1,0:T(8,128)(2,1)S(1)}, s16[7,32,128]{2,1,0:T(8,128)(2,1)S(1)}, u32[]{:S(2)}, u32[]{:S(2)}) collective-permute-start(s16[7,32,128]{2,1,0:T(8,128)(2,1)S(1)} %get-tuple-element.19), channel_id=1, source_target_pairs={{0,2},{1,3},{2,0},{3,1},{4,6},{5,7},{6,4},{7,5},{8,10},{9,11},{10,... | collective-permute-start | bytes 172040 | tf_op jit(solution)/shard_map/ppermute | solution.py:250
  20.8 5.2 %collective-permute-start.9 = (s16[7,32,128]{2,1,0:T(8,128)(2,1)S(1)}, s16[7,32,128]{2,1,0:T(8,128)(2,1)S(1)}, u32[]{:S(2)}, u32[]{:S(2)}) collective-permute-start(s16[7,32,128]{2,1,0:T(8,128)(2,1)S(1)} %get-tuple-element.20), channel_id=1, source_target_pairs={{0,4},{1,5},{2,6},{3,7},{4,0},{5,1},{6,2},{7,3},{8,12},{9,13},{10,... | collective-permute-start | bytes 172040 | tf_op jit(solution)/shard_map/ppermute | solution.py:250

commit v5 on v4

v5 whole, which is shorter than its diff:
```python
import functools

import jax
import jax.numpy as jnp
from jax import lax
from jax.experimental import pallas as pl
from jax.experimental.pallas import tpu as pltpu
from jax.sharding import PartitionSpec as P

TOP = 32766.0
VMEM = pl.BlockSpec(memory_space=pltpu.VMEM)
HBM = pl.BlockSpec(memory_space=pltpu.HBM)
in_hbm = functools.partial(pltpu.with_memory_space_constraint, memory_space=pltpu.HBM)
PARAMS = pltpu.CompilerParams(vmem_limit_bytes=24 << 20)
CORES = 2
HALVES = 2
SHIFT = 32


def code(value):
    most = jnp.max(jnp.abs(value), axis=-1, keepdims=True)
    power = jnp.ceil(jnp.log2(jnp.maximum(most, 1e-30)) + 1e-5)
    whole = jnp.round(value * (jnp.exp2(-power) * TOP))
    return whole.astype(jnp.int32).astype(jnp.int16), power.astype(jnp.int32)


def put_power(meta, lane, first, count, j, power):
    half = meta.shape[0]
    meta = jnp.where(lane == first + j, power[:half], meta)
    return jnp.where(lane == first + count + j, power[half:], meta)


def scales_of(meta):
    return jnp.exp2(meta.astype(jnp.float32)) * (1.0 / TOP)


def scale_of(scales, first, count, j):
    upper, lower = first + j, first + count + j
    return jnp.concatenate([scales[:, upper : upper + 1], scales[:, lower : lower + 1]], axis=0)


def load_all(pairs, sems):
    copies = [pltpu.make_async_copy(a, b, sems.at[i]) for i, (a, b) in enumerate(pairs)]
    for copy in copies:
        copy.start()
    return copies


def choose(dest, blocks, source, target, count, per_half, first, chosen):
    own_blocks, steps, width = blocks.shape
    slots = source.shape[1]
    lane = lax.broadcasted_iota(jnp.int32, (steps // 2, width), 1)
    live = count[0, dest]
    meta = jnp.zeros((steps // 2, width), jnp.int32)
    for j in range(slots):
        chosen[j] = blocks[source[dest, j]]
        block = target[dest, j]
        owner = (block * (-(-65536 // own_blocks))) >> 16
        place = (owner % HALVES) * per_half + (owner // HALVES) * own_blocks
        place = jnp.where(j < live, place + block - owner * own_blocks, -1)
        meta = jnp.where(lane == first + 2 * slots + j, place, meta)
    return meta


def send_slots(chosen, tiles, meta, first, out):
    slots, steps, _ = chosen.shape
    lane = lax.broadcasted_iota(jnp.int32, meta.shape, 1)
    for j in range(slots):
        part = jnp.dot(chosen[j], tiles[j], preferred_element_type=jnp.float32)
        whole, power = code(part)
        out[j * steps : (j + 1) * steps] = whole
        meta = put_power(meta, lane, first, slots, j, power)
    out[slots * steps :] = meta.astype(jnp.int16)


def first_kernel(
    per_half,
    flags_h,
    trace_h,
    source_h,
    target_h,
    count_h,
    weight,
    drive,
    out,
    next_tiles,
    next_chosen,
    next_meta,
    flags,
    trace,
    source,
    target,
    count,
    tiles,
    chosen,
    sems,
):
    n = out.shape[0]
    own_blocks, steps, width = drive.shape
    region = lax.axis_index("region")
    copies = load_all(
        [(flags_h, flags), (trace_h, trace), (source_h, source), (target_h, target), (count_h, count)]
        + [(weight.at[region ^ 1 ^ (CORES * k)], tiles.at[k]) for k in range(n)]
        + [(weight.at[region ^ (CORES * (k + 1))], next_tiles.at[k]) for k in range(n - 1)],
        sems,
    )
    for copy in copies[:5]:
        copy.wait()
    row = lax.broadcasted_iota(jnp.int32, (steps, steps), 0)
    col = lax.broadcasted_iota(jnp.int32, (steps, steps), 1)
    for b in range(own_blocks):
        spread = jnp.where(row == col, flags[b : b + 1, :], 0).astype(jnp.float32)
        on = jnp.sum(spread, axis=1, keepdims=True)
        part = trace[:, b * width : (b + 1) * width].astype(jnp.float32)
        drive[b] = (part * on).astype(jnp.bfloat16)
    for k in range(n - 1):
        next_meta[k] = choose(
            region ^ (CORES * (k + 1)), drive, source, target, count, per_half, SHIFT, next_chosen.at[k]
        )
    metas = [
        choose(region ^ 1 ^ (CORES * k), drive, source, target, count, per_half, 0, chosen.at[k])
        for k in range(n)
    ]
    for k in range(n):
        copies[5 + k].wait()
        send_slots(chosen.at[k], tiles.at[k], metas[k], 0, out.at[k])
    for copy in copies[5 + n :]:
        copy.wait()


def second_kernel(chosen, meta, tiles, theirs, out, across):
    across[...] = theirs[0]
    for k in range(out.shape[0]):
        send_slots(chosen.at[k], tiles.at[k], meta[k], SHIFT, out.at[k])


def merge_kernel(n, rows, sibling, mine, *outs):
    for k in range(n):
        outs[k][:rows] = mine[k, :rows]
        outs[k][rows : 2 * rows] = sibling[k + 1, :rows]
        meta = mine[k, rows:].astype(jnp.int32) + sibling[k + 1, rows:].astype(jnp.int32)
        outs[k][2 * rows :] = meta.astype(jnp.int16)


def pair_kernel(drive, drive_x, pair):
    half = lax.axis_index("local") % HALVES
    pair[half] = drive[...]
    pair[1 - half] = drive_x[...]


def add_packs(packs, slots, steps, per_half, total):
    half = lax.axis_index("local") % HALVES
    for ref, row, meta, first in packs:
        block = ref[meta : meta + steps // 2]
        scales = scales_of(block)
        line = block.astype(jnp.int32)[0:1]
        for j in range(slots):
            place = line[0, first + 2 * slots + j] - half * per_half
            place = jnp.where((place >= 0) & (place < per_half), place, per_half)
            rows = ref[row + j * steps : row + (j + 1) * steps].astype(jnp.float32)
            total[place] += rows * scale_of(scales, first, slots, j)


def early_kernel(slots, sibling, beside, total):
    steps = total.shape[1]
    total[...] = jnp.zeros_like(total)
    packs = [(sibling.at[0], 0, slots * steps, 0), (beside, 0, slots * steps, 0)]
    add_packs(packs, slots, steps, total.shape[0] - 1, total)


def late_kernel(n_in, n_far, slots, own_blocks, early, *refs):
    ins = refs[:n_in]
    outs = refs[n_in : n_in + n_far - 1]
    own, total = refs[n_in + n_far - 1 :]
    steps, width = total.shape[1:]
    far = lax.axis_index("local") // HALVES
    total[...] = early[...]
    packs = []
    for r in ins:
        packs += [(r, 0, 2 * slots * steps, SHIFT), (r, slots * steps, 2 * slots * steps, 0)]
    add_packs(packs, slots, steps, n_far * own_blocks, total)
    lane = lax.broadcasted_iota(jnp.int32, (steps // 2, width), 1)
    for i in range(own_blocks):
        own[i] = total[far * own_blocks + i]
    for k in range(1, n_far):
        meta = jnp.zeros((steps // 2, width), jnp.int32)
        for i in range(own_blocks):
            whole, power = code(total[(far ^ k) * own_blocks + i])
            outs[k - 1][i * steps : (i + 1) * steps] = whole
            meta = put_power(meta, lane, 0, own_blocks, i, power)
        outs[k - 1][own_blocks * steps :] = meta.astype(jnp.int16)


def inner_kernel(n_far, order, *refs):
    pairs = refs[:n_far]
    weight, out = refs[n_far:]
    halves, own_blocks, steps, width = pairs[0].shape
    depth = own_blocks * width
    far = lax.axis_index("local") // HALVES
    total = jnp.zeros((steps, depth), jnp.float32)
    for k in range(n_far):
        left = jnp.concatenate(
            [pairs[k][h, b] for h in range(halves) for b in range(own_blocks)], axis=1
        )
        rows = pl.ds(pl.multiple_of((far ^ order[k]) * halves * depth, halves * depth), halves * depth)
        total += jnp.dot(left, weight[rows, :], preferred_element_type=jnp.float32)
    for b in range(own_blocks):
        out[b] = total[:, b * width : (b + 1) * width]


def advance_kernel(n_in, inner, own, *refs):
    ins = refs[:n_in]
    g_decay, v_decay, g_start, v_start, membrane, g_last, current = refs[n_in:]
    own_blocks, steps, width = own.shape
    neurons = own_blocks * width
    a, b = g_decay[...].reshape(1, neurons), v_decay[...].reshape(1, neurons)
    g, v = g_start[...].reshape(1, neurons), v_start[...].reshape(1, neurons)
    scales = [scales_of(r[own_blocks * steps :]) for r in ins]
    for i in range(own_blocks):
        cols = slice(i * width, (i + 1) * width)
        value = inner[i] + own[i]
        for r, scale in zip(ins, scales):
            rows = r[i * steps : (i + 1) * steps].astype(jnp.float32)
            value += rows * scale_of(scale, 0, own_blocks, i)
        current[:, cols] = (1.0 - a[:, cols]) * value
    for t in range(steps):
        g = a * g + current[t : t + 1, :]
        v = b * v + (1.0 - b) * g
        membrane[t : t + 1, :] = v
    g_last[...] = g.reshape(neurons)


def local(
    regions,
    locals_,
    block_flags,
    trace,
    w_region,
    lr_weight,
    lr_source,
    lr_target,
    lr_count,
    g_decay,
    v_decay,
    g_start,
    v_start,
):
    steps = trace.shape[0]
    own_blocks = block_flags.shape[1]
    neurons = trace.shape[1]
    width = neurons // own_blocks
    slots = lr_target.shape[3]
    n_far = locals_ // HALVES
    n_hi = regions // CORES
    per_half = n_far * own_blocks
    f32, i16, bf16, i32 = jnp.float32, jnp.int16, jnp.bfloat16, jnp.int32
    shape = jax.ShapeDtypeStruct
    rows = slots * steps
    pack_rows = rows + steps // 2

    def to(value, k, j):
        pairs = [
            (r * locals_ + l, (r ^ k) * locals_ + (l ^ j))
            for r in range(regions)
            for l in range(locals_)
        ]
        return lax.ppermute(value, ("region", "local"), pairs)

    drive, theirs, *rest = pl.pallas_call(
        functools.partial(first_kernel, per_half),
        out_shape=[
            shape((own_blocks, steps, width), bf16),
            shape((n_hi, pack_rows, width), i16),
            shape((n_hi - 1, slots, width, width), bf16),
            shape((n_hi - 1, slots, steps, width), bf16),
            shape((n_hi - 1, steps // 2, width), i32),
        ],
        in_specs=[HBM] * 6,
        out_specs=[VMEM] * 5,
        scratch_shapes=[
            pltpu.VMEM((own_blocks, steps), i32),
            pltpu.VMEM((steps, neurons), bf16),
            pltpu.SMEM((regions, slots), i32),
            pltpu.SMEM((regions, slots), i32),
            pltpu.SMEM((1, regions), i32),
            pltpu.VMEM((n_hi, slots, width, width), bf16),
            pltpu.VMEM((n_hi, slots, steps, width), bf16),
            pltpu.SemaphoreType.DMA((4 + 2 * n_hi,)),
        ],
        compiler_params=PARAMS,
        name="first_partials",
    )(
        *[
            in_hbm(x)
            for x in (block_flags.T, trace, lr_source[0, 0], lr_target[0, 0], lr_count[0], lr_weight[0, 0])
        ]
    )
    sibling = to(theirs, 1, 0)
    drive_x = to(drive, 0, 1)
    tiles, chosen, meta = rest
    mine, across = pl.pallas_call(
        second_kernel,
        out_shape=[shape((n_hi - 1, pack_rows, width), i16), shape((pack_rows, width), i16)],
        in_specs=[VMEM] * 4,
        out_specs=[VMEM] * 2,
        compiler_params=PARAMS,
        name="second_partials",
    )(chosen, meta, tiles, theirs)
    beside = to(across, 1, 1)
    merged = pl.pallas_call(
        functools.partial(merge_kernel, n_hi - 1, rows),
        out_shape=[shape((2 * rows + steps // 2, width), i16)] * (n_hi - 1),
        in_specs=[VMEM] * 2,
        out_specs=[VMEM] * (n_hi - 1),
        compiler_params=PARAMS,
        name="merge",
    )(sibling, mine)
    pair = pl.pallas_call(
        pair_kernel,
        out_shape=shape((HALVES, own_blocks, steps, width), bf16),
        in_specs=[VMEM] * 2,
        out_specs=VMEM,
        compiler_params=PARAMS,
        cost_estimate=pl.CostEstimate(flops=1 << 36, bytes_accessed=1 << 28, transcendentals=1 << 26),
        name="pair",
    )(drive, drive_x)
    arrived = []
    for k in range(1, n_hi):
        for h in range(HALVES):
            arrived.append(to(merged[k - 1], CORES * k, h))
    drive_order = [2, 3, 1] if n_far == 4 else list(range(1, n_far))
    use_order = [2, 3, 1] if n_far == 4 else list(range(1, n_far))
    sum_order = [2, 3, 1] if n_far == 4 else list(range(1, n_far))
    add_order = [1, 2, 3] if n_far == 4 else list(range(1, n_far))
    pairs = {k: to(pair, 0, k * HALVES) for k in drive_order}

    early = pl.pallas_call(
        functools.partial(early_kernel, slots),
        out_shape=shape((per_half + 1, steps, width), f32),
        in_specs=[VMEM] * 2,
        out_specs=VMEM,
        compiler_params=PARAMS,
        name="add_early",
    )(sibling, beside)
    far_sent = shape((own_blocks * steps + steps // 2, width), i16)
    *sums, own = pl.pallas_call(
        functools.partial(late_kernel, len(arrived), n_far, slots, own_blocks),
        out_shape=[far_sent] * (n_far - 1) + [shape((own_blocks, steps, width), f32)],
        in_specs=[VMEM] * (len(arrived) + 1),
        out_specs=[VMEM] * n_far,
        scratch_shapes=[pltpu.VMEM((per_half + 1, steps, width), f32)],
        compiler_params=PARAMS,
        cost_estimate=pl.CostEstimate(flops=1 << 36, bytes_accessed=1 << 28, transcendentals=1 << 26),
        name="add_late",
    )(early, *arrived)
    far = {k: to(sums[k - 1], 0, k * HALVES) for k in sum_order}

    inner = pl.pallas_call(
        functools.partial(inner_kernel, n_far, (0, *use_order)),
        out_shape=shape((own_blocks, steps, width), f32),
        in_specs=[VMEM] * (n_far + 1),
        out_specs=VMEM,
        compiler_params=PARAMS,
        cost_estimate=pl.CostEstimate(
            flops=2 * steps * neurons * neurons * locals_,
            bytes_accessed=2 * neurons * neurons * locals_,
            transcendentals=0,
        ),
        name="inner",
    )(pair, *[pairs[k] for k in use_order], w_region[0])

    return pl.pallas_call(
        functools.partial(advance_kernel, n_far - 1),
        out_shape=[shape((steps, neurons), f32), shape((neurons,), f32)],
        in_specs=[VMEM] * (n_far + 5),
        out_specs=[VMEM] * 2,
        scratch_shapes=[pltpu.VMEM((steps, neurons), f32)],
        compiler_params=PARAMS,
        name="advance",
    )(inner, own, *[far[k] for k in add_order], g_decay, v_decay, g_start, v_start)


def solution(mesh):
    return jax.shard_map(
        functools.partial(local, mesh.shape["region"], mesh.shape["local"]),
        mesh=mesh,
        in_specs=(
            P(None, ("region", "local")),
            P(None, ("region", "local")),
            P("region", None, "local"),
            P("region", "local", None, None, None, None),
            P("region", "local", None, None),
            P("region", "local", None, None),
            P("region", "local", None),
            P(("region", "local")),
            P(("region", "local")),
            P(("region", "local")),
            P(("region", "local")),
        ),
        out_specs=(P(None, ("region", "local")), P(("region", "local"))),
        check_vma=False,
    )
```

time: 27.1 us -> 26.1 us (0.963)
  Pallas kernels: 6.37 us -> 5.69 us
  starting transfers between devices: 15.2 us -> 14.8 us
    pallas_call x3 -> x4, Pallas kernels: 1.89 us -> 1.32 us  [the longest x1 0.73 us: local(): pl.pallas_call(functools.partial(late_kernel, len(arrived), n_far, slots,...]
    ppermute x11, starting transfers between devices: 15.2 us -> 14.8 us  [to(): return lax.ppermute(value, ('region', 'local'), pairs)]
  transfers between devices with their start and end apart: 11 -> 11, of which waited for: 3 -> 5; matrix products, arithmetic and copies ran while one was open for 0% -> 0% of each run, Pallas kernels for 14% -> 12%
where the time goes in v5:
time: 26.1 us; the launch traced here: 25.9 us
  starting transfers between devices  14.8 us (57%)
  Pallas kernels  5.69 us (22%)
  waiting for transfers between devices  4.64 us (18%)
  between operations  0.75 us (3%)
    ppermute x11, starting transfers between devices, to(): return lax.ppermute(value, ('region', 'local'), pairs)  14.8 us
    ppermute x11, waiting for transfers between devices, to(): return lax.ppermute(value, ('region', 'local'), pairs)  4.64 us
    pallas_call x1, Pallas kernels, local(): pl.pallas_call(functools.partial(first_kernel, per_half), out_shape=[shap...  1.75 us
    pallas_call x1, Pallas kernels, local(): pl.pallas_call(functools.partial(inner_kernel, n_far, (0, *use_order)), o...  1.73 us
    pallas_call x1, Pallas kernels, local(): pl.pallas_call(functools.partial(advance_kernel, n_far - 1), out_shape=[s...  0.89 us
    pallas_call x1, Pallas kernels, local(): pl.pallas_call(functools.partial(late_kernel, len(arrived), n_far, slots,...  0.73 us
  transfers between devices with their start and end apart: 11, of which 5 were waited for; matrix products, arithmetic and copies ran while one was open for 0% of the time, Pallas kernels for 12%

profile of v5, /device:TPU:0, one launch (start us, length us, event | category | flops | bytes accessed | tf_op | source)
XLA Modules:
  0.0 25.9 jit_solution(16628712046078487976)
XLA Ops:
  0.6 1.7 %first_partials.1 = (bf16[6,32,128]{2,1,0:T(8,128)(2,1)S(1)}, s16[2,272,128]{2,1,0:T(8,128)(2,1)S(1)}, bf16[1,8,128,128]{3,2,1,0:T(8,128)(2,1)S(1)}, bf16[1,8,32...) custom-call(s32[6,32]{1,0:T(8,128)} %bitcast.10, bf16[32,768]{1,0:T(8,128)(2,1)} %trace_h.1, s32[4,8]{1,0:T(4,128)} %bitcast.11, ...), custom_call_target="tpu_custom_call" | custom-call | tf_op jit(solution)/shard_map/first_partials/pallas_call | solution.py:269
  2.4 0.5 %collective-permute-start.4 = (s16[2,272,128]{2,1,0:T(8,128)(2,1)S(1)}, s16[2,272,128]{2,1,0:T(8,128)(2,1)S(1)}, u32[]{:S(2)}, u32[]{:S(2)}) collective-permute-start(s16[2,272,128]{2,1,0:T(8,128)(2,1)S(1)} %get-tuple-element.14.theirs), channel_id=1, source_target_pairs={{0,8},{1,9},{2,10},{3,11},{4,12},{5,13},{6,14},{7,15},{8,0},{9,1},... | collective-permute-start | bytes 417800 | tf_op jit(solution)/shard_map/ppermute | solution.py:267
  2.9 2.6 %collective-permute-start = (bf16[6,32,128]{2,1,0:T(8,128)(2,1)S(1)}, bf16[6,32,128]{2,1,0:T(8,128)(2,1)S(1)}, u32[]{:S(2)}, u32[]{:S(2)}) collective-permute-start(bf16[6,32,128]{2,1,0:T(8,128)(2,1)S(1)} %get-tuple-element.13.drive), channel_id=1, source_target_pairs={{0,1},{1,0},{2,3},{3,2},{4,5},{5,4},{6,7},{7,6},{8,9},{9,8},{10,11... | collective-permute-start | bytes 147464 | tf_op jit(solution)/shard_map/ppermute | solution.py:267
  5.5 0.3 %second_partials.1 = (s16[1,272,128]{2,1,0:T(8,128)(2,1)S(1)}, s16[272,128]{1,0:T(8,128)(2,1)S(1)}) custom-call(bf16[1,8,32,128]{3,2,1,0:T(8,128)(2,1)S(1)} %get-tuple-element.15.chosen, s32[1,16,128]{2,1,0:T(8,128)S(1)} %get-tuple-element.16.meta, bf16[1,8,128,128]{3,2,1,0:T(8,128)(2,1)S(1)} %get-tuple-element.17.tiles, ...), custom_call_target="tpu_custom_call" | custom-call | tf_op jit(solution)/shard_map/second_partials/pallas_call | solution.py:301
  5.8 0.1 collective-permute-start.5
  5.9 0.0 collective-permute-done.4.sibling
  5.9 1.8 %collective-permute-start.6 = (s16[528,128]{1,0:T(8,128)(2,1)S(1)}, s16[528,128]{1,0:T(8,128)(2,1)S(1)}, u32[]{:S(2)}, u32[]{:S(2)}) collective-permute-start(s16[528,128]{1,0:T(8,128)(2,1)S(1)} %merge.1), channel_id=1, source_target_pairs={{0,16},{1,17},{2,18},{3,19},{4,20},{5,21},{6,22},{7,23},{8,24},{9,... | collective-permute-start | bytes 405512 | tf_op jit(solution)/shard_map/ppermute | solution.py:267
  7.7 1.4 %collective-permute-start.7 = (s16[528,128]{1,0:T(8,128)(2,1)S(1)}, s16[528,128]{1,0:T(8,128)(2,1)S(1)}, u32[]{:S(2)}, u32[]{:S(2)}) collective-permute-start(s16[528,128]{1,0:T(8,128)(2,1)S(1)} %merge.1), channel_id=1, source_target_pairs={{0,17},{1,16},{2,19},{3,18},{4,21},{5,20},{6,23},{7,22},{8,25},{9,... | collective-permute-start | bytes 405512 | tf_op jit(solution)/shard_map/ppermute | solution.py:267
  9.2 0.0 collective-permute-done.drive_x
  9.2 2.7 %collective-permute-start.1 = (bf16[2,6,32,128]{3,2,1,0:T(8,128)(2,1)S(1)}, bf16[2,6,32,128]{3,2,1,0:T(8,128)(2,1)S(1)}, u32[]{:S(2)}, u32[]{:S(2)}) collective-permute-start(bf16[2,6,32,128]{3,2,1,0:T(8,128)(2,1)S(1)} %pair.1.refs_0_), channel_id=1, source_target_pairs={{0,4},{1,5},{2,6},{3,7},{4,0},{5,1},{6,2},{7,3},{8,12},{9,13},{10,... | collective-permute-start | bytes 294920 | tf_op jit(solution)/shard_map/ppermute | solution.py:267
  11.9 1.3 %collective-permute-start.2 = (bf16[2,6,32,128]{3,2,1,0:T(8,128)(2,1)S(1)}, bf16[2,6,32,128]{3,2,1,0:T(8,128)(2,1)S(1)}, u32[]{:S(2)}, u32[]{:S(2)}) collective-permute-start(bf16[2,6,32,128]{3,2,1,0:T(8,128)(2,1)S(1)} %pair.1.refs_0_), channel_id=1, source_target_pairs={{0,6},{1,7},{2,4},{3,5},{4,2},{5,3},{6,0},{7,1},{8,14},{9,15},{10,... | collective-permute-start | bytes 294920 | tf_op jit(solution)/shard_map/ppermute | solution.py:267
  13.2 0.0 collective-permute-done.5.beside
  13.2 0.2 collective-permute-start.3
  13.4 0.0 slice-start
  13.4 0.3 %add_early.1.early = f32[25,32,128]{2,1,0:T(8,128)S(1)} custom-call(s16[2,272,128]{2,1,0:T(8,128)(2,1)S(1)} %collective-permute-done.4.sibling, s16[272,128]{1,0:T(8,128)(2,1)S(1)} %collective-permute-done.5.beside), custom_call_target="tpu_custom_call" | custom-call | tf_op jit(solution)/shard_map/add_early/pallas_call | solution.py:337
  13.7 0.0 slice-start.1
  13.7 0.0 slice-start.2
  13.7 1.0 %collective-permute-done.6.refs_0_ = s16[528,128]{1,0:T(8,128)(2,1)S(1)} collective-permute-done((s16[528,128]{1,0:T(8,128)(2,1)S(1)}, s16[528,128]{1,0:T(8,128)(2,1)S(1)}, u32[]{:S(2)}, u32[]{:S(2)}) %collective-permute-start.6) | collective-permute-done | bytes 135200 | tf_op jit(solution)/shard_map/ppermute | solution.py:267
  14.7 0.0 collective-permute-done.7.refs_1_
  14.7 0.7 %add_late.1 = (s16[208,128]{1,0:T(8,128)(2,1)S(1)}, s16[208,128]{1,0:T(8,128)(2,1)S(1)}, s16[208,128]{1,0:T(8,128)(2,1)S(1)}, f32[6,32,128]{2,1,0:T(8,128)S(1)}) custom-call(f32[25,32,128]{2,1,0:T(8,128)S(1)} %add_early.1.early, s16[528,128]{1,0:T(8,128)(2,1)S(1)} %collective-permute-done.6.refs_0_, s16[528,128]{1,0:T(8,128)(2,1)S(1)} %collective-permute-done.7.refs_1_), custom_call_target="tpu_custom_call" | custom-call | flops 68719476736 | bytes 268435456 | tf_op jit(solution)/shard_map/add_late/pallas_call | solution.py:346
  15.5 0.0 copy-start
  15.5 0.0 copy-start.1
  15.5 0.0 copy-start.2
  15.5 0.0 copy-start.3
  15.5 3.9 %collective-permute-start.10 = (s16[208,128]{1,0:T(8,128)(2,1)S(1)}, s16[208,128]{1,0:T(8,128)(2,1)S(1)}, u32[]{:S(2)}, u32[]{:S(2)}) collective-permute-start(s16[208,128]{1,0:T(8,128)(2,1)S(1)} %get-tuple-element.23), channel_id=1, source_target_pairs={{0,6},{1,7},{2,4},{3,5},{4,2},{5,3},{6,0},{7,1},{8,14},{9,15},{10,... | collective-permute-start | bytes 159752 | tf_op jit(solution)/shard_map/ppermute | solution.py:267
  19.4 0.0 collective-permute-start.8
  19.4 0.4 %collective-permute-done.1.refs_1_ = bf16[2,6,32,128]{3,2,1,0:T(8,128)(2,1)S(1)} collective-permute-done((bf16[2,6,32,128]{3,2,1,0:T(8,128)(2,1)S(1)}, bf16[2,6,32,128]{3,2,1,0:T(8,128)(2,1)S(1)}, u32[]{:S(2)}, u32[]{:S(2)}) %collective-permute-start.1) | collective-permute-done | bytes 98336 | tf_op jit(solution)/shard_map/ppermute | solution.py:267
  19.9 0.2 collective-permute-start.9
  20.1 0.0 collective-permute-done.2.refs_2_
  20.1 0.7 %collective-permute-done.3.refs_3_ = bf16[2,6,32,128]{3,2,1,0:T(8,128)(2,1)S(1)} collective-permute-done((bf16[2,6,32,128]{3,2,1,0:T(8,128)(2,1)S(1)}, bf16[2,6,32,128]{3,2,1,0:T(8,128)(2,1)S(1)}, u32[]{:S(2)}, u32[]{:S(2)}) %collective-permute-start.3) | collective-permute-done | bytes 98336 | tf_op jit(solution)/shard_map/ppermute | solution.py:267
  20.8 0.0 slice-done
  20.8 0.0 slice-done.1
  20.8 0.0 slice-done.2
  20.8 1.7 %inner.1 = f32[6,32,128]{2,1,0:T(8,128)S(1)} custom-call(bf16[2,6,32,128]{3,2,1,0:T(8,128)(2,1)S(1)} %pair.1.refs_0_, bf16[2,6,32,128]{3,2,1,0:T(8,128)(2,1)S(1)} %collective-permute-done.1.refs_1_, bf16[2,6,32,128]{3,2,1,0:T(8,128)(2,1)S(1)} %collective-permute-done.2.refs_2_, bf16[2,6,32,128]{3,2,1,0:T(8,128)(2,1)S(1)} %collective-permute-done.3.refs_3_, ...), custom_call_target="tpu_custom_call" | custom-call | flops 301989888 | bytes 9437184 | tf_op jit(solution)/shard_map/inner/pallas_call | solution.py:358
  22.5 0.0 collective-permute-done.10.refs_2_
  22.6 1.2 %collective-permute-done.8.refs_0_ = s16[208,128]{1,0:T(8,128)(2,1)S(1)} collective-permute-done((s16[208,128]{1,0:T(8,128)(2,1)S(1)}, s16[208,128]{1,0:T(8,128)(2,1)S(1)}, u32[]{:S(2)}, u32[]{:S(2)}) %collective-permute-start.8) | collective-permute-done | bytes 53280 | tf_op jit(solution)/shard_map/ppermute | solution.py:267
  23.8 1.2 %collective-permute-done.9.refs_1_ = s16[208,128]{1,0:T(8,128)(2,1)S(1)} collective-permute-done((s16[208,128]{1,0:T(8,128)(2,1)S(1)}, s16[208,128]{1,0:T(8,128)(2,1)S(1)}, u32[]{:S(2)}, u32[]{:S(2)}) %collective-permute-start.9) | collective-permute-done | bytes 53280 | tf_op jit(solution)/shard_map/ppermute | solution.py:267
  25.0 0.0 copy-done
  25.0 0.0 copy-done.1
  25.0 0.0 copy-done.2
  25.0 0.0 copy-done.3
  25.0 0.9 %advance.1 = (f32[32,768]{1,0:T(8,128)}, f32[768]{0:T(1024)}) custom-call(f32[6,32,128]{2,1,0:T(8,128)S(1)} %inner.1, f32[6,32,128]{2,1,0:T(8,128)S(1)} %get-tuple-element.20.own, s16[208,128]{1,0:T(8,128)(2,1)S(1)} %collective-permute-done.8.refs_0_, s16[208,128]{1,0:T(8,128)(2,1)S(1)} %collective-permute-done.9.refs_1_, ...), custom_call_target="tpu_custom_call" | custom-call | tf_op jit(solution)/shard_map/advance/pallas_call | solution.py:372
  (3 shorter events, 0.0 us)
Async XLA Ops:
  2.4 3.5 %collective-permute-start.4 = (s16[2,272,128]{2,1,0:T(8,128)(2,1)S(1)}, s16[2,272,128]{2,1,0:T(8,128)(2,1)S(1)}, u32[]{:S(2)}, u32[]{:S(2)}) collective-permute-start(s16[2,272,128]{2,1,0:T(8,128)(2,1)S(1)} %get-tuple-element.14.theirs), channel_id=1, source_target_pairs={{0,8},{1,9},{2,10},{3,11},{4,12},{5,13},{6,14},{7,15},{8,0},{9,1},... | collective-permute-start | bytes 417800 | tf_op jit(solution)/shard_map/ppermute | solution.py:267
  2.9 6.3 %collective-permute-start = (bf16[6,32,128]{2,1,0:T(8,128)(2,1)S(1)}, bf16[6,32,128]{2,1,0:T(8,128)(2,1)S(1)}, u32[]{:S(2)}, u32[]{:S(2)}) collective-permute-start(bf16[6,32,128]{2,1,0:T(8,128)(2,1)S(1)} %get-tuple-element.13.drive), channel_id=1, source_target_pairs={{0,1},{1,0},{2,3},{3,2},{4,5},{5,4},{6,7},{7,6},{8,9},{9,8},{10,11... | collective-permute-start | bytes 147464 | tf_op jit(solution)/shard_map/ppermute | solution.py:267
  5.8 7.4 %collective-permute-start.5 = (s16[272,128]{1,0:T(8,128)(2,1)S(1)}, s16[272,128]{1,0:T(8,128)(2,1)S(1)}, u32[]{:S(2)}, u32[]{:S(2)}) collective-permute-start(s16[272,128]{1,0:T(8,128)(2,1)S(1)} %get-tuple-element.18), channel_id=1, source_target_pairs={{0,9},{1,8},{2,11},{3,10},{4,13},{5,12},{6,15},{7,14},{8,1},{9,0},... | collective-permute-start | bytes 208904 | tf_op jit(solution)/shard_map/ppermute | solution.py:267
  5.9 8.8 %collective-permute-start.6 = (s16[528,128]{1,0:T(8,128)(2,1)S(1)}, s16[528,128]{1,0:T(8,128)(2,1)S(1)}, u32[]{:S(2)}, u32[]{:S(2)}) collective-permute-start(s16[528,128]{1,0:T(8,128)(2,1)S(1)} %merge.1), channel_id=1, source_target_pairs={{0,16},{1,17},{2,18},{3,19},{4,20},{5,21},{6,22},{7,23},{8,24},{9,... | collective-permute-start | bytes 405512 | tf_op jit(solution)/shard_map/ppermute | solution.py:267
  7.7 7.0 %collective-permute-start.7 = (s16[528,128]{1,0:T(8,128)(2,1)S(1)}, s16[528,128]{1,0:T(8,128)(2,1)S(1)}, u32[]{:S(2)}, u32[]{:S(2)}) collective-permute-start(s16[528,128]{1,0:T(8,128)(2,1)S(1)} %merge.1), channel_id=1, source_target_pairs={{0,17},{1,16},{2,19},{3,18},{4,21},{5,20},{6,23},{7,22},{8,25},{9,... | collective-permute-start | bytes 405512 | tf_op jit(solution)/shard_map/ppermute | solution.py:267
  9.2 10.7 %collective-permute-start.1 = (bf16[2,6,32,128]{3,2,1,0:T(8,128)(2,1)S(1)}, bf16[2,6,32,128]{3,2,1,0:T(8,128)(2,1)S(1)}, u32[]{:S(2)}, u32[]{:S(2)}) collective-permute-start(bf16[2,6,32,128]{3,2,1,0:T(8,128)(2,1)S(1)} %pair.1.refs_0_), channel_id=1, source_target_pairs={{0,4},{1,5},{2,6},{3,7},{4,0},{5,1},{6,2},{7,3},{8,12},{9,13},{10,... | collective-permute-start | bytes 294920 | tf_op jit(solution)/shard_map/ppermute | solution.py:267
  11.9 8.2 %collective-permute-start.2 = (bf16[2,6,32,128]{3,2,1,0:T(8,128)(2,1)S(1)}, bf16[2,6,32,128]{3,2,1,0:T(8,128)(2,1)S(1)}, u32[]{:S(2)}, u32[]{:S(2)}) collective-permute-start(bf16[2,6,32,128]{3,2,1,0:T(8,128)(2,1)S(1)} %pair.1.refs_0_), channel_id=1, source_target_pairs={{0,6},{1,7},{2,4},{3,5},{4,2},{5,3},{6,0},{7,1},{8,14},{9,15},{10,... | collective-permute-start | bytes 294920 | tf_op jit(solution)/shard_map/ppermute | solution.py:267
  13.2 7.6 %collective-permute-start.3 = (bf16[2,6,32,128]{3,2,1,0:T(8,128)(2,1)S(1)}, bf16[2,6,32,128]{3,2,1,0:T(8,128)(2,1)S(1)}, u32[]{:S(2)}, u32[]{:S(2)}) collective-permute-start(bf16[2,6,32,128]{3,2,1,0:T(8,128)(2,1)S(1)} %pair.1.refs_0_), channel_id=1, source_target_pairs={{0,2},{1,3},{2,0},{3,1},{4,6},{5,7},{6,4},{7,5},{8,10},{9,11},{10,... | collective-permute-start | bytes 294920 | tf_op jit(solution)/shard_map/ppermute | solution.py:267
  13.4 7.4 %slice-start = ((s8[9437184]{0:T(1024)(128)(4,1)}), s8[4194304]{0:T(1024)(128)(4,1)S(1)}, s32[]{:S(2)}) async-start(s8[9437184]{0:T(1024)(128)(4,1)} %bitcast.6), calls=%async_computation | async-start | bytes 8388608
  13.7 7.1 %slice-start.1 = ((s8[9437184]{0:T(1024)(128)(4,1)}), s8[4194304]{0:T(1024)(128)(4,1)S(1)}, s32[]{:S(2)}) async-start(s8[9437184]{0:T(1024)(128)(4,1)} %bitcast.6), calls=%async_computation.1 | async-start | bytes 8388608
  13.7 7.1 %slice-start.2 = ((s8[9437184]{0:T(1024)(128)(4,1)}), s8[1048576]{0:T(1024)(128)(4,1)S(1)}, s32[]{:S(2)}) async-start(s8[9437184]{0:T(1024)(128)(4,1)} %bitcast.6), calls=%async_computation.2 | async-start | bytes 2097152
  15.5 9.5 %copy-start = (f32[768]{0:T(1024)S(1)}, f32[768]{0:T(1024)}, u32[]{:S(2)}) copy-start(f32[768]{0:T(1024)} %refs_3_.1) | copy-start | bytes 9220
  15.5 9.5 %copy-start.1 = (f32[768]{0:T(1024)S(1)}, f32[768]{0:T(1024)}, u32[]{:S(2)}) copy-start(f32[768]{0:T(1024)} %refs_4_.1) | copy-start | bytes 9220
  15.5 9.5 %copy-start.2 = (f32[768]{0:T(1024)S(1)}, f32[768]{0:T(1024)}, u32[]{:S(2)}) copy-start(f32[768]{0:T(1024)} %refs_5_.1) | copy-start | bytes 9220
  15.5 9.5 %copy-start.3 = (f32[768]{0:T(1024)S(1)}, f32[768]{0:T(1024)}, u32[]{:S(2)}) copy-start(f32[768]{0:T(1024)} %refs_6_.1) | copy-start | bytes 9220
  15.5 7.0 %collective-permute-start.10 = (s16[208,128]{1,0:T(8,128)(2,1)S(1)}, s16[208,128]{1,0:T(8,128)(2,1)S(1)}, u32[]{:S(2)}, u32[]{:S(2)}) collective-permute-start(s16[208,128]{1,0:T(8,128)(2,1)S(1)} %get-tuple-element.23), channel_id=1, source_target_pairs={{0,6},{1,7},{2,4},{3,5},{4,2},{5,3},{6,0},{7,1},{8,14},{9,15},{10,... | collective-permute-start | bytes 159752 | tf_op jit(solution)/shard_map/ppermute | solution.py:267
  19.4 4.4 %collective-permute-start.8 = (s16[208,128]{1,0:T(8,128)(2,1)S(1)}, s16[208,128]{1,0:T(8,128)(2,1)S(1)}, u32[]{:S(2)}, u32[]{:S(2)}) collective-permute-start(s16[208,128]{1,0:T(8,128)(2,1)S(1)} %get-tuple-element.21), channel_id=1, source_target_pairs={{0,2},{1,3},{2,0},{3,1},{4,6},{5,7},{6,4},{7,5},{8,10},{9,11},{10,... | collective-permute-start | bytes 159752 | tf_op jit(solution)/shard_map/ppermute | solution.py:267
  19.9 5.1 %collective-permute-start.9 = (s16[208,128]{1,0:T(8,128)(2,1)S(1)}, s16[208,128]{1,0:T(8,128)(2,1)S(1)}, u32[]{:S(2)}, u32[]{:S(2)}) collective-permute-start(s16[208,128]{1,0:T(8,128)(2,1)S(1)} %get-tuple-element.22), channel_id=1, source_target_pairs={{0,4},{1,5},{2,6},{3,7},{4,0},{5,1},{6,2},{7,3},{8,12},{9,13},{10,... | collective-permute-start | bytes 159752 | tf_op jit(solution)/shard_map/ppermute | solution.py:267

commit v6 on v5

--- a/solution.py
+++ b/solution.py
@@ -7,7 +7,7 @@
 from jax.experimental.pallas import tpu as pltpu
 from jax.sharding import PartitionSpec as P
 
-TOP = 32766.0
+TOP = 32000.0
 VMEM = pl.BlockSpec(memory_space=pltpu.VMEM)
 HBM = pl.BlockSpec(memory_space=pltpu.HBM)
 in_hbm = functools.partial(pltpu.with_memory_space_constraint, memory_space=pltpu.HBM)
@@ -56,7 +56,7 @@
         chosen[j] = blocks[source[dest, j]]
         block = target[dest, j]
         owner = (block * (-(-65536 // own_blocks))) >> 16
-        place = (owner % HALVES) * per_half + (owner // HALVES) * own_blocks
+        place = (owner & (HALVES - 1)) * per_half + (owner >> 1) * own_blocks
         place = jnp.where(j < live, place + block - owner * own_blocks, -1)
         meta = jnp.where(lane == first + 2 * slots + j, place, meta)
     return meta
@@ -329,7 +329,7 @@
         for h in range(HALVES):
             arrived.append(to(merged[k - 1], CORES * k, h))
     drive_order = [2, 3, 1] if n_far == 4 else list(range(1, n_far))
-    use_order = [2, 3, 1] if n_far == 4 else list(range(1, n_far))
+    use_order = [2, 1, 3] if n_far == 4 else list(range(1, n_far))
     sum_order = [2, 3, 1] if n_far == 4 else list(range(1, n_far))
     add_order = [1, 2, 3] if n_far == 4 else list(range(1, n_far))
     pairs = {k: to(pair, 0, k * HALVES) for k in drive_order}

time: 26.1 us -> 25.9 us (level)
  waiting for transfers between devices: 4.64 us -> 3.89 us
  starting transfers between devices: 14.8 us -> 15.5 us
    ppermute x11, waiting for transfers between devices: 4.64 us -> 3.89 us  [to(): return lax.ppermute(value, ('region', 'local'), pairs)]
    ppermute x11, starting transfers between devices: 14.8 us -> 15.5 us  [to(): return lax.ppermute(value, ('region', 'local'), pairs)]
  transfers between devices with their start and end apart: 11 -> 11, of which waited for: 5 -> 3; matrix products, arithmetic and copies ran while one was open for 0% -> 0% of each run, Pallas kernels for 12% -> 12%
where the time goes in v6:
time: 25.9 us; the launch traced here: 25.8 us
  starting transfers between devices  15.5 us (60%)
  Pallas kernels  5.59 us (22%)
  waiting for transfers between devices  3.89 us (15%)
  between operations  0.77 us (3%)
    ppermute x11, starting transfers between devices, to(): return lax.ppermute(value, ('region', 'local'), pairs)  15.5 us
    ppermute x11, waiting for transfers between devices, to(): return lax.ppermute(value, ('region', 'local'), pairs)  3.89 us
    pallas_call x1, Pallas kernels, local(): pl.pallas_call(functools.partial(inner_kernel, n_far, (0, *use_order)), o...  1.73 us
    pallas_call x1, Pallas kernels, local(): pl.pallas_call(functools.partial(first_kernel, per_half), out_shape=[shap...  1.65 us
    pallas_call x1, Pallas kernels, local(): pl.pallas_call(functools.partial(advance_kernel, n_far - 1), out_shape=[s...  0.89 us
    pallas_call x1, Pallas kernels, local(): pl.pallas_call(functools.partial(late_kernel, len(arrived), n_far, slots,...  0.72 us
  transfers between devices with their start and end apart: 11, of which 3 were waited for; matrix products, arithmetic and copies ran while one was open for 0% of the time, Pallas kernels for 12%

profile of v6, /device:TPU:0, one launch (start us, length us, event | category | flops | bytes accessed | tf_op | source)
XLA Modules:
  0.0 25.8 jit_solution(16128815060095319665)
XLA Ops:
  0.6 1.7 %first_partials.1 = (bf16[6,32,128]{2,1,0:T(8,128)(2,1)S(1)}, s16[2,272,128]{2,1,0:T(8,128)(2,1)S(1)}, bf16[1,8,128,128]{3,2,1,0:T(8,128)(2,1)S(1)}, bf16[1,8,32...) custom-call(s32[6,32]{1,0:T(8,128)} %bitcast.10, bf16[32,768]{1,0:T(8,128)(2,1)} %trace_h.1, s32[4,8]{1,0:T(4,128)} %bitcast.11, ...), custom_call_target="tpu_custom_call" | custom-call | tf_op jit(solution)/shard_map/first_partials/pallas_call | solution.py:269
  2.3 0.5 %collective-permute-start.4 = (s16[2,272,128]{2,1,0:T(8,128)(2,1)S(1)}, s16[2,272,128]{2,1,0:T(8,128)(2,1)S(1)}, u32[]{:S(2)}, u32[]{:S(2)}) collective-permute-start(s16[2,272,128]{2,1,0:T(8,128)(2,1)S(1)} %get-tuple-element.14.theirs), channel_id=1, source_target_pairs={{0,8},{1,9},{2,10},{3,11},{4,12},{5,13},{6,14},{7,15},{8,0},{9,1},... | collective-permute-start | bytes 417800 | tf_op jit(solution)/shard_map/ppermute | solution.py:267
  2.8 2.6 %collective-permute-start = (bf16[6,32,128]{2,1,0:T(8,128)(2,1)S(1)}, bf16[6,32,128]{2,1,0:T(8,128)(2,1)S(1)}, u32[]{:S(2)}, u32[]{:S(2)}) collective-permute-start(bf16[6,32,128]{2,1,0:T(8,128)(2,1)S(1)} %get-tuple-element.13.drive), channel_id=1, source_target_pairs={{0,1},{1,0},{2,3},{3,2},{4,5},{5,4},{6,7},{7,6},{8,9},{9,8},{10,11... | collective-permute-start | bytes 147464 | tf_op jit(solution)/shard_map/ppermute | solution.py:267
  5.4 0.3 %second_partials.1 = (s16[1,272,128]{2,1,0:T(8,128)(2,1)S(1)}, s16[272,128]{1,0:T(8,128)(2,1)S(1)}) custom-call(bf16[1,8,32,128]{3,2,1,0:T(8,128)(2,1)S(1)} %get-tuple-element.15.chosen, s32[1,16,128]{2,1,0:T(8,128)S(1)} %get-tuple-element.16.meta, bf16[1,8,128,128]{3,2,1,0:T(8,128)(2,1)S(1)} %get-tuple-element.17.tiles, ...), custom_call_target="tpu_custom_call" | custom-call | tf_op jit(solution)/shard_map/second_partials/pallas_call | solution.py:301
  5.7 0.1 collective-permute-start.5
  5.8 0.0 collective-permute-done.4.sibling
  5.8 1.8 %collective-permute-start.6 = (s16[528,128]{1,0:T(8,128)(2,1)S(1)}, s16[528,128]{1,0:T(8,128)(2,1)S(1)}, u32[]{:S(2)}, u32[]{:S(2)}) collective-permute-start(s16[528,128]{1,0:T(8,128)(2,1)S(1)} %merge.1), channel_id=1, source_target_pairs={{0,16},{1,17},{2,18},{3,19},{4,20},{5,21},{6,22},{7,23},{8,24},{9,... | collective-permute-start | bytes 405512 | tf_op jit(solution)/shard_map/ppermute | solution.py:267
  7.6 1.4 %collective-permute-start.7 = (s16[528,128]{1,0:T(8,128)(2,1)S(1)}, s16[528,128]{1,0:T(8,128)(2,1)S(1)}, u32[]{:S(2)}, u32[]{:S(2)}) collective-permute-start(s16[528,128]{1,0:T(8,128)(2,1)S(1)} %merge.1), channel_id=1, source_target_pairs={{0,17},{1,16},{2,19},{3,18},{4,21},{5,20},{6,23},{7,22},{8,25},{9,... | collective-permute-start | bytes 405512 | tf_op jit(solution)/shard_map/ppermute | solution.py:267
  9.1 0.0 collective-permute-done.drive_x
  9.1 2.7 %collective-permute-start.1 = (bf16[2,6,32,128]{3,2,1,0:T(8,128)(2,1)S(1)}, bf16[2,6,32,128]{3,2,1,0:T(8,128)(2,1)S(1)}, u32[]{:S(2)}, u32[]{:S(2)}) collective-permute-start(bf16[2,6,32,128]{3,2,1,0:T(8,128)(2,1)S(1)} %pair.1.refs_0_), channel_id=1, source_target_pairs={{0,4},{1,5},{2,6},{3,7},{4,0},{5,1},{6,2},{7,3},{8,12},{9,13},{10,... | collective-permute-start | bytes 294920 | tf_op jit(solution)/shard_map/ppermute | solution.py:267
  11.8 1.6 %collective-permute-start.2 = (bf16[2,6,32,128]{3,2,1,0:T(8,128)(2,1)S(1)}, bf16[2,6,32,128]{3,2,1,0:T(8,128)(2,1)S(1)}, u32[]{:S(2)}, u32[]{:S(2)}) collective-permute-start(bf16[2,6,32,128]{3,2,1,0:T(8,128)(2,1)S(1)} %pair.1.refs_0_), channel_id=1, source_target_pairs={{0,2},{1,3},{2,0},{3,1},{4,6},{5,7},{6,4},{7,5},{8,10},{9,11},{10,... | collective-permute-start | bytes 294920 | tf_op jit(solution)/shard_map/ppermute | solution.py:267
  13.3 0.0 collective-permute-done.5.beside
  13.3 0.2 collective-permute-start.3
  13.6 0.0 slice-start
  13.6 0.3 %add_early.1.early = f32[25,32,128]{2,1,0:T(8,128)S(1)} custom-call(s16[2,272,128]{2,1,0:T(8,128)(2,1)S(1)} %collective-permute-done.4.sibling, s16[272,128]{1,0:T(8,128)(2,1)S(1)} %collective-permute-done.5.beside), custom_call_target="tpu_custom_call" | custom-call | tf_op jit(solution)/shard_map/add_early/pallas_call | solution.py:337
  13.9 0.0 slice-start.1
  13.9 0.0 slice-start.2
  13.9 0.8 %collective-permute-done.6.refs_0_ = s16[528,128]{1,0:T(8,128)(2,1)S(1)} collective-permute-done((s16[528,128]{1,0:T(8,128)(2,1)S(1)}, s16[528,128]{1,0:T(8,128)(2,1)S(1)}, u32[]{:S(2)}, u32[]{:S(2)}) %collective-permute-start.6) | collective-permute-done | bytes 135200 | tf_op jit(solution)/shard_map/ppermute | solution.py:267
  14.6 0.0 collective-permute-done.7.refs_1_
  14.6 0.7 %add_late.1 = (s16[208,128]{1,0:T(8,128)(2,1)S(1)}, s16[208,128]{1,0:T(8,128)(2,1)S(1)}, s16[208,128]{1,0:T(8,128)(2,1)S(1)}, f32[6,32,128]{2,1,0:T(8,128)S(1)}) custom-call(f32[25,32,128]{2,1,0:T(8,128)S(1)} %add_early.1.early, s16[528,128]{1,0:T(8,128)(2,1)S(1)} %collective-permute-done.6.refs_0_, s16[528,128]{1,0:T(8,128)(2,1)S(1)} %collective-permute-done.7.refs_1_), custom_call_target="tpu_custom_call" | custom-call | flops 68719476736 | bytes 268435456 | tf_op jit(solution)/shard_map/add_late/pallas_call | solution.py:346
  15.4 0.0 copy-start
  15.4 0.0 copy-start.1
  15.4 0.0 copy-start.2
  15.4 0.0 copy-start.3
  15.4 3.9 %collective-permute-start.10 = (s16[208,128]{1,0:T(8,128)(2,1)S(1)}, s16[208,128]{1,0:T(8,128)(2,1)S(1)}, u32[]{:S(2)}, u32[]{:S(2)}) collective-permute-start(s16[208,128]{1,0:T(8,128)(2,1)S(1)} %get-tuple-element.23), channel_id=1, source_target_pairs={{0,6},{1,7},{2,4},{3,5},{4,2},{5,3},{6,0},{7,1},{8,14},{9,15},{10,... | collective-permute-start | bytes 159752 | tf_op jit(solution)/shard_map/ppermute | solution.py:267
  19.3 0.0 collective-permute-start.8
  19.3 0.0 collective-permute-done.1.refs_1_
  19.3 0.6 %collective-permute-start.9 = (s16[208,128]{1,0:T(8,128)(2,1)S(1)}, s16[208,128]{1,0:T(8,128)(2,1)S(1)}, u32[]{:S(2)}, u32[]{:S(2)}) collective-permute-start(s16[208,128]{1,0:T(8,128)(2,1)S(1)} %get-tuple-element.22), channel_id=1, source_target_pairs={{0,4},{1,5},{2,6},{3,7},{4,0},{5,1},{6,2},{7,3},{8,12},{9,13},{10,... | collective-permute-start | bytes 159752 | tf_op jit(solution)/shard_map/ppermute | solution.py:267
  20.0 0.0 collective-permute-done.2.refs_2_
  20.0 0.0 collective-permute-done.3.refs_3_
  20.0 0.0 slice-done
  20.0 0.0 slice-done.1
  20.0 0.0 slice-done.2
  20.0 1.7 %inner.1 = f32[6,32,128]{2,1,0:T(8,128)S(1)} custom-call(bf16[2,6,32,128]{3,2,1,0:T(8,128)(2,1)S(1)} %pair.1.refs_0_, bf16[2,6,32,128]{3,2,1,0:T(8,128)(2,1)S(1)} %collective-permute-done.1.refs_1_, bf16[2,6,32,128]{3,2,1,0:T(8,128)(2,1)S(1)} %collective-permute-done.2.refs_2_, bf16[2,6,32,128]{3,2,1,0:T(8,128)(2,1)S(1)} %collective-permute-done.3.refs_3_, ...), custom_call_target="tpu_custom_call" | custom-call | flops 301989888 | bytes 9437184 | tf_op jit(solution)/shard_map/inner/pallas_call | solution.py:358
  21.7 0.0 collective-permute-done.10.refs_2_
  21.7 1.9 %collective-permute-done.8.refs_0_ = s16[208,128]{1,0:T(8,128)(2,1)S(1)} collective-permute-done((s16[208,128]{1,0:T(8,128)(2,1)S(1)}, s16[208,128]{1,0:T(8,128)(2,1)S(1)}, u32[]{:S(2)}, u32[]{:S(2)}) %collective-permute-start.8) | collective-permute-done | bytes 53280 | tf_op jit(solution)/shard_map/ppermute | solution.py:267
  23.7 1.2 %collective-permute-done.9.refs_1_ = s16[208,128]{1,0:T(8,128)(2,1)S(1)} collective-permute-done((s16[208,128]{1,0:T(8,128)(2,1)S(1)}, s16[208,128]{1,0:T(8,128)(2,1)S(1)}, u32[]{:S(2)}, u32[]{:S(2)}) %collective-permute-start.9) | collective-permute-done | bytes 53280 | tf_op jit(solution)/shard_map/ppermute | solution.py:267
  24.9 0.0 copy-done
  24.9 0.0 copy-done.1
  24.9 0.0 copy-done.2
  24.9 0.0 copy-done.3
  24.9 0.9 %advance.1 = (f32[32,768]{1,0:T(8,128)}, f32[768]{0:T(1024)}) custom-call(f32[6,32,128]{2,1,0:T(8,128)S(1)} %inner.1, f32[6,32,128]{2,1,0:T(8,128)S(1)} %get-tuple-element.20.own, s16[208,128]{1,0:T(8,128)(2,1)S(1)} %collective-permute-done.8.refs_0_, s16[208,128]{1,0:T(8,128)(2,1)S(1)} %collective-permute-done.9.refs_1_, ...), custom_call_target="tpu_custom_call" | custom-call | tf_op jit(solution)/shard_map/advance/pallas_call | solution.py:372
  (3 shorter events, 0.0 us)
Async XLA Ops:
  2.3 3.5 %collective-permute-start.4 = (s16[2,272,128]{2,1,0:T(8,128)(2,1)S(1)}, s16[2,272,128]{2,1,0:T(8,128)(2,1)S(1)}, u32[]{:S(2)}, u32[]{:S(2)}) collective-permute-start(s16[2,272,128]{2,1,0:T(8,128)(2,1)S(1)} %get-tuple-element.14.theirs), channel_id=1, source_target_pairs={{0,8},{1,9},{2,10},{3,11},{4,12},{5,13},{6,14},{7,15},{8,0},{9,1},... | collective-permute-start | bytes 417800 | tf_op jit(solution)/shard_map/ppermute | solution.py:267
  2.8 6.3 %collective-permute-start = (bf16[6,32,128]{2,1,0:T(8,128)(2,1)S(1)}, bf16[6,32,128]{2,1,0:T(8,128)(2,1)S(1)}, u32[]{:S(2)}, u32[]{:S(2)}) collective-permute-start(bf16[6,32,128]{2,1,0:T(8,128)(2,1)S(1)} %get-tuple-element.13.drive), channel_id=1, source_target_pairs={{0,1},{1,0},{2,3},{3,2},{4,5},{5,4},{6,7},{7,6},{8,9},{9,8},{10,11... | collective-permute-start | bytes 147464 | tf_op jit(solution)/shard_map/ppermute | solution.py:267
  5.7 7.7 %collective-permute-start.5 = (s16[272,128]{1,0:T(8,128)(2,1)S(1)}, s16[272,128]{1,0:T(8,128)(2,1)S(1)}, u32[]{:S(2)}, u32[]{:S(2)}) collective-permute-start(s16[272,128]{1,0:T(8,128)(2,1)S(1)} %get-tuple-element.18), channel_id=1, source_target_pairs={{0,9},{1,8},{2,11},{3,10},{4,13},{5,12},{6,15},{7,14},{8,1},{9,0},... | collective-permute-start | bytes 208904 | tf_op jit(solution)/shard_map/ppermute | solution.py:267
  5.8 8.8 %collective-permute-start.6 = (s16[528,128]{1,0:T(8,128)(2,1)S(1)}, s16[528,128]{1,0:T(8,128)(2,1)S(1)}, u32[]{:S(2)}, u32[]{:S(2)}) collective-permute-start(s16[528,128]{1,0:T(8,128)(2,1)S(1)} %merge.1), channel_id=1, source_target_pairs={{0,16},{1,17},{2,18},{3,19},{4,20},{5,21},{6,22},{7,23},{8,24},{9,... | collective-permute-start | bytes 405512 | tf_op jit(solution)/shard_map/ppermute | solution.py:267
  7.6 7.0 %collective-permute-start.7 = (s16[528,128]{1,0:T(8,128)(2,1)S(1)}, s16[528,128]{1,0:T(8,128)(2,1)S(1)}, u32[]{:S(2)}, u32[]{:S(2)}) collective-permute-start(s16[528,128]{1,0:T(8,128)(2,1)S(1)} %merge.1), channel_id=1, source_target_pairs={{0,17},{1,16},{2,19},{3,18},{4,21},{5,20},{6,23},{7,22},{8,25},{9,... | collective-permute-start | bytes 405512 | tf_op jit(solution)/shard_map/ppermute | solution.py:267
  9.1 10.2 %collective-permute-start.1 = (bf16[2,6,32,128]{3,2,1,0:T(8,128)(2,1)S(1)}, bf16[2,6,32,128]{3,2,1,0:T(8,128)(2,1)S(1)}, u32[]{:S(2)}, u32[]{:S(2)}) collective-permute-start(bf16[2,6,32,128]{3,2,1,0:T(8,128)(2,1)S(1)} %pair.1.refs_0_), channel_id=1, source_target_pairs={{0,4},{1,5},{2,6},{3,7},{4,0},{5,1},{6,2},{7,3},{8,12},{9,13},{10,... | collective-permute-start | bytes 294920 | tf_op jit(solution)/shard_map/ppermute | solution.py:267
  11.8 8.2 %collective-permute-start.2 = (bf16[2,6,32,128]{3,2,1,0:T(8,128)(2,1)S(1)}, bf16[2,6,32,128]{3,2,1,0:T(8,128)(2,1)S(1)}, u32[]{:S(2)}, u32[]{:S(2)}) collective-permute-start(bf16[2,6,32,128]{3,2,1,0:T(8,128)(2,1)S(1)} %pair.1.refs_0_), channel_id=1, source_target_pairs={{0,2},{1,3},{2,0},{3,1},{4,6},{5,7},{6,4},{7,5},{8,10},{9,11},{10,... | collective-permute-start | bytes 294920 | tf_op jit(solution)/shard_map/ppermute | solution.py:267
  13.3 6.6 %collective-permute-start.3 = (bf16[2,6,32,128]{3,2,1,0:T(8,128)(2,1)S(1)}, bf16[2,6,32,128]{3,2,1,0:T(8,128)(2,1)S(1)}, u32[]{:S(2)}, u32[]{:S(2)}) collective-permute-start(bf16[2,6,32,128]{3,2,1,0:T(8,128)(2,1)S(1)} %pair.1.refs_0_), channel_id=1, source_target_pairs={{0,6},{1,7},{2,4},{3,5},{4,2},{5,3},{6,0},{7,1},{8,14},{9,15},{10,... | collective-permute-start | bytes 294920 | tf_op jit(solution)/shard_map/ppermute | solution.py:267
  13.6 6.4 %slice-start = ((s8[9437184]{0:T(1024)(128)(4,1)}), s8[4194304]{0:T(1024)(128)(4,1)S(1)}, s32[]{:S(2)}) async-start(s8[9437184]{0:T(1024)(128)(4,1)} %bitcast.6), calls=%async_computation | async-start | bytes 8388608
  13.9 6.1 %slice-start.1 = ((s8[9437184]{0:T(1024)(128)(4,1)}), s8[4194304]{0:T(1024)(128)(4,1)S(1)}, s32[]{:S(2)}) async-start(s8[9437184]{0:T(1024)(128)(4,1)} %bitcast.6), calls=%async_computation.1 | async-start | bytes 8388608
  13.9 6.1 %slice-start.2 = ((s8[9437184]{0:T(1024)(128)(4,1)}), s8[1048576]{0:T(1024)(128)(4,1)S(1)}, s32[]{:S(2)}) async-start(s8[9437184]{0:T(1024)(128)(4,1)} %bitcast.6), calls=%async_computation.2 | async-start | bytes 2097152
  15.4 9.5 %copy-start = (f32[768]{0:T(1024)S(1)}, f32[768]{0:T(1024)}, u32[]{:S(2)}) copy-start(f32[768]{0:T(1024)} %refs_3_.1) | copy-start | bytes 9220
  15.4 9.5 %copy-start.1 = (f32[768]{0:T(1024)S(1)}, f32[768]{0:T(1024)}, u32[]{:S(2)}) copy-start(f32[768]{0:T(1024)} %refs_4_.1) | copy-start | bytes 9220
  15.4 9.5 %copy-start.2 = (f32[768]{0:T(1024)S(1)}, f32[768]{0:T(1024)}, u32[]{:S(2)}) copy-start(f32[768]{0:T(1024)} %refs_5_.1) | copy-start | bytes 9220
  15.4 9.5 %copy-start.3 = (f32[768]{0:T(1024)S(1)}, f32[768]{0:T(1024)}, u32[]{:S(2)}) copy-start(f32[768]{0:T(1024)} %refs_6_.1) | copy-start | bytes 9220
  15.4 6.3 %collective-permute-start.10 = (s16[208,128]{1,0:T(8,128)(2,1)S(1)}, s16[208,128]{1,0:T(8,128)(2,1)S(1)}, u32[]{:S(2)}, u32[]{:S(2)}) collective-permute-start(s16[208,128]{1,0:T(8,128)(2,1)S(1)} %get-tuple-element.23), channel_id=1, source_target_pairs={{0,6},{1,7},{2,4},{3,5},{4,2},{5,3},{6,0},{7,1},{8,14},{9,15},{10,... | collective-permute-start | bytes 159752 | tf_op jit(solution)/shard_map/ppermute | solution.py:267
  19.3 4.4 %collective-permute-start.8 = (s16[208,128]{1,0:T(8,128)(2,1)S(1)}, s16[208,128]{1,0:T(8,128)(2,1)S(1)}, u32[]{:S(2)}, u32[]{:S(2)}) collective-permute-start(s16[208,128]{1,0:T(8,128)(2,1)S(1)} %get-tuple-element.21), channel_id=1, source_target_pairs={{0,2},{1,3},{2,0},{3,1},{4,6},{5,7},{6,4},{7,5},{8,10},{9,11},{10,... | collective-permute-start | bytes 159752 | tf_op jit(solution)/shard_map/ppermute | solution.py:267
  19.3 5.5 %collective-permute-start.9 = (s16[208,128]{1,0:T(8,128)(2,1)S(1)}, s16[208,128]{1,0:T(8,128)(2,1)S(1)}, u32[]{:S(2)}, u32[]{:S(2)}) collective-permute-start(s16[208,128]{1,0:T(8,128)(2,1)S(1)} %get-tuple-element.22), channel_id=1, source_target_pairs={{0,4},{1,5},{2,6},{3,7},{4,0},{5,1},{6,2},{7,3},{8,12},{9,13},{10,... | collective-permute-start | bytes 159752 | tf_op jit(solution)/shard_map/ppermute | solution.py:267

commit v7 on v6

--- a/solution.py
+++ b/solution.py
@@ -121,11 +121,10 @@
         choose(region ^ 1 ^ (CORES * k), drive, source, target, count, per_half, 0, chosen.at[k])
         for k in range(n)
     ]
+    for copy in copies[5:]:
+        copy.wait()
     for k in range(n):
-        copies[5 + k].wait()
         send_slots(chosen.at[k], tiles.at[k], metas[k], 0, out.at[k])
-    for copy in copies[5 + n :]:
-        copy.wait()
 
 
 def second_kernel(chosen, meta, tiles, theirs, out, across):

time: 25.9 us -> 25.9 us (level)
  no operation moved by 1% of the time
where the time goes in v7:
time: 25.9 us; the launch traced here: 25.7 us
  starting transfers between devices  15.5 us (60%)
  Pallas kernels  5.51 us (21%)
  waiting for transfers between devices  3.9 us (15%)
  between operations  0.77 us (3%)
    ppermute x11, starting transfers between devices, to(): return lax.ppermute(value, ('region', 'local'), pairs)  15.5 us
    ppermute x11, waiting for transfers between devices, to(): return lax.ppermute(value, ('region', 'local'), pairs)  3.9 us
    pallas_call x1, Pallas kernels, local(): pl.pallas_call(functools.partial(inner_kernel, n_far, (0, *use_order)), o...  1.73 us
    pallas_call x1, Pallas kernels, local(): pl.pallas_call(functools.partial(first_kernel, per_half), out_shape=[shap...  1.58 us
    pallas_call x1, Pallas kernels, local(): pl.pallas_call(functools.partial(advance_kernel, n_far - 1), out_shape=[s...  0.89 us
    pallas_call x1, Pallas kernels, local(): pl.pallas_call(functools.partial(late_kernel, len(arrived), n_far, slots,...  0.72 us
  transfers between devices with their start and end apart: 11, of which 3 were waited for; matrix products, arithmetic and copies ran while one was open for 0% of the time, Pallas kernels for 12%

profile of v7, /device:TPU:0, one launch (start us, length us, event | category | flops | bytes accessed | tf_op | source)
XLA Modules:
  0.0 25.7 jit_solution(17872947187594659515)
XLA Ops:
  0.6 1.6 %first_partials.1 = (bf16[6,32,128]{2,1,0:T(8,128)(2,1)S(1)}, s16[2,272,128]{2,1,0:T(8,128)(2,1)S(1)}, bf16[1,8,128,128]{3,2,1,0:T(8,128)(2,1)S(1)}, bf16[1,8,32...) custom-call(s32[6,32]{1,0:T(8,128)} %bitcast.10, bf16[32,768]{1,0:T(8,128)(2,1)} %trace_h.1, s32[4,8]{1,0:T(4,128)} %bitcast.11, ...), custom_call_target="tpu_custom_call" | custom-call | tf_op jit(solution)/shard_map/first_partials/pallas_call | solution.py:268
  2.2 0.5 %collective-permute-start.4 = (s16[2,272,128]{2,1,0:T(8,128)(2,1)S(1)}, s16[2,272,128]{2,1,0:T(8,128)(2,1)S(1)}, u32[]{:S(2)}, u32[]{:S(2)}) collective-permute-start(s16[2,272,128]{2,1,0:T(8,128)(2,1)S(1)} %get-tuple-element.14.theirs), channel_id=1, source_target_pairs={{0,8},{1,9},{2,10},{3,11},{4,12},{5,13},{6,14},{7,15},{8,0},{9,1},... | collective-permute-start | bytes 417800 | tf_op jit(solution)/shard_map/ppermute | solution.py:266
  2.7 2.6 %collective-permute-start = (bf16[6,32,128]{2,1,0:T(8,128)(2,1)S(1)}, bf16[6,32,128]{2,1,0:T(8,128)(2,1)S(1)}, u32[]{:S(2)}, u32[]{:S(2)}) collective-permute-start(bf16[6,32,128]{2,1,0:T(8,128)(2,1)S(1)} %get-tuple-element.13.drive), channel_id=1, source_target_pairs={{0,1},{1,0},{2,3},{3,2},{4,5},{5,4},{6,7},{7,6},{8,9},{9,8},{10,11... | collective-permute-start | bytes 147464 | tf_op jit(solution)/shard_map/ppermute | solution.py:266
  5.3 0.3 %second_partials.1 = (s16[1,272,128]{2,1,0:T(8,128)(2,1)S(1)}, s16[272,128]{1,0:T(8,128)(2,1)S(1)}) custom-call(bf16[1,8,32,128]{3,2,1,0:T(8,128)(2,1)S(1)} %get-tuple-element.15.chosen, s32[1,16,128]{2,1,0:T(8,128)S(1)} %get-tuple-element.16.meta, bf16[1,8,128,128]{3,2,1,0:T(8,128)(2,1)S(1)} %get-tuple-element.17.tiles, ...), custom_call_target="tpu_custom_call" | custom-call | tf_op jit(solution)/shard_map/second_partials/pallas_call | solution.py:300
  5.6 0.1 collective-permute-start.5
  5.7 0.0 collective-permute-done.4.sibling
  5.7 1.8 %collective-permute-start.6 = (s16[528,128]{1,0:T(8,128)(2,1)S(1)}, s16[528,128]{1,0:T(8,128)(2,1)S(1)}, u32[]{:S(2)}, u32[]{:S(2)}) collective-permute-start(s16[528,128]{1,0:T(8,128)(2,1)S(1)} %merge.1), channel_id=1, source_target_pairs={{0,16},{1,17},{2,18},{3,19},{4,20},{5,21},{6,22},{7,23},{8,24},{9,... | collective-permute-start | bytes 405512 | tf_op jit(solution)/shard_map/ppermute | solution.py:266
  7.6 1.4 %collective-permute-start.7 = (s16[528,128]{1,0:T(8,128)(2,1)S(1)}, s16[528,128]{1,0:T(8,128)(2,1)S(1)}, u32[]{:S(2)}, u32[]{:S(2)}) collective-permute-start(s16[528,128]{1,0:T(8,128)(2,1)S(1)} %merge.1), channel_id=1, source_target_pairs={{0,17},{1,16},{2,19},{3,18},{4,21},{5,20},{6,23},{7,22},{8,25},{9,... | collective-permute-start | bytes 405512 | tf_op jit(solution)/shard_map/ppermute | solution.py:266
  9.0 0.0 collective-permute-done.drive_x
  9.0 2.7 %collective-permute-start.1 = (bf16[2,6,32,128]{3,2,1,0:T(8,128)(2,1)S(1)}, bf16[2,6,32,128]{3,2,1,0:T(8,128)(2,1)S(1)}, u32[]{:S(2)}, u32[]{:S(2)}) collective-permute-start(bf16[2,6,32,128]{3,2,1,0:T(8,128)(2,1)S(1)} %pair.1.refs_0_), channel_id=1, source_target_pairs={{0,4},{1,5},{2,6},{3,7},{4,0},{5,1},{6,2},{7,3},{8,12},{9,13},{10,... | collective-permute-start | bytes 294920 | tf_op jit(solution)/shard_map/ppermute | solution.py:266
  11.7 1.6 %collective-permute-start.2 = (bf16[2,6,32,128]{3,2,1,0:T(8,128)(2,1)S(1)}, bf16[2,6,32,128]{3,2,1,0:T(8,128)(2,1)S(1)}, u32[]{:S(2)}, u32[]{:S(2)}) collective-permute-start(bf16[2,6,32,128]{3,2,1,0:T(8,128)(2,1)S(1)} %pair.1.refs_0_), channel_id=1, source_target_pairs={{0,2},{1,3},{2,0},{3,1},{4,6},{5,7},{6,4},{7,5},{8,10},{9,11},{10,... | collective-permute-start | bytes 294920 | tf_op jit(solution)/shard_map/ppermute | solution.py:266
  13.3 0.0 collective-permute-done.5.beside
  13.3 0.2 collective-permute-start.3
  13.5 0.0 slice-start
  13.5 0.3 %add_early.1.early = f32[25,32,128]{2,1,0:T(8,128)S(1)} custom-call(s16[2,272,128]{2,1,0:T(8,128)(2,1)S(1)} %collective-permute-done.4.sibling, s16[272,128]{1,0:T(8,128)(2,1)S(1)} %collective-permute-done.5.beside), custom_call_target="tpu_custom_call" | custom-call | tf_op jit(solution)/shard_map/add_early/pallas_call | solution.py:336
  13.8 0.0 slice-start.1
  13.8 0.0 slice-start.2
  13.8 0.8 %collective-permute-done.6.refs_0_ = s16[528,128]{1,0:T(8,128)(2,1)S(1)} collective-permute-done((s16[528,128]{1,0:T(8,128)(2,1)S(1)}, s16[528,128]{1,0:T(8,128)(2,1)S(1)}, u32[]{:S(2)}, u32[]{:S(2)}) %collective-permute-start.6) | collective-permute-done | bytes 135200 | tf_op jit(solution)/shard_map/ppermute | solution.py:266
  14.6 0.0 collective-permute-done.7.refs_1_
  14.6 0.7 %add_late.1 = (s16[208,128]{1,0:T(8,128)(2,1)S(1)}, s16[208,128]{1,0:T(8,128)(2,1)S(1)}, s16[208,128]{1,0:T(8,128)(2,1)S(1)}, f32[6,32,128]{2,1,0:T(8,128)S(1)}) custom-call(f32[25,32,128]{2,1,0:T(8,128)S(1)} %add_early.1.early, s16[528,128]{1,0:T(8,128)(2,1)S(1)} %collective-permute-done.6.refs_0_, s16[528,128]{1,0:T(8,128)(2,1)S(1)} %collective-permute-done.7.refs_1_), custom_call_target="tpu_custom_call" | custom-call | flops 68719476736 | bytes 268435456 | tf_op jit(solution)/shard_map/add_late/pallas_call | solution.py:345
  15.3 0.0 copy-start
  15.3 0.0 copy-start.1
  15.3 0.0 copy-start.2
  15.3 0.0 copy-start.3
  15.3 3.9 %collective-permute-start.10 = (s16[208,128]{1,0:T(8,128)(2,1)S(1)}, s16[208,128]{1,0:T(8,128)(2,1)S(1)}, u32[]{:S(2)}, u32[]{:S(2)}) collective-permute-start(s16[208,128]{1,0:T(8,128)(2,1)S(1)} %get-tuple-element.23), channel_id=1, source_target_pairs={{0,6},{1,7},{2,4},{3,5},{4,2},{5,3},{6,0},{7,1},{8,14},{9,15},{10,... | collective-permute-start | bytes 159752 | tf_op jit(solution)/shard_map/ppermute | solution.py:266
  19.2 0.0 collective-permute-start.8
  19.2 0.0 collective-permute-done.1.refs_1_
  19.2 0.6 %collective-permute-start.9 = (s16[208,128]{1,0:T(8,128)(2,1)S(1)}, s16[208,128]{1,0:T(8,128)(2,1)S(1)}, u32[]{:S(2)}, u32[]{:S(2)}) collective-permute-start(s16[208,128]{1,0:T(8,128)(2,1)S(1)} %get-tuple-element.22), channel_id=1, source_target_pairs={{0,4},{1,5},{2,6},{3,7},{4,0},{5,1},{6,2},{7,3},{8,12},{9,13},{10,... | collective-permute-start | bytes 159752 | tf_op jit(solution)/shard_map/ppermute | solution.py:266
  19.9 0.0 collective-permute-done.2.refs_2_
  19.9 0.0 collective-permute-done.3.refs_3_
  19.9 0.0 slice-done
  19.9 0.0 slice-done.1
  19.9 0.0 slice-done.2
  19.9 1.7 %inner.1 = f32[6,32,128]{2,1,0:T(8,128)S(1)} custom-call(bf16[2,6,32,128]{3,2,1,0:T(8,128)(2,1)S(1)} %pair.1.refs_0_, bf16[2,6,32,128]{3,2,1,0:T(8,128)(2,1)S(1)} %collective-permute-done.1.refs_1_, bf16[2,6,32,128]{3,2,1,0:T(8,128)(2,1)S(1)} %collective-permute-done.2.refs_2_, bf16[2,6,32,128]{3,2,1,0:T(8,128)(2,1)S(1)} %collective-permute-done.3.refs_3_, ...), custom_call_target="tpu_custom_call" | custom-call | flops 301989888 | bytes 9437184 | tf_op jit(solution)/shard_map/inner/pallas_call | solution.py:357
  21.7 0.0 collective-permute-done.10.refs_2_
  21.7 2.0 %collective-permute-done.8.refs_0_ = s16[208,128]{1,0:T(8,128)(2,1)S(1)} collective-permute-done((s16[208,128]{1,0:T(8,128)(2,1)S(1)}, s16[208,128]{1,0:T(8,128)(2,1)S(1)}, u32[]{:S(2)}, u32[]{:S(2)}) %collective-permute-start.8) | collective-permute-done | bytes 53280 | tf_op jit(solution)/shard_map/ppermute | solution.py:266
  23.6 1.2 %collective-permute-done.9.refs_1_ = s16[208,128]{1,0:T(8,128)(2,1)S(1)} collective-permute-done((s16[208,128]{1,0:T(8,128)(2,1)S(1)}, s16[208,128]{1,0:T(8,128)(2,1)S(1)}, u32[]{:S(2)}, u32[]{:S(2)}) %collective-permute-start.9) | collective-permute-done | bytes 53280 | tf_op jit(solution)/shard_map/ppermute | solution.py:266
  24.8 0.0 copy-done
  24.8 0.0 copy-done.1
  24.8 0.0 copy-done.2
  24.8 0.0 copy-done.3
  24.8 0.9 %advance.1 = (f32[32,768]{1,0:T(8,128)}, f32[768]{0:T(1024)}) custom-call(f32[6,32,128]{2,1,0:T(8,128)S(1)} %inner.1, f32[6,32,128]{2,1,0:T(8,128)S(1)} %get-tuple-element.20.own, s16[208,128]{1,0:T(8,128)(2,1)S(1)} %collective-permute-done.8.refs_0_, s16[208,128]{1,0:T(8,128)(2,1)S(1)} %collective-permute-done.9.refs_1_, ...), custom_call_target="tpu_custom_call" | custom-call | tf_op jit(solution)/shard_map/advance/pallas_call | solution.py:371
  (3 shorter events, 0.0 us)
Async XLA Ops:
  2.2 3.5 %collective-permute-start.4 = (s16[2,272,128]{2,1,0:T(8,128)(2,1)S(1)}, s16[2,272,128]{2,1,0:T(8,128)(2,1)S(1)}, u32[]{:S(2)}, u32[]{:S(2)}) collective-permute-start(s16[2,272,128]{2,1,0:T(8,128)(2,1)S(1)} %get-tuple-element.14.theirs), channel_id=1, source_target_pairs={{0,8},{1,9},{2,10},{3,11},{4,12},{5,13},{6,14},{7,15},{8,0},{9,1},... | collective-permute-start | bytes 417800 | tf_op jit(solution)/shard_map/ppermute | solution.py:266
  2.7 6.3 %collective-permute-start = (bf16[6,32,128]{2,1,0:T(8,128)(2,1)S(1)}, bf16[6,32,128]{2,1,0:T(8,128)(2,1)S(1)}, u32[]{:S(2)}, u32[]{:S(2)}) collective-permute-start(bf16[6,32,128]{2,1,0:T(8,128)(2,1)S(1)} %get-tuple-element.13.drive), channel_id=1, source_target_pairs={{0,1},{1,0},{2,3},{3,2},{4,5},{5,4},{6,7},{7,6},{8,9},{9,8},{10,11... | collective-permute-start | bytes 147464 | tf_op jit(solution)/shard_map/ppermute | solution.py:266
  5.6 7.7 %collective-permute-start.5 = (s16[272,128]{1,0:T(8,128)(2,1)S(1)}, s16[272,128]{1,0:T(8,128)(2,1)S(1)}, u32[]{:S(2)}, u32[]{:S(2)}) collective-permute-start(s16[272,128]{1,0:T(8,128)(2,1)S(1)} %get-tuple-element.18), channel_id=1, source_target_pairs={{0,9},{1,8},{2,11},{3,10},{4,13},{5,12},{6,15},{7,14},{8,1},{9,0},... | collective-permute-start | bytes 208904 | tf_op jit(solution)/shard_map/ppermute | solution.py:266
  5.7 8.8 %collective-permute-start.6 = (s16[528,128]{1,0:T(8,128)(2,1)S(1)}, s16[528,128]{1,0:T(8,128)(2,1)S(1)}, u32[]{:S(2)}, u32[]{:S(2)}) collective-permute-start(s16[528,128]{1,0:T(8,128)(2,1)S(1)} %merge.1), channel_id=1, source_target_pairs={{0,16},{1,17},{2,18},{3,19},{4,20},{5,21},{6,22},{7,23},{8,24},{9,... | collective-permute-start | bytes 405512 | tf_op jit(solution)/shard_map/ppermute | solution.py:266
  7.6 7.0 %collective-permute-start.7 = (s16[528,128]{1,0:T(8,128)(2,1)S(1)}, s16[528,128]{1,0:T(8,128)(2,1)S(1)}, u32[]{:S(2)}, u32[]{:S(2)}) collective-permute-start(s16[528,128]{1,0:T(8,128)(2,1)S(1)} %merge.1), channel_id=1, source_target_pairs={{0,17},{1,16},{2,19},{3,18},{4,21},{5,20},{6,23},{7,22},{8,25},{9,... | collective-permute-start | bytes 405512 | tf_op jit(solution)/shard_map/ppermute | solution.py:266
  9.0 10.2 %collective-permute-start.1 = (bf16[2,6,32,128]{3,2,1,0:T(8,128)(2,1)S(1)}, bf16[2,6,32,128]{3,2,1,0:T(8,128)(2,1)S(1)}, u32[]{:S(2)}, u32[]{:S(2)}) collective-permute-start(bf16[2,6,32,128]{3,2,1,0:T(8,128)(2,1)S(1)} %pair.1.refs_0_), channel_id=1, source_target_pairs={{0,4},{1,5},{2,6},{3,7},{4,0},{5,1},{6,2},{7,3},{8,12},{9,13},{10,... | collective-permute-start | bytes 294920 | tf_op jit(solution)/shard_map/ppermute | solution.py:266
  11.7 8.2 %collective-permute-start.2 = (bf16[2,6,32,128]{3,2,1,0:T(8,128)(2,1)S(1)}, bf16[2,6,32,128]{3,2,1,0:T(8,128)(2,1)S(1)}, u32[]{:S(2)}, u32[]{:S(2)}) collective-permute-start(bf16[2,6,32,128]{3,2,1,0:T(8,128)(2,1)S(1)} %pair.1.refs_0_), channel_id=1, source_target_pairs={{0,2},{1,3},{2,0},{3,1},{4,6},{5,7},{6,4},{7,5},{8,10},{9,11},{10,... | collective-permute-start | bytes 294920 | tf_op jit(solution)/shard_map/ppermute | solution.py:266
  13.3 6.6 %collective-permute-start.3 = (bf16[2,6,32,128]{3,2,1,0:T(8,128)(2,1)S(1)}, bf16[2,6,32,128]{3,2,1,0:T(8,128)(2,1)S(1)}, u32[]{:S(2)}, u32[]{:S(2)}) collective-permute-start(bf16[2,6,32,128]{3,2,1,0:T(8,128)(2,1)S(1)} %pair.1.refs_0_), channel_id=1, source_target_pairs={{0,6},{1,7},{2,4},{3,5},{4,2},{5,3},{6,0},{7,1},{8,14},{9,15},{10,... | collective-permute-start | bytes 294920 | tf_op jit(solution)/shard_map/ppermute | solution.py:266
  13.5 6.4 %slice-start = ((s8[9437184]{0:T(1024)(128)(4,1)}), s8[4194304]{0:T(1024)(128)(4,1)S(1)}, s32[]{:S(2)}) async-start(s8[9437184]{0:T(1024)(128)(4,1)} %bitcast.6), calls=%async_computation | async-start | bytes 8388608
  13.8 6.1 %slice-start.1 = ((s8[9437184]{0:T(1024)(128)(4,1)}), s8[4194304]{0:T(1024)(128)(4,1)S(1)}, s32[]{:S(2)}) async-start(s8[9437184]{0:T(1024)(128)(4,1)} %bitcast.6), calls=%async_computation.1 | async-start | bytes 8388608
  13.8 6.1 %slice-start.2 = ((s8[9437184]{0:T(1024)(128)(4,1)}), s8[1048576]{0:T(1024)(128)(4,1)S(1)}, s32[]{:S(2)}) async-start(s8[9437184]{0:T(1024)(128)(4,1)} %bitcast.6), calls=%async_computation.2 | async-start | bytes 2097152
  15.3 9.5 %copy-start = (f32[768]{0:T(1024)S(1)}, f32[768]{0:T(1024)}, u32[]{:S(2)}) copy-start(f32[768]{0:T(1024)} %refs_3_.1) | copy-start | bytes 9220
  15.3 9.5 %copy-start.1 = (f32[768]{0:T(1024)S(1)}, f32[768]{0:T(1024)}, u32[]{:S(2)}) copy-start(f32[768]{0:T(1024)} %refs_4_.1) | copy-start | bytes 9220
  15.3 9.5 %copy-start.2 = (f32[768]{0:T(1024)S(1)}, f32[768]{0:T(1024)}, u32[]{:S(2)}) copy-start(f32[768]{0:T(1024)} %refs_5_.1) | copy-start | bytes 9220
  15.3 9.5 %copy-start.3 = (f32[768]{0:T(1024)S(1)}, f32[768]{0:T(1024)}, u32[]{:S(2)}) copy-start(f32[768]{0:T(1024)} %refs_6_.1) | copy-start | bytes 9220
  15.3 6.3 %collective-permute-start.10 = (s16[208,128]{1,0:T(8,128)(2,1)S(1)}, s16[208,128]{1,0:T(8,128)(2,1)S(1)}, u32[]{:S(2)}, u32[]{:S(2)}) collective-permute-start(s16[208,128]{1,0:T(8,128)(2,1)S(1)} %get-tuple-element.23), channel_id=1, source_target_pairs={{0,6},{1,7},{2,4},{3,5},{4,2},{5,3},{6,0},{7,1},{8,14},{9,15},{10,... | collective-permute-start | bytes 159752 | tf_op jit(solution)/shard_map/ppermute | solution.py:266
  19.2 4.4 %collective-permute-start.8 = (s16[208,128]{1,0:T(8,128)(2,1)S(1)}, s16[208,128]{1,0:T(8,128)(2,1)S(1)}, u32[]{:S(2)}, u32[]{:S(2)}) collective-permute-start(s16[208,128]{1,0:T(8,128)(2,1)S(1)} %get-tuple-element.21), channel_id=1, source_target_pairs={{0,2},{1,3},{2,0},{3,1},{4,6},{5,7},{6,4},{7,5},{8,10},{9,11},{10,... | collective-permute-start | bytes 159752 | tf_op jit(solution)/shard_map/ppermute | solution.py:266
  19.2 5.5 %collective-permute-start.9 = (s16[208,128]{1,0:T(8,128)(2,1)S(1)}, s16[208,128]{1,0:T(8,128)(2,1)S(1)}, u32[]{:S(2)}, u32[]{:S(2)}) collective-permute-start(s16[208,128]{1,0:T(8,128)(2,1)S(1)} %get-tuple-element.22), channel_id=1, source_target_pairs={{0,4},{1,5},{2,6},{3,7},{4,0},{5,1},{6,2},{7,3},{8,12},{9,13},{10,... | collective-permute-start | bytes 159752 | tf_op jit(solution)/shard_map/ppermute | solution.py:266

commit v8 on v7

--- a/solution.py
+++ b/solution.py
@@ -320,7 +320,7 @@
         in_specs=[VMEM] * 2,
         out_specs=VMEM,
         compiler_params=PARAMS,
-        cost_estimate=pl.CostEstimate(flops=1 << 36, bytes_accessed=1 << 28, transcendentals=1 << 26),
+        cost_estimate=pl.CostEstimate(flops=1 << 31, bytes_accessed=1 << 23, transcendentals=1 << 21),
         name="pair",
     )(drive, drive_x)
     arrived = []
@@ -328,7 +328,7 @@
         for h in range(HALVES):
             arrived.append(to(merged[k - 1], CORES * k, h))
     drive_order = [2, 3, 1] if n_far == 4 else list(range(1, n_far))
-    use_order = [2, 1, 3] if n_far == 4 else list(range(1, n_far))
+    use_order = [2, 3, 1] if n_far == 4 else list(range(1, n_far))
     sum_order = [2, 3, 1] if n_far == 4 else list(range(1, n_far))
     add_order = [1, 2, 3] if n_far == 4 else list(range(1, n_far))
     pairs = {k: to(pair, 0, k * HALVES) for k in drive_order}
@@ -339,6 +339,7 @@
         in_specs=[VMEM] * 2,
         out_specs=VMEM,
         compiler_params=PARAMS,
+        cost_estimate=pl.CostEstimate(flops=1 << 26, bytes_accessed=1 << 18, transcendentals=1 << 16),
         name="add_early",
     )(sibling, beside)
     far_sent = shape((own_blocks * steps + steps // 2, width), i16)
@@ -349,7 +350,7 @@
         out_specs=[VMEM] * n_far,
         scratch_shapes=[pltpu.VMEM((per_half + 1, steps, width), f32)],
         compiler_params=PARAMS,
-        cost_estimate=pl.CostEstimate(flops=1 << 36, bytes_accessed=1 << 28, transcendentals=1 << 26),
+        cost_estimate=pl.CostEstimate(flops=1 << 37, bytes_accessed=1 << 29, transcendentals=1 << 27),
         name="add_late",
     )(early, *arrived)
     far = {k: to(sums[k - 1], 0, k * HALVES) for k in sum_order}
@@ -360,11 +361,6 @@
         in_specs=[VMEM] * (n_far + 1),
         out_specs=VMEM,
         compiler_params=PARAMS,
-        cost_estimate=pl.CostEstimate(
-            flops=2 * steps * neurons * neurons * locals_,
-            bytes_accessed=2 * neurons * neurons * locals_,
-            transcendentals=0,
-        ),
         name="inner",
     )(pair, *[pairs[k] for k in use_order], w_region[0])
 

time: 25.9 us -> 25.9 us (level)
  waiting for transfers between devices: 3.9 us -> 4.61 us
  starting transfers between devices: 15.5 us -> 14.8 us
    ppermute x11, waiting for transfers between devices: 3.9 us -> 4.61 us  [to(): return lax.ppermute(value, ('region', 'local'), pairs)]
    ppermute x11, starting transfers between devices: 15.5 us -> 14.8 us  [to(): return lax.ppermute(value, ('region', 'local'), pairs)]
  transfers between devices with their start and end apart: 11 -> 11, of which waited for: 3 -> 5; matrix products, arithmetic and copies ran while one was open for 0% -> 0% of each run, Pallas kernels for 12% -> 12%
where the time goes in v8:
time: 25.9 us; the launch traced here: 25.7 us
  starting transfers between devices  14.8 us (57%)
  Pallas kernels  5.53 us (21%)
  waiting for transfers between devices  4.61 us (18%)
  between operations  0.75 us (3%)
    ppermute x11, starting transfers between devices, to(): return lax.ppermute(value, ('region', 'local'), pairs)  14.8 us
    ppermute x11, waiting for transfers between devices, to(): return lax.ppermute(value, ('region', 'local'), pairs)  4.61 us
    pallas_call x1, Pallas kernels, local(): pl.pallas_call(functools.partial(inner_kernel, n_far, (0, *use_order)), o...  1.73 us
    pallas_call x1, Pallas kernels, local(): pl.pallas_call(functools.partial(first_kernel, per_half), out_shape=[shap...  1.58 us
    pallas_call x1, Pallas kernels, local(): pl.pallas_call(functools.partial(advance_kernel, n_far - 1), out_shape=[s...  0.89 us
    pallas_call x1, Pallas kernels, local(): pl.pallas_call(functools.partial(late_kernel, len(arrived), n_far, slots,...  0.74 us
  transfers between devices with their start and end apart: 11, of which 5 were waited for; matrix products, arithmetic and copies ran while one was open for 0% of the time, Pallas kernels for 12%

profile of v8, /device:TPU:0, one launch (start us, length us, event | category | flops | bytes accessed | tf_op | source)
XLA Modules:
  0.0 25.7 jit_solution(9939545815795093690)
XLA Ops:
  0.6 1.6 %first_partials.1 = (bf16[6,32,128]{2,1,0:T(8,128)(2,1)S(1)}, s16[2,272,128]{2,1,0:T(8,128)(2,1)S(1)}, bf16[1,8,128,128]{3,2,1,0:T(8,128)(2,1)S(1)}, bf16[1,8,32...) custom-call(s32[6,32]{1,0:T(8,128)} %bitcast.10, bf16[32,768]{1,0:T(8,128)(2,1)} %trace_h.1, s32[4,8]{1,0:T(4,128)} %bitcast.11, ...), custom_call_target="tpu_custom_call" | custom-call | tf_op jit(solution)/shard_map/first_partials/pallas_call | solution.py:268
  2.2 0.5 %collective-permute-start.4 = (s16[2,272,128]{2,1,0:T(8,128)(2,1)S(1)}, s16[2,272,128]{2,1,0:T(8,128)(2,1)S(1)}, u32[]{:S(2)}, u32[]{:S(2)}) collective-permute-start(s16[2,272,128]{2,1,0:T(8,128)(2,1)S(1)} %get-tuple-element.14.theirs), channel_id=1, source_target_pairs={{0,8},{1,9},{2,10},{3,11},{4,12},{5,13},{6,14},{7,15},{8,0},{9,1},... | collective-permute-start | bytes 417800 | tf_op jit(solution)/shard_map/ppermute | solution.py:266
  2.7 2.6 %collective-permute-start = (bf16[6,32,128]{2,1,0:T(8,128)(2,1)S(1)}, bf16[6,32,128]{2,1,0:T(8,128)(2,1)S(1)}, u32[]{:S(2)}, u32[]{:S(2)}) collective-permute-start(bf16[6,32,128]{2,1,0:T(8,128)(2,1)S(1)} %get-tuple-element.13.drive), channel_id=1, source_target_pairs={{0,1},{1,0},{2,3},{3,2},{4,5},{5,4},{6,7},{7,6},{8,9},{9,8},{10,11... | collective-permute-start | bytes 147464 | tf_op jit(solution)/shard_map/ppermute | solution.py:266
  5.3 0.3 %second_partials.1 = (s16[1,272,128]{2,1,0:T(8,128)(2,1)S(1)}, s16[272,128]{1,0:T(8,128)(2,1)S(1)}) custom-call(bf16[1,8,32,128]{3,2,1,0:T(8,128)(2,1)S(1)} %get-tuple-element.15.chosen, s32[1,16,128]{2,1,0:T(8,128)S(1)} %get-tuple-element.16.meta, bf16[1,8,128,128]{3,2,1,0:T(8,128)(2,1)S(1)} %get-tuple-element.17.tiles, ...), custom_call_target="tpu_custom_call" | custom-call | tf_op jit(solution)/shard_map/second_partials/pallas_call | solution.py:300
  5.6 0.1 collective-permute-start.5
  5.7 0.0 collective-permute-done.4.sibling
  5.7 1.8 %collective-permute-start.6 = (s16[528,128]{1,0:T(8,128)(2,1)S(1)}, s16[528,128]{1,0:T(8,128)(2,1)S(1)}, u32[]{:S(2)}, u32[]{:S(2)}) collective-permute-start(s16[528,128]{1,0:T(8,128)(2,1)S(1)} %merge.1), channel_id=1, source_target_pairs={{0,16},{1,17},{2,18},{3,19},{4,20},{5,21},{6,22},{7,23},{8,24},{9,... | collective-permute-start | bytes 405512 | tf_op jit(solution)/shard_map/ppermute | solution.py:266
  7.6 1.4 %collective-permute-start.7 = (s16[528,128]{1,0:T(8,128)(2,1)S(1)}, s16[528,128]{1,0:T(8,128)(2,1)S(1)}, u32[]{:S(2)}, u32[]{:S(2)}) collective-permute-start(s16[528,128]{1,0:T(8,128)(2,1)S(1)} %merge.1), channel_id=1, source_target_pairs={{0,17},{1,16},{2,19},{3,18},{4,21},{5,20},{6,23},{7,22},{8,25},{9,... | collective-permute-start | bytes 405512 | tf_op jit(solution)/shard_map/ppermute | solution.py:266
  9.0 0.0 collective-permute-done.drive_x
  9.0 2.7 %collective-permute-start.1 = (bf16[2,6,32,128]{3,2,1,0:T(8,128)(2,1)S(1)}, bf16[2,6,32,128]{3,2,1,0:T(8,128)(2,1)S(1)}, u32[]{:S(2)}, u32[]{:S(2)}) collective-permute-start(bf16[2,6,32,128]{3,2,1,0:T(8,128)(2,1)S(1)} %pair.1.refs_0_), channel_id=1, source_target_pairs={{0,4},{1,5},{2,6},{3,7},{4,0},{5,1},{6,2},{7,3},{8,12},{9,13},{10,... | collective-permute-start | bytes 294920 | tf_op jit(solution)/shard_map/ppermute | solution.py:266
  11.7 1.3 %collective-permute-start.2 = (bf16[2,6,32,128]{3,2,1,0:T(8,128)(2,1)S(1)}, bf16[2,6,32,128]{3,2,1,0:T(8,128)(2,1)S(1)}, u32[]{:S(2)}, u32[]{:S(2)}) collective-permute-start(bf16[2,6,32,128]{3,2,1,0:T(8,128)(2,1)S(1)} %pair.1.refs_0_), channel_id=1, source_target_pairs={{0,6},{1,7},{2,4},{3,5},{4,2},{5,3},{6,0},{7,1},{8,14},{9,15},{10,... | collective-permute-start | bytes 294920 | tf_op jit(solution)/shard_map/ppermute | solution.py:266
  13.0 0.0 collective-permute-done.5.beside
  13.0 0.2 collective-permute-start.3
  13.3 0.0 slice-start
  13.3 0.3 %add_early.1.early = f32[25,32,128]{2,1,0:T(8,128)S(1)} custom-call(s16[2,272,128]{2,1,0:T(8,128)(2,1)S(1)} %collective-permute-done.4.sibling, s16[272,128]{1,0:T(8,128)(2,1)S(1)} %collective-permute-done.5.beside), custom_call_target="tpu_custom_call" | custom-call | flops 67108864 | bytes 262144 | tf_op jit(solution)/shard_map/add_early/pallas_call | solution.py:336
  13.5 0.0 slice-start.1
  13.6 0.0 slice-start.2
  13.6 1.0 %collective-permute-done.6.refs_0_ = s16[528,128]{1,0:T(8,128)(2,1)S(1)} collective-permute-done((s16[528,128]{1,0:T(8,128)(2,1)S(1)}, s16[528,128]{1,0:T(8,128)(2,1)S(1)}, u32[]{:S(2)}, u32[]{:S(2)}) %collective-permute-start.6) | collective-permute-done | bytes 135200 | tf_op jit(solution)/shard_map/ppermute | solution.py:266
  14.6 0.0 collective-permute-done.7.refs_1_
  14.6 0.7 %add_late.1 = (s16[208,128]{1,0:T(8,128)(2,1)S(1)}, s16[208,128]{1,0:T(8,128)(2,1)S(1)}, s16[208,128]{1,0:T(8,128)(2,1)S(1)}, f32[6,32,128]{2,1,0:T(8,128)S(1)}) custom-call(f32[25,32,128]{2,1,0:T(8,128)S(1)} %add_early.1.early, s16[528,128]{1,0:T(8,128)(2,1)S(1)} %collective-permute-done.6.refs_0_, s16[528,128]{1,0:T(8,128)(2,1)S(1)} %collective-permute-done.7.refs_1_), custom_call_target="tpu_custom_call" | custom-call | flops 137438953472 | bytes 536870912 | tf_op jit(solution)/shard_map/add_late/pallas_call | solution.py:346
  15.3 0.0 copy-start
  15.3 0.0 copy-start.1
  15.3 0.0 copy-start.2
  15.3 0.0 copy-start.3
  15.4 3.9 %collective-permute-start.10 = (s16[208,128]{1,0:T(8,128)(2,1)S(1)}, s16[208,128]{1,0:T(8,128)(2,1)S(1)}, u32[]{:S(2)}, u32[]{:S(2)}) collective-permute-start(s16[208,128]{1,0:T(8,128)(2,1)S(1)} %get-tuple-element.23), channel_id=1, source_target_pairs={{0,6},{1,7},{2,4},{3,5},{4,2},{5,3},{6,0},{7,1},{8,14},{9,15},{10,... | collective-permute-start | bytes 159752 | tf_op jit(solution)/shard_map/ppermute | solution.py:266
  19.2 0.0 collective-permute-start.8
  19.3 0.4 %collective-permute-done.1.refs_1_ = bf16[2,6,32,128]{3,2,1,0:T(8,128)(2,1)S(1)} collective-permute-done((bf16[2,6,32,128]{3,2,1,0:T(8,128)(2,1)S(1)}, bf16[2,6,32,128]{3,2,1,0:T(8,128)(2,1)S(1)}, u32[]{:S(2)}, u32[]{:S(2)}) %collective-permute-start.1) | collective-permute-done | bytes 98336 | tf_op jit(solution)/shard_map/ppermute | solution.py:266
  19.7 0.2 collective-permute-start.9
  19.9 0.0 collective-permute-done.2.refs_2_
  19.9 0.7 %collective-permute-done.3.refs_3_ = bf16[2,6,32,128]{3,2,1,0:T(8,128)(2,1)S(1)} collective-permute-done((bf16[2,6,32,128]{3,2,1,0:T(8,128)(2,1)S(1)}, bf16[2,6,32,128]{3,2,1,0:T(8,128)(2,1)S(1)}, u32[]{:S(2)}, u32[]{:S(2)}) %collective-permute-start.3) | collective-permute-done | bytes 98336 | tf_op jit(solution)/shard_map/ppermute | solution.py:266
  20.6 0.0 slice-done
  20.6 0.0 slice-done.1
  20.6 0.0 slice-done.2
  20.6 1.7 %inner.1 = f32[6,32,128]{2,1,0:T(8,128)S(1)} custom-call(bf16[2,6,32,128]{3,2,1,0:T(8,128)(2,1)S(1)} %pair.1.refs_0_, bf16[2,6,32,128]{3,2,1,0:T(8,128)(2,1)S(1)} %collective-permute-done.1.refs_1_, bf16[2,6,32,128]{3,2,1,0:T(8,128)(2,1)S(1)} %collective-permute-done.2.refs_2_, bf16[2,6,32,128]{3,2,1,0:T(8,128)(2,1)S(1)} %collective-permute-done.3.refs_3_, ...), custom_call_target="tpu_custom_call" | custom-call | tf_op jit(solution)/shard_map/inner/pallas_call | solution.py:358
  22.4 0.0 collective-permute-done.10.refs_2_
  22.4 1.2 %collective-permute-done.8.refs_0_ = s16[208,128]{1,0:T(8,128)(2,1)S(1)} collective-permute-done((s16[208,128]{1,0:T(8,128)(2,1)S(1)}, s16[208,128]{1,0:T(8,128)(2,1)S(1)}, u32[]{:S(2)}, u32[]{:S(2)}) %collective-permute-start.8) | collective-permute-done | bytes 53280 | tf_op jit(solution)/shard_map/ppermute | solution.py:266
  23.6 1.2 %collective-permute-done.9.refs_1_ = s16[208,128]{1,0:T(8,128)(2,1)S(1)} collective-permute-done((s16[208,128]{1,0:T(8,128)(2,1)S(1)}, s16[208,128]{1,0:T(8,128)(2,1)S(1)}, u32[]{:S(2)}, u32[]{:S(2)}) %collective-permute-start.9) | collective-permute-done | bytes 53280 | tf_op jit(solution)/shard_map/ppermute | solution.py:266
  24.8 0.0 copy-done
  24.8 0.0 copy-done.1
  24.8 0.0 copy-done.2
  24.8 0.0 copy-done.3
  24.9 0.9 %advance.1 = (f32[32,768]{1,0:T(8,128)}, f32[768]{0:T(1024)}) custom-call(f32[6,32,128]{2,1,0:T(8,128)S(1)} %inner.1, f32[6,32,128]{2,1,0:T(8,128)S(1)} %get-tuple-element.20.own, s16[208,128]{1,0:T(8,128)(2,1)S(1)} %collective-permute-done.8.refs_0_, s16[208,128]{1,0:T(8,128)(2,1)S(1)} %collective-permute-done.9.refs_1_, ...), custom_call_target="tpu_custom_call" | custom-call | tf_op jit(solution)/shard_map/advance/pallas_call | solution.py:367
  (3 shorter events, 0.0 us)
Async XLA Ops:
  2.2 3.5 %collective-permute-start.4 = (s16[2,272,128]{2,1,0:T(8,128)(2,1)S(1)}, s16[2,272,128]{2,1,0:T(8,128)(2,1)S(1)}, u32[]{:S(2)}, u32[]{:S(2)}) collective-permute-start(s16[2,272,128]{2,1,0:T(8,128)(2,1)S(1)} %get-tuple-element.14.theirs), channel_id=1, source_target_pairs={{0,8},{1,9},{2,10},{3,11},{4,12},{5,13},{6,14},{7,15},{8,0},{9,1},... | collective-permute-start | bytes 417800 | tf_op jit(solution)/shard_map/ppermute | solution.py:266
  2.7 6.3 %collective-permute-start = (bf16[6,32,128]{2,1,0:T(8,128)(2,1)S(1)}, bf16[6,32,128]{2,1,0:T(8,128)(2,1)S(1)}, u32[]{:S(2)}, u32[]{:S(2)}) collective-permute-start(bf16[6,32,128]{2,1,0:T(8,128)(2,1)S(1)} %get-tuple-element.13.drive), channel_id=1, source_target_pairs={{0,1},{1,0},{2,3},{3,2},{4,5},{5,4},{6,7},{7,6},{8,9},{9,8},{10,11... | collective-permute-start | bytes 147464 | tf_op jit(solution)/shard_map/ppermute | solution.py:266
  5.6 7.4 %collective-permute-start.5 = (s16[272,128]{1,0:T(8,128)(2,1)S(1)}, s16[272,128]{1,0:T(8,128)(2,1)S(1)}, u32[]{:S(2)}, u32[]{:S(2)}) collective-permute-start(s16[272,128]{1,0:T(8,128)(2,1)S(1)} %get-tuple-element.18), channel_id=1, source_target_pairs={{0,9},{1,8},{2,11},{3,10},{4,13},{5,12},{6,15},{7,14},{8,1},{9,0},... | collective-permute-start | bytes 208904 | tf_op jit(solution)/shard_map/ppermute | solution.py:266
  5.7 8.8 %collective-permute-start.6 = (s16[528,128]{1,0:T(8,128)(2,1)S(1)}, s16[528,128]{1,0:T(8,128)(2,1)S(1)}, u32[]{:S(2)}, u32[]{:S(2)}) collective-permute-start(s16[528,128]{1,0:T(8,128)(2,1)S(1)} %merge.1), channel_id=1, source_target_pairs={{0,16},{1,17},{2,18},{3,19},{4,20},{5,21},{6,22},{7,23},{8,24},{9,... | collective-permute-start | bytes 405512 | tf_op jit(solution)/shard_map/ppermute | solution.py:266
  7.6 7.0 %collective-permute-start.7 = (s16[528,128]{1,0:T(8,128)(2,1)S(1)}, s16[528,128]{1,0:T(8,128)(2,1)S(1)}, u32[]{:S(2)}, u32[]{:S(2)}) collective-permute-start(s16[528,128]{1,0:T(8,128)(2,1)S(1)} %merge.1), channel_id=1, source_target_pairs={{0,17},{1,16},{2,19},{3,18},{4,21},{5,20},{6,23},{7,22},{8,25},{9,... | collective-permute-start | bytes 405512 | tf_op jit(solution)/shard_map/ppermute | solution.py:266
  9.0 10.7 %collective-permute-start.1 = (bf16[2,6,32,128]{3,2,1,0:T(8,128)(2,1)S(1)}, bf16[2,6,32,128]{3,2,1,0:T(8,128)(2,1)S(1)}, u32[]{:S(2)}, u32[]{:S(2)}) collective-permute-start(bf16[2,6,32,128]{3,2,1,0:T(8,128)(2,1)S(1)} %pair.1.refs_0_), channel_id=1, source_target_pairs={{0,4},{1,5},{2,6},{3,7},{4,0},{5,1},{6,2},{7,3},{8,12},{9,13},{10,... | collective-permute-start | bytes 294920 | tf_op jit(solution)/shard_map/ppermute | solution.py:266
  11.7 8.2 %collective-permute-start.2 = (bf16[2,6,32,128]{3,2,1,0:T(8,128)(2,1)S(1)}, bf16[2,6,32,128]{3,2,1,0:T(8,128)(2,1)S(1)}, u32[]{:S(2)}, u32[]{:S(2)}) collective-permute-start(bf16[2,6,32,128]{3,2,1,0:T(8,128)(2,1)S(1)} %pair.1.refs_0_), channel_id=1, source_target_pairs={{0,6},{1,7},{2,4},{3,5},{4,2},{5,3},{6,0},{7,1},{8,14},{9,15},{10,... | collective-permute-start | bytes 294920 | tf_op jit(solution)/shard_map/ppermute | solution.py:266
  13.0 7.6 %collective-permute-start.3 = (bf16[2,6,32,128]{3,2,1,0:T(8,128)(2,1)S(1)}, bf16[2,6,32,128]{3,2,1,0:T(8,128)(2,1)S(1)}, u32[]{:S(2)}, u32[]{:S(2)}) collective-permute-start(bf16[2,6,32,128]{3,2,1,0:T(8,128)(2,1)S(1)} %pair.1.refs_0_), channel_id=1, source_target_pairs={{0,2},{1,3},{2,0},{3,1},{4,6},{5,7},{6,4},{7,5},{8,10},{9,11},{10,... | collective-permute-start | bytes 294920 | tf_op jit(solution)/shard_map/ppermute | solution.py:266
  13.3 7.4 %slice-start = ((s8[9437184]{0:T(1024)(128)(4,1)}), s8[4194304]{0:T(1024)(128)(4,1)S(1)}, s32[]{:S(2)}) async-start(s8[9437184]{0:T(1024)(128)(4,1)} %bitcast.6), calls=%async_computation | async-start | bytes 8388608
  13.5 7.1 %slice-start.1 = ((s8[9437184]{0:T(1024)(128)(4,1)}), s8[4194304]{0:T(1024)(128)(4,1)S(1)}, s32[]{:S(2)}) async-start(s8[9437184]{0:T(1024)(128)(4,1)} %bitcast.6), calls=%async_computation.1 | async-start | bytes 8388608
  13.6 7.1 %slice-start.2 = ((s8[9437184]{0:T(1024)(128)(4,1)}), s8[1048576]{0:T(1024)(128)(4,1)S(1)}, s32[]{:S(2)}) async-start(s8[9437184]{0:T(1024)(128)(4,1)} %bitcast.6), calls=%async_computation.2 | async-start | bytes 2097152
  15.3 9.5 %copy-start = (f32[768]{0:T(1024)S(1)}, f32[768]{0:T(1024)}, u32[]{:S(2)}) copy-start(f32[768]{0:T(1024)} %refs_3_.1) | copy-start | bytes 9220
  15.3 9.5 %copy-start.1 = (f32[768]{0:T(1024)S(1)}, f32[768]{0:T(1024)}, u32[]{:S(2)}) copy-start(f32[768]{0:T(1024)} %refs_4_.1) | copy-start | bytes 9220
  15.3 9.5 %copy-start.2 = (f32[768]{0:T(1024)S(1)}, f32[768]{0:T(1024)}, u32[]{:S(2)}) copy-start(f32[768]{0:T(1024)} %refs_5_.1) | copy-start | bytes 9220
  15.3 9.5 %copy-start.3 = (f32[768]{0:T(1024)S(1)}, f32[768]{0:T(1024)}, u32[]{:S(2)}) copy-start(f32[768]{0:T(1024)} %refs_6_.1) | copy-start | bytes 9220
  15.4 7.0 %collective-permute-start.10 = (s16[208,128]{1,0:T(8,128)(2,1)S(1)}, s16[208,128]{1,0:T(8,128)(2,1)S(1)}, u32[]{:S(2)}, u32[]{:S(2)}) collective-permute-start(s16[208,128]{1,0:T(8,128)(2,1)S(1)} %get-tuple-element.23), channel_id=1, source_target_pairs={{0,6},{1,7},{2,4},{3,5},{4,2},{5,3},{6,0},{7,1},{8,14},{9,15},{10,... | collective-permute-start | bytes 159752 | tf_op jit(solution)/shard_map/ppermute | solution.py:266
  19.2 4.4 %collective-permute-start.8 = (s16[208,128]{1,0:T(8,128)(2,1)S(1)}, s16[208,128]{1,0:T(8,128)(2,1)S(1)}, u32[]{:S(2)}, u32[]{:S(2)}) collective-permute-start(s16[208,128]{1,0:T(8,128)(2,1)S(1)} %get-tuple-element.21), channel_id=1, source_target_pairs={{0,2},{1,3},{2,0},{3,1},{4,6},{5,7},{6,4},{7,5},{8,10},{9,11},{10,... | collective-permute-start | bytes 159752 | tf_op jit(solution)/shard_map/ppermute | solution.py:266
  19.7 5.1 %collective-permute-start.9 = (s16[208,128]{1,0:T(8,128)(2,1)S(1)}, s16[208,128]{1,0:T(8,128)(2,1)S(1)}, u32[]{:S(2)}, u32[]{:S(2)}) collective-permute-start(s16[208,128]{1,0:T(8,128)(2,1)S(1)} %get-tuple-element.22), channel_id=1, source_target_pairs={{0,4},{1,5},{2,6},{3,7},{4,0},{5,1},{6,2},{7,3},{8,12},{9,13},{10,... | collective-permute-start | bytes 159752 | tf_op jit(solution)/shard_map/ppermute | solution.py:266
